TPU v7x, 256 devices: a whole 4x4x8 slice. The times are simulated.
256 devices in a mesh: seq: 32 (over x, z), exp: 8 (over y, core).
Axes of the slice: x: 4, y: 4, z: 8, core: 2. Of those that a mesh axis runs over, the one named last changes fastest.
Arguments:
- residual: bfloat16 [8, 8192, 2048], P('exp', 'seq'), may hold values from -36 to 36
- kept_index: int32 [8, 2048], P('exp', 'seq'), may hold values from 0 to 255, as said below
- kept_count: int32 [8, 32], P('exp', 'seq'), may hold values from 16 to 64, as said below
- projected: bfloat16 [8, 2048, 6144], P('exp', 'seq'), may hold values from -6 to 6
- expert_ids: int32 [8, 2048, 6], P('exp', 'seq'), may hold values from 0 to 63, as said below
- gate_values: float32 [8, 2048, 6], P('exp', 'seq'), may hold values from 0.1 to 0.9
- gate_weight: bfloat16 [8, 2048, 1408], P('exp', 'seq'), may hold values from -0.125 to 0.125
- up_weight: bfloat16 [8, 2048, 1408], P('exp', 'seq'), may hold values from -0.125 to 0.125
- down_weight: bfloat16 [8, 1408, 2048], P('exp', None, 'seq'), may hold values from -0.15625 to 0.15625
- cotangent: bfloat16 [8, 8192, 2048], P('exp', 'seq'), may hold values from -6 to 6
Outputs:
- output: bfloat16 [8, 8192, 2048], P('exp', 'seq')
- input_grad: bfloat16 [8, 8192, 2048], P('exp', 'seq')
- projected_grad: bfloat16 [8, 2048, 6144], P('exp', 'seq')
- gate_grads: float32 [8, 2048, 6], P('exp', 'seq')
Inputs may be any that keep to these rules, and one draw needn't show every extreme that they name: `kept_index`: within each device's list of 64 entries the local indices are distinct and rise; the first kept_count entries are the kept tokens, the rest are padding. `kept_count`: every sequence has a device whose list is entirely live. `expert_ids`: each entry names 6 different experts; every expert is named. In one device's list each expert below 8 is named at most 12 times, only by live entries, and for every index of seq one such expert is named exactly 12 times in the list of every device of that index.
All inputs are finite; a program needn't handle non-finite values.
Results may differ from a plain program's by a relative error of at most 0.014.
Values may be sent and summed in bfloat16 or wider, within the bound.
A program may use at most 128 MiB of HBM per device.

v0:
```python
import jax
import jax.numpy as jnp
from jax import lax
from jax.sharding import PartitionSpec as P

HS = 128
CAP = 12


EPSILON = 1e-06


def dispatch_tables(expert_list, live_rows, weight_list, flight, capacity):
    experts = jnp.arange(flight, dtype=jnp.int32)
    matches = (expert_list[:, :, None] == experts[None, None, :]) & live_rows[:, None, None]
    assigned = jnp.any(matches, axis=1).astype(jnp.int32)
    slot_rank = jnp.cumsum(assigned, axis=0) - assigned
    slot_ids = jnp.arange(capacity, dtype=jnp.int32)
    chosen = (assigned[None, :, :] == 1) & (slot_rank[None, :, :] == slot_ids[:, None, None])
    slot_table = jnp.transpose(chosen, (2, 0, 1)).astype(jnp.float32)
    weight_at = jnp.sum(jnp.where(matches, weight_list[:, :, None], 0.0), axis=1)
    slot_gate = jnp.sum(slot_table * jnp.transpose(weight_at)[:, None, :], axis=2)
    return (slot_table, matches.astype(jnp.float32), weight_at, slot_gate)


def block_probabilities(queries, key_rows, query_pos, query_live, key_pos, key_live, score_scale):
    scores = (
        jnp.einsum("qhd,khd->hqk", queries, key_rows, preferred_element_type=jnp.float32)
        * score_scale
    )
    causal = key_live[None, :] & (key_pos[None, :] <= query_pos[:, None])
    first_key = (jnp.arange(key_rows.shape[0]) == 0)[None, :]
    allowed = jnp.where(query_live[:, None], causal, first_key)
    scores = jnp.where(allowed[None], scores, -jnp.inf)
    row_max = jnp.max(scores, axis=-1, keepdims=True)
    exponent = jnp.exp(scores - row_max)
    return exponent / jnp.sum(exponent, axis=-1, keepdims=True)


def expert_forward(row_data, gate_w, up_w, down_w):
    gate_pre = jnp.dot(row_data, gate_w, preferred_element_type=jnp.float32)
    up_pre = jnp.dot(row_data, up_w, preferred_element_type=jnp.float32)
    middle = (gate_pre * jax.nn.sigmoid(gate_pre) * up_pre).astype(jnp.bfloat16)
    return (gate_pre, up_pre, jnp.dot(middle, down_w, preferred_element_type=jnp.float32))


def expert_partial(grads, gate_pre, up_pre, gate_w, up_w, down_w):
    mid_grad = jnp.dot(grads, down_w.T, preferred_element_type=jnp.float32)
    sigma = jax.nn.sigmoid(gate_pre)
    gate_grad = (mid_grad * up_pre * sigma * (1.0 + gate_pre * (1.0 - sigma))).astype(jnp.bfloat16)
    up_grad = (mid_grad * gate_pre * sigma).astype(jnp.bfloat16)
    return jnp.dot(gate_grad, gate_w.T, preferred_element_type=jnp.float32) + jnp.dot(
        up_grad, up_w.T, preferred_element_type=jnp.float32
    )


def body(
    residual,
    kept_index,
    kept_count,
    projected,
    expert_ids,
    gate_values,
    gate_weight,
    up_weight,
    down_weight,
    cotangent,
):
    seq_count = lax.axis_size("seq")
    exp_count = lax.axis_size("exp")
    seq_rank = lax.axis_index("seq")
    keep_rows = kept_index.shape[1]
    tok_dev = residual.shape[1]
    model_width = residual.shape[2]
    head_total = model_width // HS
    query_splits = max(1, seq_count // head_total)
    heads_here = head_total * query_splits // seq_count
    head_groups = seq_count // query_splits
    part_rows = keep_rows // query_splits
    lane_width = heads_here * HS
    score_scale = HS ** (-0.5)
    query_part = seq_rank % query_splits
    local_index = kept_index[0]
    live_rows = jnp.arange(keep_rows) < kept_count[0, 0]
    every_index, every_count = (
        lax.all_gather(kept_index, "seq", axis=1, tiled=True),
        lax.all_gather(kept_count, "seq", axis=1, tiled=True),
    )
    entries = jnp.arange(keep_rows * seq_count)
    key_shard = entries // keep_rows
    key_live = entries % keep_rows < every_count[0][key_shard]
    key_pos = key_shard * tok_dev + every_index[0]
    query_index = (
        jnp.arange(seq_count)[:, None] * keep_rows
        + query_part * part_rows
        + jnp.arange(part_rows)[None, :]
    ).reshape(-1)
    query_pos = key_pos[query_index]
    query_live = key_live[query_index]
    sections = projected[0].reshape(keep_rows, 3, head_groups, lane_width)
    query_send = jnp.transpose(
        sections[:, 0].reshape(query_splits, part_rows, head_groups, lane_width), (2, 0, 1, 3)
    ).reshape(seq_count, part_rows, lane_width)
    pair_rows = jnp.transpose(sections[:, 1:], (2, 0, 1, 3)).reshape(
        head_groups, keep_rows, 2 * lane_width
    )
    pair_send = jnp.broadcast_to(
        pair_rows[:, None], (head_groups, query_splits, keep_rows, 2 * lane_width)
    ).reshape(seq_count, keep_rows, 2 * lane_width)
    query_in, pair_in = (
        lax.all_to_all(query_send, "seq", split_axis=0, concat_axis=0, tiled=True),
        lax.all_to_all(pair_send, "seq", split_axis=0, concat_axis=0, tiled=True),
    )
    queries = query_in.reshape(seq_count * part_rows, heads_here, HS)
    key_rows = pair_in[:, :, :lane_width].reshape(seq_count * keep_rows, heads_here, HS)
    value_rows = pair_in[:, :, lane_width:].reshape(seq_count * keep_rows, heads_here, HS)
    sources_per = min(seq_count, max(1, 512 // part_rows))
    bounds = []
    for block_no in range(seq_count // sources_per):
        bounds.append(
            (
                block_no * sources_per * part_rows,
                (block_no + 1) * sources_per * part_rows,
                (block_no + 1) * sources_per * keep_rows,
            )
        )
    pieces = []
    for row_start, row_stop, key_stop in bounds:
        attention = block_probabilities(
            queries[row_start:row_stop],
            key_rows[:key_stop],
            query_pos[row_start:row_stop],
            query_live[row_start:row_stop],
            key_pos[:key_stop],
            key_live[:key_stop],
            score_scale,
        )
        pieces.append(
            jnp.einsum(
                "hqk,khd->qhd",
                attention.astype(jnp.bfloat16),
                value_rows[:key_stop],
                preferred_element_type=jnp.float32,
            )
        )
    attended_f = jnp.concatenate(pieces, 0)
    returned = lax.all_to_all(
        attended_f.astype(jnp.bfloat16).reshape(seq_count, part_rows, lane_width),
        "seq",
        split_axis=0,
        concat_axis=0,
        tiled=True,
    )
    attended_rows = jnp.transpose(
        returned.reshape(head_groups, query_splits, part_rows, lane_width), (1, 2, 0, 3)
    ).reshape(keep_rows, model_width)
    kept_rows = residual[0][local_index]
    hidden_one = jnp.where(
        live_rows[:, None], kept_rows.astype(jnp.float32) + attended_rows.astype(jnp.float32), 0.0
    )
    inv_rms = lax.rsqrt(jnp.mean(hidden_one * hidden_one, axis=-1, keepdims=True) + EPSILON)
    normed = (hidden_one * inv_rms).astype(jnp.bfloat16)
    slot_table, matches, weight_at, slot_gate = dispatch_tables(
        expert_ids[0], live_rows, gate_values[0], exp_count, CAP
    )
    table_half = slot_table.astype(jnp.bfloat16)
    outgoing = jnp.einsum(
        "eci,id->ecd", table_half, normed, preferred_element_type=jnp.float32
    ).astype(jnp.bfloat16)
    incoming = lax.all_to_all(outgoing, "exp", split_axis=0, concat_axis=0, tiled=True).reshape(
        exp_count * CAP, model_width
    )
    full_gate, full_up, full_down = (
        lax.all_gather(gate_weight, "seq", axis=1, tiled=True),
        lax.all_gather(up_weight, "seq", axis=1, tiled=True),
        lax.all_gather(down_weight, "seq", axis=2, tiled=True),
    )
    gate_pre, up_pre, produced_f = expert_forward(incoming, full_gate[0], full_up[0], full_down[0])
    produced = produced_f.astype(jnp.bfloat16)
    results = lax.all_to_all(
        produced.reshape(exp_count, CAP, model_width),
        "exp",
        split_axis=0,
        concat_axis=0,
        tiled=True,
    )
    selected = jnp.einsum("eci,ecd->eid", table_half, results, preferred_element_type=jnp.float32)
    mixture = jnp.sum(jnp.transpose(weight_at)[:, :, None] * selected, axis=0)
    new_rows = jnp.where(live_rows[:, None], (hidden_one + mixture).astype(jnp.bfloat16), kept_rows)
    output = residual[0].at[local_index].set(new_rows)[None]
    grad_rows = cotangent[0][local_index]
    grad_f = grad_rows.astype(jnp.float32)
    per_entry = jnp.sum(selected * grad_f[None], axis=-1)
    gate_grads = jnp.sum(matches * jnp.transpose(per_entry)[:, None, :], axis=-1)[None]
    expert_grad = (
        slot_gate[:, :, None]
        * jnp.einsum("eci,id->ecd", table_half, grad_rows, preferred_element_type=jnp.float32)
    ).astype(jnp.bfloat16)
    grad_in = lax.all_to_all(expert_grad, "exp", split_axis=0, concat_axis=0, tiled=True).reshape(
        exp_count * CAP, model_width
    )
    rows_grad = expert_partial(
        grad_in, gate_pre, up_pre, full_gate[0], full_up[0], full_down[0]
    ).astype(jnp.bfloat16)
    back = lax.all_to_all(
        rows_grad.reshape(exp_count, CAP, model_width),
        "exp",
        split_axis=0,
        concat_axis=0,
        tiled=True,
    )
    normed_grad = jnp.einsum("eci,ecd->id", table_half, back, preferred_element_type=jnp.float32)
    cubed = inv_rms * inv_rms * inv_rms
    hidden_grad = (
        grad_f
        + inv_rms * normed_grad
        - hidden_one * cubed * jnp.mean(normed_grad * hidden_one, axis=-1, keepdims=True)
    )
    hidden_grad = jnp.where(live_rows[:, None], hidden_grad, 0.0).astype(jnp.bfloat16)
    input_grad = (
        cotangent[0]
        .at[local_index]
        .set(jnp.where(live_rows[:, None], hidden_grad, grad_rows))[None]
    )
    grad_send = jnp.transpose(
        hidden_grad.reshape(query_splits, part_rows, head_groups, lane_width), (2, 0, 1, 3)
    ).reshape(seq_count, part_rows, lane_width)
    grad_heads = lax.all_to_all(grad_send, "seq", split_axis=0, concat_axis=0, tiled=True).reshape(
        seq_count * part_rows, heads_here, HS
    )
    query_pieces = []
    key_accum = jnp.zeros((seq_count * keep_rows, heads_here, HS), jnp.float32)
    value_accum = jnp.zeros((seq_count * keep_rows, heads_here, HS), jnp.float32)
    for row_start, row_stop, key_stop in bounds:
        attention = block_probabilities(
            queries[row_start:row_stop],
            key_rows[:key_stop],
            query_pos[row_start:row_stop],
            query_live[row_start:row_stop],
            key_pos[:key_stop],
            key_live[:key_stop],
            score_scale,
        )
        rounded = attention.astype(jnp.bfloat16)
        grad_block = grad_heads[row_start:row_stop]
        row_delta = jnp.sum(
            grad_block.astype(jnp.float32) * attended_f[row_start:row_stop], axis=-1
        )
        grad_prob = jnp.einsum(
            "qhd,khd->hqk", grad_block, value_rows[:key_stop], preferred_element_type=jnp.float32
        )
        score_grad = (
            attention * (grad_prob - jnp.transpose(row_delta)[:, :, None]) * score_scale
        ).astype(jnp.bfloat16)
        query_pieces.append(
            jnp.einsum(
                "hqk,khd->qhd", score_grad, key_rows[:key_stop], preferred_element_type=jnp.float32
            ).astype(jnp.bfloat16)
        )
        key_accum = key_accum.at[:key_stop].add(
            jnp.einsum(
                "hqk,qhd->khd",
                score_grad,
                queries[row_start:row_stop],
                preferred_element_type=jnp.float32,
            )
        )
        value_accum = value_accum.at[:key_stop].add(
            jnp.einsum("hqk,qhd->khd", rounded, grad_block, preferred_element_type=jnp.float32)
        )
    query_grad = jnp.concatenate(query_pieces, 0).reshape(seq_count, part_rows, lane_width)
    pair_grad = jnp.concatenate(
        [
            key_accum.reshape(seq_count, keep_rows, lane_width),
            value_accum.reshape(seq_count, keep_rows, lane_width),
        ],
        -1,
    )
    query_back = lax.all_to_all(query_grad, "seq", split_axis=0, concat_axis=0, tiled=True)
    pair_back = lax.all_to_all(
        pair_grad.astype(jnp.bfloat16), "seq", split_axis=0, concat_axis=0, tiled=True
    ).astype(pair_grad.dtype)
    summed = jnp.sum(
        pair_back.reshape(head_groups, query_splits, keep_rows, 2 * lane_width), axis=1
    ).astype(jnp.bfloat16)
    query_part_rows = jnp.transpose(
        query_back.reshape(head_groups, query_splits, part_rows, lane_width), (1, 2, 0, 3)
    ).reshape(keep_rows, 1, model_width)
    pair_part_rows = jnp.transpose(
        summed.reshape(head_groups, keep_rows, 2, lane_width), (1, 2, 0, 3)
    ).reshape(keep_rows, 2, model_width)
    projected_grad = jnp.concatenate([query_part_rows, pair_part_rows], 1).reshape(
        1, keep_rows, 3 * model_width
    )
    return (output, input_grad, projected_grad, gate_grads)


def solution(mesh):
    in_specs = (
        P("exp", "seq", None),
        P("exp", "seq"),
        P("exp", "seq"),
        P("exp", "seq", None),
        P("exp", "seq", None),
        P("exp", "seq", None),
        P("exp", "seq", None),
        P("exp", "seq", None),
        P("exp", None, "seq"),
        P("exp", "seq", None),
    )
    out_specs = (
        P("exp", "seq", None),
        P("exp", "seq", None),
        P("exp", "seq", None),
        P("exp", "seq", None),
    )
    return jax.shard_map(body, mesh=mesh, in_specs=in_specs, out_specs=out_specs, check_vma=False)
```

profile of v0, /device:TPU:1, one launch (start us, length us, event | category | flops | bytes accessed | tf_op | source)
XLA Modules:
  0.0 418.0 jit_solution(2103100094838460477)
XLA Ops:
  13.7 11.9 %all-to-all-start = ((bf16[32,32,128]{2,1,0:T(8,128)(2,1)}), bf16[32,32,128]{2,1,0:T(8,128)(2,1)S(1)}, u32[]{:S(2)}, u32[]{:S(2)}) async-start(bf16[32,32,128]{2,1,0:T(8,128)(2,1)} %bitcast.294), calls=%async_computation | async-start | bytes 524288 | tf_op jit(solution)/shard_map/all_to_all | solution.py:111
  28.5 19.4 %all-reduce.4 = (s32[2048]{0:T(1024)S(1)}, s32[32]{0:T(128)S(1)}) all-reduce(s32[2048]{0:T(1024)S(1)} %bitcast_dynamic-update-slice_fusion, s32[32]{0:T(128)S(1)} %bitcast_dynamic-update-slice_fusion.1), channel_id=1, replica_groups=mesh['seq'=32,'exp'=8] {'seq'}, use_global_device_ids=true, to_apply=%add.3 | all-reduce | flops 2080 | bytes 16640 | tf_op jit(solution)/shard_map/squeeze | solution.py:92
  58.3 16.0 %fusion.70 = pred[2048]{0:T(1024)(128)(4,1)S(1)} fusion(pred[2048]{0:T(1024)(128)(4,1)S(1)} %compare_reduce_fusion, pred[2048]{0:T(1024)(128)(4,1)S(1)} %compare_reduce_fusion.1, pred[2048]{0:T(1024)(128)(4,1)S(1)} %compare_reduce_fusion.2, pred[2048]{0:T(1024)(128)(4,1)S(1)} %compare_reduce_fusion.3, pred[2048]{0:T(1024)(128)(4,1)S(1)} %compare_reduce_fusion.4, ...), kind=kLoop, calls=%fused_computation.161 | loop fusion | flops 65536 | bytes 61540 | tf_op jit(solution)/shard_map/lt | solution.py:91
  75.5 4.7 %all-to-all-start.1 = ((bf16[32,64,256]{2,1,0:T(8,128)(2,1)}), bf16[32,64,256]{2,1,0:T(8,128)(2,1)}, u32[]{:S(2)}, u32[]{:S(2)}) async-start(bf16[32,64,256]{2,1,0:T(8,128)(2,1)} %bitcast.277), calls=%async_computation.1 | async-start | bytes 2097152 | tf_op jit(solution)/shard_map/all_to_all | solution.py:112
  80.2 6.2 %gather_fusion.2 = s32[1024]{0:T(1024)S(1)} fusion(s32[2048]{0:T(1024)S(1)} %fusion.73, s32[1024]{0:T(1024)S(1)} %broadcast_clamp_fusion), kind=kCustom, calls=%fused_computation.2 | custom fusion | bytes 12288 | tf_op jit(solution)/shard_map/gather | solution.py:98
  86.4 6.8 %gather_fusion.1 = pred[1024]{0:T(1024)(128)(4,1)S(1)} fusion(pred[2048]{0:T(1024)(128)(4,1)S(1)} %fusion.70, s32[1024]{0:T(1024)S(1)} %broadcast_clamp_fusion), kind=kCustom, calls=%fused_computation.1 | custom fusion | bytes 6144 | tf_op jit(solution)/shard_map/gather | solution.py:99
  98.8 14.7 %all-to-all-done.1 = bf16[32,64,256]{2,1,0:T(8,128)(2,1)} async-done(((bf16[32,64,256]{2,1,0:T(8,128)(2,1)}), bf16[32,64,256]{2,1,0:T(8,128)(2,1)}, u32[]{:S(2)}, u32[]{:S(2)}) %all-to-all-start.1) | async-done | bytes 1048608 | tf_op jit(solution)/shard_map/all_to_all | solution.py:112
  125.3 9.6 %all-to-all-start.2 = ((bf16[32,32,128]{2,1,0:T(8,128)(2,1)}), bf16[32,32,128]{2,1,0:T(8,128)(2,1)}, u32[]{:S(2)}, u32[]{:S(2)}) async-start(bf16[32,32,128]{2,1,0:T(8,128)(2,1)} %bitcast.295), calls=%async_computation.2 | async-start | bytes 524288 | tf_op jit(solution)/shard_map/all_to_all | solution.py:147
  144.4 13.2 %all-to-all-start.5 = ((bf16[8,12,2048]{2,1,0:T(8,128)(2,1)}), bf16[8,12,2048]{2,1,0:T(8,128)(2,1)S(1)}, u32[]{:S(2)}, u32[]{:S(2)}) async-start(bf16[8,12,2048]{2,1,0:T(8,128)(2,1)} %fusion.18), calls=%async_computation.5 | async-start | bytes 1048576 | tf_op jit(solution)/shard_map/all_to_all | solution.py:199
  167.1 4.9 %all-to-all-start.3 = ((bf16[8,12,2048]{2,1,0:T(8,128)(2,1)}), bf16[8,12,2048]{2,1,0:T(8,128)(2,1)}, u32[]{:S(2)}, u32[]{:S(2)}) async-start(bf16[8,12,2048]{2,1,0:T(8,128)(2,1)} %convolution_convert_fusion), calls=%async_computation.3 | async-start | bytes 1048576 | tf_op jit(solution)/shard_map/all_to_all | solution.py:170
  172.8 8.8 %all-to-all-done.3 = bf16[8,12,2048]{2,1,0:T(8,128)(2,1)} async-done(((bf16[8,12,2048]{2,1,0:T(8,128)(2,1)}), bf16[8,12,2048]{2,1,0:T(8,128)(2,1)}, u32[]{:S(2)}, u32[]{:S(2)}) %all-to-all-start.3) | async-done | bytes 393248 | tf_op jit(solution)/shard_map/all_to_all | solution.py:170
  182.7 4.5 %fusion.6 = f32[96,1408]{1,0:T(8,128)} fusion(bf16[96,2048]{1,0:T(8,128)(2,1)S(1)} %reshape.633, bf16[1,2048,1408]{2,1,0:T(8,128)(2,1)} %all-gather.6.cloned.1.call-done), kind=kOutput, calls=%fused_computation.12 | convolution fusion | flops 553648128 | bytes 6701056 | tf_op jit(solution)/shard_map/dot_general | solution.py:42
  187.3 21.0 %all-gather.4.cloned.1.call-done = bf16[1,2048,1408]{2,1,0:T(8,128)(2,1)} async-done(((bf16[1,64,1408]{2,1,0:T(8,128)(2,1)}), bf16[1,2048,1408]{2,1,0:T(8,128)(2,1)}) %all-gather.4.cloned.1.call-update) | async-done | bytes 5767184 | tf_op jit(solution)/shard_map/all_gather | solution.py:174
  208.3 4.5 %fusion.10 = f32[96,1408]{1,0:T(8,128)} fusion(bf16[96,2048]{1,0:T(8,128)(2,1)S(1)} %reshape.633, bf16[1,2048,1408]{2,1,0:T(8,128)(2,1)} %all-gather.4.cloned.1.call-done), kind=kOutput, calls=%fused_computation.16 | convolution fusion | flops 553648128 | bytes 6701056 | tf_op jit(solution)/shard_map/dot_general | solution.py:41
  212.8 81.6 %all-gather.8.cloned.1.call-done = bf16[1,1408,2048]{1,2,0:T(8,128)(2,1)} async-done(((bf16[1,1408,64]{1,2,0:T(8,128)(2,1)}), bf16[1,1408,2048]{1,2,0:T(8,128)(2,1)}) %all-gather.8.cloned.1.call-update) | async-done | bytes 5767184 | tf_op jit(solution)/shard_map/all_gather | solution.py:176
  298.3 4.7 %fusion.4 = f32[96,2048]{1,0:T(8,128)S(1)} fusion(bf16[1,2048,1408]{2,1,0:T(8,128)(2,1)} %all-gather.6.cloned.1.call-done, f32[96,1408]{1,0:T(8,128)S(1)} %fusion, f32[96,1408]{1,0:T(8,128)S(1)} %copy-done.12), kind=kOutput, calls=%fused_computation.10 | convolution fusion | flops 554459136 | bytes 7634944 | tf_op jit(solution)/shard_map/dot_general | solution.py:52
  307.6 6.6 %all-to-all-start.6 = ((bf16[8,12,2048]{2,1,0:T(8,128)(2,1)}), bf16[8,12,2048]{2,1,0:T(8,128)(2,1)}, u32[]{:S(2)}, u32[]{:S(2)}) async-start(bf16[8,12,2048]{2,1,0:T(8,128)(2,1)} %reshape.636), calls=%async_computation.6 | async-start | bytes 1048576 | tf_op jit(solution)/shard_map/all_to_all | solution.py:205
  314.7 9.1 %all-to-all-done.6 = bf16[8,12,2048]{2,1,0:T(8,128)(2,1)} async-done(((bf16[8,12,2048]{2,1,0:T(8,128)(2,1)}), bf16[8,12,2048]{2,1,0:T(8,128)(2,1)}, u32[]{:S(2)}, u32[]{:S(2)}) %all-to-all-start.6) | async-done | bytes 393248 | tf_op jit(solution)/shard_map/all_to_all | solution.py:205
  327.0 5.2 %all-to-all-start.7 = ((bf16[32,32,128]{2,1,0:T(8,128)(2,1)}), bf16[32,32,128]{2,1,0:T(8,128)(2,1)}, u32[]{:S(2)}, u32[]{:S(2)}) async-start(bf16[32,32,128]{2,1,0:T(8,128)(2,1)} %bitcast.296), calls=%async_computation.7 | async-start | bytes 524288 | tf_op jit(solution)/shard_map/all_to_all | solution.py:228
  332.2 5.6 %fusion.22 = bf16[96,2048]{1,0:T(8,128)(2,1)} fusion(bf16[1,1408,2048]{1,2,0:T(8,128)(2,1)} %all-gather.8.cloned.1.call-done, f32[96,1408]{1,0:T(8,128)} %fusion.6, f32[96,1408]{1,0:T(8,128)} %fusion.10), kind=kOutput, calls=%fused_computation.35 | convolution fusion | flops 554655744 | bytes 7241728 | tf_op jit(solution)/shard_map/dot_general | solution.py:44
  341.9 7.6 %all-to-all-start.4 = ((bf16[8,12,2048]{2,1,0:T(8,128)(2,1)}), bf16[8,12,2048]{2,1,0:T(8,128)(2,1)}, u32[]{:S(2)}, u32[]{:S(2)}) async-start(bf16[8,12,2048]{2,1,0:T(8,128)(2,1)} %reshape.634), calls=%async_computation.4 | async-start | bytes 1048576 | tf_op jit(solution)/shard_map/all_to_all | solution.py:180
  359.1 5.0 %all-to-all-start.8 = ((bf16[32,32,128]{2,1,0:T(8,128)(2,1)}), bf16[32,32,128]{2,1,0:T(8,128)(2,1)}, u32[]{:S(2)}, u32[]{:S(2)}) async-start(bf16[32,32,128]{2,1,0:T(8,128)(2,1)} %bitcast.91), calls=%async_computation.8 | async-start | bytes 524288 | tf_op jit(solution)/shard_map/all_to_all | solution.py:279
  373.8 8.4 %all-to-all-start.9 = ((bf16[32,64,256]{2,1,0:T(8,128)(2,1)}), bf16[32,64,256]{2,1,0:T(8,128)(2,1)}, u32[]{:S(2)}, u32[]{:S(2)}) async-start(bf16[32,64,256]{2,1,0:T(8,128)(2,1)} %pad_maximum_fusion), calls=%async_computation.9 | async-start | bytes 2097152 | tf_op jit(solution)/shard_map/all_to_all | solution.py:280
  391.3 15.5 %all-to-all-done.9 = bf16[32,64,256]{2,1,0:T(8,128)(2,1)} async-done(((bf16[32,64,256]{2,1,0:T(8,128)(2,1)}), bf16[32,64,256]{2,1,0:T(8,128)(2,1)}, u32[]{:S(2)}, u32[]{:S(2)}) %all-to-all-start.9) | async-done | bytes 1048608 | tf_op jit(solution)/shard_map/all_to_all | solution.py:280
  (240 shorter events, 106.6 us)
Async XLA Ops:
  7.2 19.2 %copy-start.41 = (u32[256]{0:T(256)S(1)}, u32[256]{0:T(256)}, u32[]{:S(2)}) copy-start(u32[256]{0:T(256)} %constant.251) | copy-start | bytes 3076
  7.2 21.2 %copy-start.40 = (s32[1,64]{1,0:T(1,128)S(1)}, s32[1,64]{1,0:T(1,128)}, u32[]{:S(2)}) copy-start(s32[1,64]{1,0:T(1,128)} %param.23) | copy-start | bytes 772
  7.2 175.5 %all-gather.6.cloned.1.call-start = ((), (), s32[]{:S(2)}) async-start(), calls=%async_computation.11 | async-start | bytes 5947392 | tf_op jit(solution)/shard_map/all_gather | solution.py:175
  8.5 84.8 %copy-start.5 = (bf16[1,256,2048]{2,1,0:T(8,128)(2,1)}, bf16[1,256,2048]{2,1,0:T(8,128)(2,1)S(1)}, u32[]{:S(2)}) copy-start(bf16[1,256,2048]{2,1,0:T(8,128)(2,1)S(1)} %copy.102) | copy-start | bytes 3145732
  10.1 125.4 %copy-start.8 = (bf16[1,256,2048]{2,1,0:T(8,128)(2,1)}, bf16[1,256,2048]{2,1,0:T(8,128)(2,1)S(1)}, u32[]{:S(2)}) copy-start(bf16[1,256,2048]{2,1,0:T(8,128)(2,1)S(1)} %copy.103) | copy-start | bytes 3145732
  10.1 198.2 %all-gather.4.cloned.1.call-start = ((), (), s32[]{:S(2)}) async-start(), calls=%async_computation.10 | async-start | bytes 5947392 | tf_op jit(solution)/shard_map/all_gather | solution.py:174
  10.9 283.5 %all-gather.8.cloned.1.call-start = ((), (), s32[]{:S(2)}) async-start(), calls=%async_computation.12 | async-start | bytes 5947392 | tf_op jit(solution)/shard_map/all_gather | solution.py:176
  13.7 60.7 %all-to-all-start = ((bf16[32,32,128]{2,1,0:T(8,128)(2,1)}), bf16[32,32,128]{2,1,0:T(8,128)(2,1)S(1)}, u32[]{:S(2)}, u32[]{:S(2)}) async-start(bf16[32,32,128]{2,1,0:T(8,128)(2,1)} %bitcast.294), calls=%async_computation | async-start | bytes 524288 | tf_op jit(solution)/shard_map/all_to_all | solution.py:111
  54.5 31.9 %copy-start = (s32[2048]{0:T(1024)}, s32[2048]{0:T(1024)S(1)}, u32[]{:S(2)}) copy-start(s32[2048]{0:T(1024)S(1)} %fusion.73) | copy-start | bytes 24580
  74.4 18.8 %copy-start.1 = (pred[2048]{0:T(1024)(128)(4,1)}, pred[2048]{0:T(1024)(128)(4,1)S(1)}, u32[]{:S(2)}) copy-start(pred[2048]{0:T(1024)(128)(4,1)S(1)} %fusion.70) | copy-start | bytes 6148
  75.5 38.0 %all-to-all-start.1 = ((bf16[32,64,256]{2,1,0:T(8,128)(2,1)}), bf16[32,64,256]{2,1,0:T(8,128)(2,1)}, u32[]{:S(2)}, u32[]{:S(2)}) async-start(bf16[32,64,256]{2,1,0:T(8,128)(2,1)} %bitcast.277), calls=%async_computation.1 | async-start | bytes 2097152 | tf_op jit(solution)/shard_map/all_to_all | solution.py:112
  93.2 21.4 %slice-start = ((s32[2048]{0:T(1024)}), s32[1024]{0:T(1024)S(1)}, s32[]{:S(2)}) async-start(s32[2048]{0:T(1024)} %copy-done), calls=%async_computation.13 | async-start | bytes 8192 | tf_op jit(solution)/shard_map/slice | solution.py:134
  93.2 21.4 %slice-start.1 = ((pred[2048]{0:T(1024)(128)(4,1)}), pred[1024]{0:T(1024)(128)(4,1)S(1)}, s32[]{:S(2)}) async-start(pred[2048]{0:T(1024)(128)(4,1)} %copy-done.1), calls=%async_computation.14 | async-start | bytes 2048 | tf_op jit(solution)/shard_map/slice | solution.py:135
  125.3 19.1 %all-to-all-start.2 = ((bf16[32,32,128]{2,1,0:T(8,128)(2,1)}), bf16[32,32,128]{2,1,0:T(8,128)(2,1)}, u32[]{:S(2)}, u32[]{:S(2)}) async-start(bf16[32,32,128]{2,1,0:T(8,128)(2,1)} %bitcast.295), calls=%async_computation.2 | async-start | bytes 524288 | tf_op jit(solution)/shard_map/all_to_all | solution.py:147
  144.4 22.7 %all-to-all-start.5 = ((bf16[8,12,2048]{2,1,0:T(8,128)(2,1)}), bf16[8,12,2048]{2,1,0:T(8,128)(2,1)S(1)}, u32[]{:S(2)}, u32[]{:S(2)}) async-start(bf16[8,12,2048]{2,1,0:T(8,128)(2,1)} %fusion.18), calls=%async_computation.5 | async-start | bytes 1048576 | tf_op jit(solution)/shard_map/all_to_all | solution.py:199
  167.1 14.5 %all-to-all-start.3 = ((bf16[8,12,2048]{2,1,0:T(8,128)(2,1)}), bf16[8,12,2048]{2,1,0:T(8,128)(2,1)}, u32[]{:S(2)}, u32[]{:S(2)}) async-start(bf16[8,12,2048]{2,1,0:T(8,128)(2,1)} %convolution_convert_fusion), calls=%async_computation.3 | async-start | bytes 1048576 | tf_op jit(solution)/shard_map/all_to_all | solution.py:170
  303.0 22.2 %copy-start.13 = (bf16[64,2048]{1,0:T(8,128)(2,1)S(1)}, bf16[64,2048]{1,0:T(8,128)(2,1)}, u32[]{:S(2)}) copy-start(bf16[64,2048]{1,0:T(8,128)(2,1)} %gather_fusion.3) | copy-start | bytes 786436
  307.6 16.1 %all-to-all-start.6 = ((bf16[8,12,2048]{2,1,0:T(8,128)(2,1)}), bf16[8,12,2048]{2,1,0:T(8,128)(2,1)}, u32[]{:S(2)}, u32[]{:S(2)}) async-start(bf16[8,12,2048]{2,1,0:T(8,128)(2,1)} %reshape.636), calls=%async_computation.6 | async-start | bytes 1048576 | tf_op jit(solution)/shard_map/all_to_all | solution.py:205
  327.0 14.9 %all-to-all-start.7 = ((bf16[32,32,128]{2,1,0:T(8,128)(2,1)}), bf16[32,32,128]{2,1,0:T(8,128)(2,1)}, u32[]{:S(2)}, u32[]{:S(2)}) async-start(bf16[32,32,128]{2,1,0:T(8,128)(2,1)} %bitcast.296), calls=%async_computation.7 | async-start | bytes 524288 | tf_op jit(solution)/shard_map/all_to_all | solution.py:228
  341.9 17.2 %all-to-all-start.4 = ((bf16[8,12,2048]{2,1,0:T(8,128)(2,1)}), bf16[8,12,2048]{2,1,0:T(8,128)(2,1)}, u32[]{:S(2)}, u32[]{:S(2)}) async-start(bf16[8,12,2048]{2,1,0:T(8,128)(2,1)} %reshape.634), calls=%async_computation.4 | async-start | bytes 1048576 | tf_op jit(solution)/shard_map/all_to_all | solution.py:180
  359.1 14.6 %all-to-all-start.8 = ((bf16[32,32,128]{2,1,0:T(8,128)(2,1)}), bf16[32,32,128]{2,1,0:T(8,128)(2,1)}, u32[]{:S(2)}, u32[]{:S(2)}) async-start(bf16[32,32,128]{2,1,0:T(8,128)(2,1)} %bitcast.91), calls=%async_computation.8 | async-start | bytes 524288 | tf_op jit(solution)/shard_map/all_to_all | solution.py:279
  373.8 33.0 %all-to-all-start.9 = ((bf16[32,64,256]{2,1,0:T(8,128)(2,1)}), bf16[32,64,256]{2,1,0:T(8,128)(2,1)}, u32[]{:S(2)}, u32[]{:S(2)}) async-start(bf16[32,64,256]{2,1,0:T(8,128)(2,1)} %pad_maximum_fusion), calls=%async_computation.9 | async-start | bytes 2097152 | tf_op jit(solution)/shard_map/all_to_all | solution.py:280
  384.9 23.3 %copy-start.10 = (bf16[256,2048]{1,0:T(8,128)(2,1)}, bf16[256,2048]{1,0:T(8,128)(2,1)S(1)}, u32[]{:S(2)}) copy-start(bf16[256,2048]{1,0:T(8,128)(2,1)S(1)} %scatter_custom_fusion.1) | copy-start | bytes 3145732
  389.3 20.3 %copy-start.7 = (bf16[256,2048]{1,0:T(8,128)(2,1)}, bf16[256,2048]{1,0:T(8,128)(2,1)S(1)}, u32[]{:S(2)}) copy-start(bf16[256,2048]{1,0:T(8,128)(2,1)S(1)} %scatter_custom_fusion) | copy-start | bytes 3145732
  (35 other events, 250.6 us)
Sparse Core Ops, SparseCore 0:
  10.6 111.8 all-gather.5
  125.1 83.1 all-gather.3
  210.9 83.4 all-gather.7
where the time goes:
time: 424 us; the launch traced here: 418 us
  waiting for transfers between devices  162 us (38%)
  starting transfers between devices  77.1 us (18%)
  local copies, waits for them, and re-layouts  54 us (13%)
  matrix products  46.4 us (11%)
  other arithmetic  43.1 us (10%)
  blocking collectives  19.4 us (5%)
  between operations  16.1 us (4%)
    all_gather x1, waiting for transfers between devices, body(): lax.all_gather(down_weight, 'seq', axis=2, tiled=True)  81.6 us
    all_gather x1, waiting for transfers between devices, body(): lax.all_gather(gate_weight, 'seq', axis=1, tiled=True)  21 us
    squeeze x1, blocking collectives, body(): key_pos = key_shard * tok_dev + every_index[0]  19.4 us
    lt x1, other arithmetic, body(): key_live = entries % keep_rows < every_count[0][key_shard]  16 us
    all_to_all x1, waiting for transfers between devices, body(): lax.all_to_all(pair_grad.astype(jnp.bfloat16), 'seq', split_axis=0, conca...  15.5 us
    all_to_all x1, waiting for transfers between devices, body(): lax.all_to_all(pair_send, 'seq', split_axis=0, concat_axis=0, tiled=True)  14.7 us
    all_to_all x1, starting transfers between devices, body(): lax.all_to_all(expert_grad, 'exp', split_axis=0, concat_axis=0, tiled=True)  13.2 us
    unnamed x102, local copies, waits for them, and re-layouts  12.8 us
  transfers between devices with their start and end apart: 13, of which 11 were waited for; matrix products, arithmetic and copies ran while one was open for 28% of the time, Pallas kernels for 0%

commit v1 on v0

v1 whole, which is shorter than its diff:
```python
import functools

import jax
import jax.numpy as jnp
from jax import lax
from jax.experimental import pallas as pl
from jax.experimental.pallas import tpu as pltpu
from jax.sharding import PartitionSpec as P

HS = 128
SLOT = 16
EPSILON = 1e-06
X = 4
QSRC = 8
F32 = jnp.float32
BF16 = jnp.bfloat16
MESH = pl.DeviceIdType.MESH
NEG = -1e30


def nn(a, b):
    return lax.dot_general(a, b, (((1,), (0,)), ((), ())), preferred_element_type=F32)


def nt(a, b):
    return lax.dot_general(a, b, (((1,), (1,)), ((), ())), preferred_element_type=F32)


def kernel(
    S,
    E,
    residual,
    kept_index,
    kept_count,
    projected,
    expert_ids,
    gate_values,
    gate_w,
    up_w,
    down_w,
    cotangent,
    output,
    input_grad,
    projected_grad,
    gate_grads,
    q_send,
    q_recv,
    a_send,
    a_recv,
    g_send,
    g_recv,
    b_send,
    b_recv,
    x_send,
    x_recv,
    gu,
    dn,
    bias,
    k_t,
    v_t,
    prob,
    att_t,
    dk_acc,
    dv_acc,
    q_ss,
    q_rs,
    a_ss,
    a_rs,
    g_ss,
    g_rs,
    b_ss,
    b_rs,
    x_ss,
    x_rs,
    gu_rs,
    dn_rs,
    gu_zs,
    gu_xs,
    dn_xs,
    dn_zs,
):
    Z = S // X
    KEEP = kept_index.shape[1]
    TOK, D = residual.shape
    FF = gate_w.shape[1]
    HEADS = D // HS
    SPLIT = S // HEADS
    PR = KEEP // SPLIT
    NB = S // QSRC
    KB = QSRC * KEEP
    QB = QSRC * PR
    NS = E * SLOT
    XD = X
    scale = HS**-0.5
    me = lax.axis_index("seq")
    ex = lax.axis_index("exp")
    mx = me // Z
    mz = lax.rem(me, Z)
    part = lax.rem(me, SPLIT)

    barrier = pltpu.get_barrier_semaphore()

    def greet_seq(k, c):
        pl.semaphore_signal(
            barrier, inc=1, device_id={"seq": lax.rem(me + k, S)}, device_id_type=MESH
        )
        return c

    def greet_exp(k, c):
        pl.semaphore_signal(
            barrier, inc=1, device_id={"exp": lax.rem(ex + k, E)}, device_id_type=MESH
        )
        return c

    lax.fori_loop(1, S, greet_seq, 0)
    lax.fori_loop(1, E, greet_exp, 0)

    count = kept_count[...]
    meta = jnp.broadcast_to(count.astype(F32), (16, HS)).astype(BF16)
    for d in range(S):
        h, p = d // SPLIT, d % SPLIT
        c0 = h * HS
        q_send[d, 0:KEEP] = projected[:, D + c0 : D + c0 + HS]
        q_send[d, KEEP : 2 * KEEP] = projected[:, 2 * D + c0 : 2 * D + c0 + HS]
        q_send[d, 2 * KEEP : 2 * KEEP + PR] = projected[p * PR : (p + 1) * PR, c0 : c0 + HS]
        q_send[d, 2 * KEEP + PR :] = meta
    gu[mx, mz, 0] = gate_w[...]
    gu[mx, mz, 1] = up_w[...]
    dn[mx, mz] = down_w[...]
    q_recv[me] = q_send[me]

    pl.semaphore_wait(barrier, S - 1 + E - 1)

    def to_seq(send, recv, ss, rs, d):
        return pltpu.make_async_remote_copy(
            src_ref=send.at[d],
            dst_ref=recv.at[me],
            send_sem=ss.at[d],
            recv_sem=rs.at[me],
            device_id={"seq": d},
            device_id_type=MESH,
        )

    def from_seq(send, recv, ss, rs, d):
        return pltpu.make_async_remote_copy(
            src_ref=send.at[d],
            dst_ref=recv.at[d],
            send_sem=ss.at[d],
            recv_sem=rs.at[d],
            device_id={"seq": d},
            device_id_type=MESH,
        )

    def start_all(*arrays):
        def step(k, c):
            to_seq(*arrays, lax.rem(me + k, S)).start()
            return c

        lax.fori_loop(1, S, step, 0)

    def start_block(block, *arrays):
        def step(k, c):
            d = block * QSRC + lax.rem(me + k, QSRC)

            @pl.when(d != me)
            def _():
                to_seq(*arrays, d).start()

            return c

        lax.fori_loop(0, QSRC, step, 0)

    def recv_all(*arrays):
        def step(k, c):
            from_seq(*arrays, lax.rem(me + k, S)).wait_recv()
            return c

        lax.fori_loop(1, S, step, 0)

    def sent_all(*arrays):
        def step(k, c):
            to_seq(*arrays, lax.rem(me + k, S)).wait_send()
            return c

        lax.fori_loop(1, S, step, 0)

    def exp_copy(n, d, slot):
        return pltpu.make_async_remote_copy(
            src_ref=x_send.at[n, d],
            dst_ref=x_recv.at[n, slot],
            send_sem=x_ss.at[n, d],
            recv_sem=x_rs.at[n, slot],
            device_id={"exp": d},
            device_id_type=MESH,
        )

    def exp_start(n):
        x_recv[n, ex] = x_send[n, ex]

        def step(k, c):
            exp_copy(n, lax.rem(ex + k, E), ex).start()
            return c

        lax.fori_loop(1, E, step, 0)

    def exp_recv(n):
        def step(k, c):
            d = lax.rem(ex + k, E)
            exp_copy(n, d, d).wait_recv()
            return c

        lax.fori_loop(1, E, step, 0)

    def exp_sent(n):
        def step(k, c):
            exp_copy(n, lax.rem(ex + k, E), ex).wait_send()
            return c

        lax.fori_loop(1, E, step, 0)

    sent = []

    def at_x(o):
        return lax.rem(mx + o + X, X)

    def at_z(o):
        return lax.rem(mz + o + Z, Z)

    def piece(ref, sems, ox, oz, half, dev, ss):
        ax, az = at_x(ox), at_z(oz)
        view = ref.at[ax, az]
        if half is not None:
            view = ref.at[ax, az, half]
        return pltpu.make_async_remote_copy(
            src_ref=view,
            dst_ref=view,
            send_sem=ss,
            recv_sem=sems.at[ax, az, half or 0],
            device_id={"seq": dev},
            device_id_type=MESH,
        )

    def send(ref, sems, ox, oz, half, dev, ss):
        copy = piece(ref, sems, ox, oz, half, dev, ss)
        copy.start()
        sent.append(copy)

    def wait(ref, sems, ox, oz, halves):
        for half in (0, 1) if halves else (None,):
            piece(ref, sems, ox, oz, half, me, gu_zs.at[0, 0]).wait_recv()

    def side(axis, sgn):
        if axis == "x":
            return at_x(sgn) * Z + mz
        return mx * Z + at_z(sgn)

    def hop(ref, sems, axis, sgn, k, other, ss):
        n = X if axis == "x" else Z
        if k >= n // 2:
            return
        half = None if k < n // 2 - 1 else (0 if sgn > 0 else 1)
        ox, oz = (-sgn * k, other) if axis == "x" else (other, -sgn * k)
        send(ref, sems, ox, oz, half, side(axis, sgn), ss.at[0 if sgn > 0 else 1, other % 8, k])

    def gu_z(sgn, k):
        hop(gu, gu_rs, "z", sgn, k, 0, gu_zs)

    def gu_x(sgn, k, oz):
        hop(gu, gu_rs, "x", sgn, k, oz, gu_xs)

    def dn_x(sgn, k):
        hop(dn, dn_rs, "x", sgn, k, 0, dn_xs)

    def dn_z(sgn, k, ox):
        hop(dn, dn_rs, "z", sgn, k, ox, dn_zs)

    both = (1, -1)

    def gu_along_z(k):
        if k == Z // 2:
            wait(gu, gu_rs, 0, k, True)
            for s in both:
                gu_x(s, 0, k)
            return
        for s in both:
            wait(gu, gu_rs, 0, -s * k, False)
            gu_z(s, k)
            for t in both:
                gu_x(t, 0, -s * k)

    def gu_along_x(oz):
        for s in both:
            wait(gu, gu_rs, -s, oz, False)
            gu_x(s, 1, oz)

    def dn_along_x(k):
        if k == X // 2:
            wait(dn, dn_rs, k, 0, True)
            for s in both:
                dn_z(s, 0, k)
            return
        for s in both:
            wait(dn, dn_rs, -s * k, 0, False)
            dn_x(s, k)
            for t in both:
                dn_z(t, 0, -s * k)

    def dn_along_z(k, ox):
        for s in both:
            wait(dn, dn_rs, ox, -s * k, False)
            dn_z(s, k, ox)

    def ring_start():
        for s in both:
            gu_z(s, 0)
        for s in both:
            dn_x(s, 0)
        for s in both:
            gu_x(s, 0, 0)
        for s in both:
            dn_z(s, 0, 0)

    def ring_first():
        dn_along_x(1)
        gu_along_z(1)
        dn_along_x(2)
        gu_along_x(0)
        dn_along_z(1, 0)

    def ring_round(k):
        gu_along_z(k)
        for oz in (k - 1, 1 - k):
            gu_along_x(oz)
        if k < Z // 2:
            for ox in (1, -1, 2):
                dn_along_z(k - 1, ox)
            dn_along_z(k, 0)
        else:
            for ox in (1, -1, 2):
                dn_along_z(k - 1, ox)

    def ring_last():
        gu_along_x(Z // 2)
        for oz in range(Z):
            wait(gu, gu_rs, X // 2, oz, True)
        for ox in (0, 1, -1, 2):
            wait(dn, dn_rs, ox, Z // 2, True)

    start_all(q_send, q_recv, q_ss, q_rs)
    ring_start()

    slot_row = lax.broadcasted_iota(jnp.int32, (NS, KEEP), 0)
    slot_exp = slot_row // SLOT
    slot_pos = slot_row - slot_exp * SLOT
    entry = lax.broadcasted_iota(jnp.int32, (NS, KEEP), 1)
    live = entry < count
    assigned = jnp.zeros((NS, KEEP), F32)
    weight = jnp.zeros((NS, KEEP), F32)
    for k in range(expert_ids.shape[0]):
        match = (expert_ids[k : k + 1, :] == slot_exp) & live
        assigned = assigned + jnp.where(match, 1.0, 0.0)
        weight = weight + jnp.where(match, gate_values[k : k + 1, :], 0.0)
    ei = lax.broadcasted_iota(jnp.int32, (KEEP, KEEP), 0)
    ej = lax.broadcasted_iota(jnp.int32, (KEEP, KEEP), 1)
    earlier = jnp.where(ei < ej, 1.0, 0.0).astype(BF16)
    rank = nn(assigned.astype(BF16), earlier)
    table = jnp.where((assigned > 0.5) & (rank == slot_pos.astype(F32)), 1.0, 0.0)
    table_half = table.astype(BF16)
    weighted = table * weight
    slot_gate = jnp.sum(weighted, axis=1, keepdims=True)

    def turned(a):
        if a.shape[1] < 128:
            a = jnp.concatenate([a, jnp.zeros((a.shape[0], 128 - a.shape[1]), F32)], 1)
        return a.T

    table_t = turned(table)[:KEEP].astype(BF16)
    weighted_t = turned(weighted)[:KEEP]
    w_high = weighted_t.astype(BF16)
    w_low = (weighted_t - w_high.astype(F32)).astype(BF16)

    index_row = kept_index[...]
    index_col = jnp.sum(jnp.where(ei == ej, index_row, 0), axis=1, keepdims=True)
    pick = jnp.where(
        lax.broadcasted_iota(jnp.int32, (KEEP, TOK), 1) == index_col, 1.0, 0.0
    ).astype(BF16)
    live_col = lax.broadcasted_iota(jnp.int32, (KEEP, 1), 0) < count
    grad_f = nn(pick, cotangent[...])
    kept_f = nn(pick, residual[...])
    grad_sel = nn(table_half, grad_f.astype(BF16))
    x_send[0] = (slot_gate * grad_sel).astype(BF16).reshape(E, SLOT, D)
    grad_sel = grad_sel.astype(BF16)
    exp_start(0)

    ring_first()
    recv_all(q_send, q_recv, q_ss, q_rs)

    row_in = lax.broadcasted_iota(jnp.int32, (S, KEEP, HS), 1).astype(F32)
    counts = q_recv[:, 2 * KEEP + PR : 2 * KEEP + PR + 16, :].astype(F32)[:, 0:1, :]
    bias[...] = jnp.where(row_in < counts, 0.0, NEG).reshape(S * KEEP, HS)
    for b in range(NB):
        k_blk = q_recv[b * QSRC : (b + 1) * QSRC, 0:KEEP].reshape(KB, HS)
        v_blk = q_recv[b * QSRC : (b + 1) * QSRC, KEEP : 2 * KEEP].reshape(KB, HS)
        k_t[:, b * KB : (b + 1) * KB] = k_blk.astype(F32).T.astype(BF16)
        v_t[:, b * KB : (b + 1) * KB] = v_blk.astype(F32).T.astype(BF16)

    qcol = lax.broadcasted_iota(jnp.int32, (KB, QB), 1)
    qent = (qcol // PR) * KEEP + part * PR + lax.rem(qcol, PR)
    causal = lax.broadcasted_iota(jnp.int32, (KB, QB), 0) <= qent

    def key_block(c):
        return q_recv[c * QSRC : (c + 1) * QSRC, 0:KEEP].reshape(KB, HS)

    def value_block(c):
        return q_recv[c * QSRC : (c + 1) * QSRC, KEEP : 2 * KEEP].reshape(KB, HS)

    def query_block(b):
        return q_recv[b * QSRC : (b + 1) * QSRC, 2 * KEEP : 2 * KEEP + PR].reshape(QB, HS)

    def forward_block(b):
        cols = slice(b * QB, (b + 1) * QB)
        q_blk = query_block(b)
        top = None
        for c in range(b + 1):
            rows = slice(c * KB, (c + 1) * KB)
            half = bias[rows, :]
            sc = nt(key_block(c), q_blk) * scale + jnp.concatenate([half] * (QB // HS), 1)
            if c == b:
                sc = jnp.where(causal, sc, NEG)
            prob[rows, cols] = sc
            m = jnp.max(sc, axis=0, keepdims=True)
            top = m if top is None else jnp.maximum(top, m)
        total = jnp.zeros((1, QB), F32)
        for c in range(b + 1):
            rows = slice(c * KB, (c + 1) * KB)
            e = jnp.exp(prob[rows, cols] - top)
            prob[rows, cols] = e
            total = total + jnp.sum(e, axis=0, keepdims=True)
        inv = 1.0 / total
        acc = jnp.zeros((HS, QB), F32)
        for c in range(b + 1):
            rows = slice(c * KB, (c + 1) * KB)
            pr = prob[rows, cols] * inv
            prob[rows, cols] = pr
            acc = acc + nn(v_t[:, rows], pr.astype(BF16))
        att_t[:, cols] = acc
        a_send[b * QSRC : (b + 1) * QSRC] = acc.T.astype(BF16).reshape(QSRC, PR, HS)
        start_block(b, a_send, a_recv, a_ss, a_rs)

    for b in range(NB):
        forward_block(b)
        if b == 1:
            ring_round(2)
    a_recv[me] = a_send[me]
    recv_all(a_send, a_recv, a_ss, a_rs)

    def rows_of(recv):
        parts = []
        for p in range(SPLIT):
            parts.append(jnp.concatenate([recv[h * SPLIT + p] for h in range(HEADS)], 1))
        return jnp.concatenate(parts, 0)

    h1 = jnp.where(live_col, kept_f + rows_of(a_recv).astype(F32), 0.0)
    inv_rms = lax.rsqrt(jnp.mean(h1 * h1, axis=1, keepdims=True) + EPSILON)
    normed = (h1 * inv_rms).astype(BF16)
    x_send[1] = nn(table_half, normed).astype(BF16).reshape(E, SLOT, D)
    exp_start(1)
    for k in range(3, Z // 2 + 1):
        ring_round(k)
    exp_recv(0)
    exp_recv(1)
    ring_last()

    rows_in = x_recv[1].reshape(NS, D)
    grads_in = x_recv[0].reshape(NS, D)
    KC = Z * KEEP
    gate_pre = jnp.zeros((NS, FF), F32)
    up_pre = jnp.zeros((NS, FF), F32)
    mid_grad = jnp.zeros((NS, FF), F32)
    for c in range(XD):
        r = rows_in[:, c * KC : (c + 1) * KC]
        gate_pre = gate_pre + nn(r, gu[c, :, 0].reshape(KC, FF))
        up_pre = up_pre + nn(r, gu[c, :, 1].reshape(KC, FF))
        mid_grad = mid_grad + nn(
            grads_in[:, c * KC : (c + 1) * KC], dn[c].reshape(KC, FF)
        )
    sig = 1.0 / (1.0 + jnp.exp(-gate_pre))
    act = gate_pre * sig
    gate_grad = (mid_grad * up_pre * sig * (1.0 + gate_pre * (1.0 - sig))).astype(BF16)
    up_grad = (mid_grad * act).astype(BF16)
    mid = (act * up_pre).astype(BF16)
    for c in range(XD):
        back = nt(gate_grad, gu[c, :, 0].reshape(KC, FF)) + nt(
            up_grad, gu[c, :, 1].reshape(KC, FF)
        )
        x_send[2, :, :, c * KC : (c + 1) * KC] = back.astype(BF16).reshape(E, SLOT, KC)
    exp_start(2)
    for c in range(XD):
        made = nt(mid, dn[c].reshape(KC, FF))
        x_send[3, :, :, c * KC : (c + 1) * KC] = made.astype(BF16).reshape(E, SLOT, KC)
    exp_start(3)
    exp_recv(2)
    normed_grad = nn(table_t, x_recv[2].reshape(NS, D))
    cubed = inv_rms * inv_rms * inv_rms
    h1_grad = (
        grad_f
        + inv_rms * normed_grad
        - h1 * cubed * jnp.mean(normed_grad * h1, axis=1, keepdims=True)
    )
    h1_grad = jnp.where(live_col, h1_grad, 0.0).astype(BF16)
    for d in range(S):
        h, p = d // SPLIT, d % SPLIT
        g_send[d] = h1_grad[p * PR : (p + 1) * PR, h * HS : (h + 1) * HS]
    g_recv[me] = g_send[me]
    start_all(g_send, g_recv, g_ss, g_rs)

    token = lax.broadcasted_iota(jnp.int32, (TOK, KEEP), 0)
    put = jnp.where(
        (token == index_row)
        & (lax.broadcasted_iota(jnp.int32, (TOK, KEEP), 1) < count),
        1.0,
        0.0,
    )
    replaced = jnp.sum(put, axis=1, keepdims=True) > 0.5
    put = put.astype(BF16)
    input_grad[...] = jnp.where(replaced, nn(put, h1_grad), cotangent[...].astype(F32)).astype(
        BF16
    )
    exp_recv(3)
    results = x_recv[3].reshape(NS, D)
    mixture = nn(w_high, results) + nn(w_low, results)
    new_rows = (h1 + mixture).astype(BF16)
    output[...] = jnp.where(replaced, nn(put, new_rows), residual[...].astype(F32)).astype(BF16)
    per_slot = jnp.sum(results.astype(F32) * grad_sel.astype(F32), axis=1, keepdims=True)
    spread = table * per_slot
    for k in range(expert_ids.shape[0]):
        hit = expert_ids[k : k + 1, :] == slot_exp
        gate_grads[k : k + 1, :] = jnp.sum(jnp.where(hit, spread, 0.0), axis=0, keepdims=True)

    recv_all(g_send, g_recv, g_ss, g_rs)
    dk_acc[...] = jnp.zeros_like(dk_acc)
    dv_acc[...] = jnp.zeros_like(dv_acc)
    for b in reversed(range(NB)):
        cols = slice(b * QB, (b + 1) * QB)
        q_blk = query_block(b)
        dout = g_recv[b * QSRC : (b + 1) * QSRC].reshape(QB, HS)
        delta = jnp.sum(dout.astype(F32).T * att_t[:, cols], axis=0, keepdims=True)
        dq_t = jnp.zeros((HS, QB), F32)
        for c in range(b + 1):
            rows = slice(c * KB, (c + 1) * KB)
            pr = prob[rows, cols]
            ds = (pr * (nt(value_block(c), dout) - delta) * scale).astype(BF16)
            dq_t = dq_t + nn(k_t[:, rows], ds)
            dk_acc[rows] += nn(ds, q_blk)
            dv_acc[rows] += nn(pr.astype(BF16), dout)
        rows = slice(b * KB, (b + 1) * KB)
        src = slice(b * QSRC, (b + 1) * QSRC)
        b_send[src, 0:KEEP] = dk_acc[rows].astype(BF16).reshape(QSRC, KEEP, HS)
        b_send[src, KEEP : 2 * KEEP] = dv_acc[rows].astype(BF16).reshape(QSRC, KEEP, HS)
        b_send[src, 2 * KEEP :] = dq_t.T.astype(BF16).reshape(QSRC, PR, HS)
        start_block(b, b_send, b_recv, b_ss, b_rs)
    b_recv[me] = b_send[me]
    recv_all(b_send, b_recv, b_ss, b_rs)
    for h in range(HEADS):
        c0 = h * HS
        dk = b_recv[h * SPLIT, 0:KEEP].astype(F32)
        dv = b_recv[h * SPLIT, KEEP : 2 * KEEP].astype(F32)
        for p in range(SPLIT):
            projected_grad[p * PR : (p + 1) * PR, c0 : c0 + HS] = b_recv[
                h * SPLIT + p, 2 * KEEP :
            ]
            if p:
                dk = dk + b_recv[h * SPLIT + p, 0:KEEP].astype(F32)
                dv = dv + b_recv[h * SPLIT + p, KEEP : 2 * KEEP].astype(F32)
        projected_grad[:, D + c0 : D + c0 + HS] = dk.astype(BF16)
        projected_grad[:, 2 * D + c0 : 2 * D + c0 + HS] = dv.astype(BF16)

    sent_all(q_send, q_recv, q_ss, q_rs)
    sent_all(a_send, a_recv, a_ss, a_rs)
    sent_all(g_send, g_recv, g_ss, g_rs)
    sent_all(b_send, b_recv, b_ss, b_rs)
    for n in range(4):
        exp_sent(n)
    for copy in sent:
        copy.wait_send()


def body(
    residual,
    kept_index,
    kept_count,
    projected,
    expert_ids,
    gate_values,
    gate_weight,
    up_weight,
    down_weight,
    cotangent,
):
    S = lax.axis_size("seq")
    E = lax.axis_size("exp")
    _, TOK, D = residual.shape
    KEEP = kept_index.shape[1]
    FF = gate_weight.shape[2]
    TOPK = expert_ids.shape[2]
    Z = S // X
    HEADS = D // HS
    PR = KEEP * HEADS // S
    vm = pl.BlockSpec(memory_space=pltpu.VMEM)
    dma = pltpu.SemaphoreType.DMA
    pay = 2 * KEEP + PR + 16
    back = 2 * KEEP + PR
    out = pl.pallas_call(
        functools.partial(kernel, S, E),
        out_shape=[
            jax.ShapeDtypeStruct((TOK, D), BF16),
            jax.ShapeDtypeStruct((TOK, D), BF16),
            jax.ShapeDtypeStruct((KEEP, 3 * D), BF16),
            jax.ShapeDtypeStruct((TOPK, KEEP), F32),
        ],
        in_specs=[vm] * 10,
        out_specs=[vm] * 4,
        scratch_shapes=[
            pltpu.VMEM((S, pay, HS), BF16),
            pltpu.VMEM((S, pay, HS), BF16),
            pltpu.VMEM((S, PR, HS), BF16),
            pltpu.VMEM((S, PR, HS), BF16),
            pltpu.VMEM((S, PR, HS), BF16),
            pltpu.VMEM((S, PR, HS), BF16),
            pltpu.VMEM((S, back, HS), BF16),
            pltpu.VMEM((S, back, HS), BF16),
            pltpu.VMEM((4, E, SLOT, D), BF16),
            pltpu.VMEM((4, E, SLOT, D), BF16),
            pltpu.VMEM((X, Z, 2, KEEP, FF), BF16),
            pltpu.VMEM((X, Z, 2, KEEP // 2, FF), BF16),
            pltpu.VMEM((S * KEEP, HS), F32),
            pltpu.VMEM((HS, S * KEEP), BF16),
            pltpu.VMEM((HS, S * KEEP), BF16),
            pltpu.VMEM((S * KEEP, S * PR), F32),
            pltpu.VMEM((HS, S * PR), F32),
            pltpu.VMEM((S * KEEP, HS), F32),
            pltpu.VMEM((S * KEEP, HS), F32),
        ]
        + [dma((S,))] * 8
        + [dma((4, E))] * 2
        + [
            dma((X, Z, 2)),
            dma((X, Z, 2)),
            dma((2, 8, Z // 2)),
            dma((2, 8, X // 2)),
            dma((2, 8, X // 2)),
            dma((2, 8, Z // 2)),
        ],
        compiler_params=pltpu.CompilerParams(
            collective_id=0, has_side_effects=True, vmem_limit_bytes=60 * 1024 * 1024
        ),
    )(
        residual[0],
        kept_index,
        kept_count,
        projected[0],
        expert_ids[0].T,
        gate_values[0].T,
        gate_weight[0],
        up_weight[0],
        down_weight[0].T.reshape(2, KEEP // 2, FF),
        cotangent[0],
    )
    return (out[0][None], out[1][None], out[2][None], out[3].T[None])


def solution(mesh):
    row = P("exp", "seq", None)
    in_specs = (row, P("exp", "seq"), P("exp", "seq")) + (row,) * 5 + (P("exp", None, "seq"), row)
    return jax.shard_map(
        body, mesh=mesh, in_specs=in_specs, out_specs=(row,) * 4, check_vma=False
    )
```

time: 424 us -> 237 us (0.56); the launches traced: 418 us -> 237 us
  Pallas kernels: 0 us -> 227 us
  waiting for transfers between devices: 162 us -> 0 us
  starting transfers between devices: 77.1 us -> 0 us
  matrix products: 46.4 us -> 0 us
  local copies, waits for them, and re-layouts: 54 us -> 7.99 us
  other arithmetic: 43.1 us -> 0 us
  blocking collectives: 19.4 us -> 0 us
  between operations: 16.1 us -> 1.31 us
    pallas_call x0 -> x1, Pallas kernels: none -> 227 us  [body(): pl.pallas_call(functools.partial(kernel, S, E), out_shape=[jax.ShapeDtype...]
    all_gather x3 -> x0, waiting for transfers between devices: 103 us -> none  [the longest x1 81.6 us: body(): lax.all_gather(down_weight, 'seq', axis=2, tiled=True)]
    all_to_all x10 -> x0, starting transfers between devices: 77 us -> none  [the longest x1 13.2 us: body(): lax.all_to_all(expert_grad, 'exp', split_axis=0, concat_axis=0, tiled=True)]
    all_to_all x10 -> x0, waiting for transfers between devices: 57.9 us -> none  [the longest x1 15.5 us: body(): lax.all_to_all(pair_grad.astype(jnp.bfloat16), 'seq', split_axis=0, conca...]
    dot_general x22 -> x0, matrix products: 46.4 us -> none  [the longest x1 5.64 us: expert_forward(): jnp.dot(middle, down_w, preferred_element_type=jnp.float32)]
    squeeze x1 -> x0, blocking collectives: 19.4 us -> none  [body(): key_pos = key_shard * tok_dev + every_index[0]]
    gather x6 -> x0, local copies, waits for them, and re-layouts: 16.6 us -> none  [the longest x1 6.8 us: body(): query_live = key_live[query_index]]
    lt x3 -> x0, other arithmetic: 16.5 us -> none  [the longest x1 16 us: body(): key_live = entries % keep_rows < every_count[0][key_shard]]
  transfers between devices with their start and end apart: 13 -> 0, of which waited for: 11 -> 0; matrix products, arithmetic and copies ran while one was open for 28% -> 0% of each run, Pallas kernels for 0% -> 0%
where the time goes in v1:
time: 237 us
  Pallas kernels  227 us (96%)
  local copies, waits for them, and re-layouts  7.99 us (3%)
    pallas_call x1, Pallas kernels, body(): pl.pallas_call(functools.partial(kernel, S, E), out_shape=[jax.ShapeDtype...  227 us
    unnamed x16, local copies, waits for them, and re-layouts  7.99 us

profile of v1, /device:TPU:1, one launch (start us, length us, event | category | flops | bytes accessed | tf_op | source)
XLA Modules:
  0.0 236.5 jit_solution(17221157816408699962)
XLA Ops:
  1.3 0.0 copy-start.3
  1.3 0.7 copy-done.3
  2.0 0.0 copy-start.4
  2.0 0.6 copy.20
  2.6 0.1 copy-done.4
  2.7 0.6 copy.19
  3.2 227.2 %shard_map.129 = (bf16[256,2048]{1,0:T(8,128)(2,1)}, bf16[256,2048]{1,0:T(8,128)(2,1)}, bf16[64,6144]{1,0:T(8,128)(2,1)}, f32[6,64]{1,0:T(8,128)}) custom-call(bf16[256,2048]{1,0:T(8,128)(2,1)} %bitcast.26, s32[1,64]{1,0:T(1,128)} %kept_index.1, s32[1,1]{1,0:T(1,128)S(6)} %copy.24.kept_count, bf16[64,6144]{1,0:T(8,128)(2,1)} %bitcast.31, s32[6,64]{1,0:T(8,128)} %bitcast.35, ...), custom_call_target="tpu_custom_call" | custom-call | tf_op jit(solution)/shard_map/pallas_call | solution.py:613
  230.5 0.0 copy-start.2
  230.5 0.7 copy-done.2
  231.2 0.6 copy.14
  231.7 0.0 copy-start
  231.7 2.4 %copy.25 = bf16[1,256,2048]{2,1,0:T(8,128)(2,1)} copy(bf16[1,256,2048]{2,1,0:T(8,128)(2,1)} %bitcast.29) | data formatting | bytes 2097152
  234.1 0.0 copy-done
  234.1 0.0 copy-start.1
  234.1 1.0 copy.26
  235.1 0.5 copy-done.1
  235.7 0.9 copy.27
Async XLA Ops:
  1.3 0.7 copy-start.3
  2.0 0.7 copy-start.4
  230.5 0.7 copy-start.2
  231.7 2.4 %copy-start = (bf16[256,2048]{1,0:T(8,128)(2,1)S(1)}, bf16[256,2048]{1,0:T(8,128)(2,1)}, u32[]{:S(2)}) copy-start(bf16[256,2048]{1,0:T(8,128)(2,1)} %get-tuple-element.9) | copy-start | bytes 3145732
  234.1 1.5 copy-start.1

commit v2 on v1

v2 whole, which is shorter than its diff:
```python
import functools

import jax
import jax.numpy as jnp
from jax import lax
from jax.experimental import pallas as pl
from jax.experimental.pallas import tpu as pltpu
from jax.sharding import PartitionSpec as P

HS = 128
SLOT = 16
EPSILON = 1e-06
X = 4
QSRC = 8
F32 = jnp.float32
BF16 = jnp.bfloat16
MESH = pl.DeviceIdType.MESH
NEG = -1e30
MARK = 1024.0


def nn(a, b):
    return lax.dot_general(a, b, (((1,), (0,)), ((), ())), preferred_element_type=F32)


def nt(a, b):
    return lax.dot_general(a, b, (((1,), (1,)), ((), ())), preferred_element_type=F32)


def kernel(
    S,
    E,
    residual,
    kept_index,
    kept_count,
    projected,
    expert_ids,
    gate_values,
    gate_w,
    up_w,
    down_w,
    cotangent,
    output,
    input_grad,
    projected_grad,
    gate_grads,
    kv_send,
    kv,
    q_send,
    q_recv,
    a_send,
    a_recv,
    g_send,
    g_recv,
    b_send,
    b_recv,
    x_send,
    x_recv,
    gu,
    dn,
    bias,
    k_t,
    v_t,
    prob,
    att_t,
    acc,
    other,
    kv_ss,
    q_ss,
    g_ss,
    a_rs,
    b_rs,
    kv_rs,
    q_rs,
    g_rs,
    a_ss,
    b_ss,
    x_ss,
    x_rs,
    swap_ss,
    swap_rs,
    gu_rs,
    dn_rs,
    ring_ss,
    pair_ss,
    core_ss,
    init_ss,
):
    Z = S // X
    KEEP = kept_index.shape[1]
    TOK, D = residual.shape
    FF = gate_w.shape[1]
    HEADS = D // HS
    PR = KEEP // 2
    NB = S // QSRC
    KB = QSRC * KEEP
    QB = QSRC * PR
    NS = E * SLOT
    scale = HS**-0.5
    me = lax.axis_index("seq")
    ex = lax.axis_index("exp")
    mx = me // Z
    mz = lax.rem(me, Z)
    yy = ex // 2
    core = lax.rem(ex, 2)
    sib = 1 - core
    grp = mx // 2
    mirror = X - 1 - mx
    partner = 4 * grp + 1 - mx
    head = me // 2
    par = lax.rem(me, 2)
    expert = 2 * yy + grp

    barrier = pltpu.get_barrier_semaphore()

    def greet(seq, exp):
        pl.semaphore_signal(
            barrier, inc=1, device_id={"seq": seq, "exp": exp}, device_id_type=MESH
        )

    def greet_plane(k, t):
        i = lax.rem(2 * me + core + k, 2 * S)
        greet(i // 2, 2 * yy + lax.rem(i, 2))
        return t

    def greet_others(k, t):
        e = lax.rem(2 * yy + 2 + k, E)
        greet(me, e)
        greet(mirror * Z + mz, e)
        return t

    lax.fori_loop(1, 2 * S, greet_plane, 0)
    lax.fori_loop(0, E - 2, greet_others, 0)

    count = kept_count[...]
    live_col = lax.broadcasted_iota(jnp.int32, (KEEP, 1), 0) < count
    for h in range(HEADS):
        c0 = h * HS
        keys = projected[:, D + c0 : D + c0 + HS].astype(F32)
        kv_send[0, h] = jnp.where(live_col, keys, MARK).astype(BF16)
        kv_send[1, h] = projected[:, 2 * D + c0 : 2 * D + c0 + HS]
        for p in range(2):
            q_send[p, h] = projected[p * PR : (p + 1) * PR, c0 : c0 + HS]

    @pl.when(par == core)
    def _():
        kv[core, me] = kv_send[core, head]
        q_recv[me] = q_send[core, head]

    origin = mx + core * (X - 1 - 2 * mx)
    origin_p = partner + core * (X - 1 - 2 * partner)
    other_o = mx + sib * (X - 1 - 2 * mx)
    other_p = partner + sib * (X - 1 - 2 * partner)

    @pl.when((core == 0) & (grp == 0))
    def _():
        gu[mx, mz, 0] = gate_w[...]
        gu[mx, mz, 1] = up_w[...]
        dn[mx, mz] = down_w[...]

    pl.semaphore_wait(barrier, 2 * S - 1 + 2 * (E - 2))

    def remote(src, dst, ss, rs, seq, exp):
        return pltpu.make_async_remote_copy(
            src_ref=src,
            dst_ref=dst,
            send_sem=ss,
            recv_sem=rs,
            device_id={"seq": seq, "exp": exp},
            device_id_type=MESH,
        )

    def kv_copy(h, p):
        return remote(
            kv_send.at[p, h], kv.at[p, me], kv_ss.at[p, h], kv_rs.at[me], 2 * h + core, 2 * yy + p
        )

    def head_copy(send, recv, ss, rs, h, p):
        return remote(
            send.at[p, h], recv.at[me], ss.at[p, h], rs.at[me], 2 * h + core, 2 * yy + p
        )

    def each_head(do):
        def step(k, t):
            i = lax.rem(k + 2 * head, 2 * HEADS)
            h, p = i // 2, lax.rem(i, 2)

            @pl.when((2 * h + core != me) | (p != core))
            def _():
                do(h, p)

            return t

        lax.fori_loop(0, 2 * HEADS, step, 0)

    def each_source(do, first=0, n=S):
        def step(k, t):
            d = first + lax.rem(me + k, n)

            @pl.when((d != me) | (par != core))
            def _():
                do(d)

            return t

        lax.fori_loop(0, n, step, 0)

    def source_copy(send, recv, ss, rs, d):
        return remote(
            send.at[d], recv.at[core, head], ss.at[d], rs.at[core, head], d, 2 * yy + par
        )

    def wait_kv(d):
        view = kv.at[core, d]
        remote(view, view, kv_ss.at[0, 0], kv_rs.at[d], d, 2 * yy + par).wait_recv()

    def wait_source(recv, ss, rs, d):
        view = recv.at[d]
        remote(view, view, ss.at[0, 0], rs.at[d], d, 2 * yy + par).wait_recv()

    def wait_head(recv, ss, rs, h, p):
        view = recv.at[p, h]
        remote(view, view, ss.at[0], rs.at[p, h], 2 * h + core, 2 * yy + p).wait_recv()

    def expert_at(e):
        cross = (lax.rem(e, 2) - grp) * (lax.rem(e, 2) - grp)
        seq = (mx + cross * (X - 1 - 2 * mx)) * Z + mz
        return seq, 2 * (e // 2) + cross

    def to_expert(n, e):
        seq, exp = expert_at(e)
        return remote(
            x_send.at[n, e], x_recv.at[n, ex], x_ss.at[n, e], x_rs.at[n, ex], seq, exp
        )

    def to_list(n, b):
        return remote(
            x_send.at[n, b],
            x_recv.at[n, expert],
            x_ss.at[n, b],
            x_rs.at[n, expert],
            origin * Z + mz,
            b,
        )

    def wait_x(n, i, seq, exp):
        view = x_recv.at[n, i]
        remote(view, view, x_ss.at[n, i], x_rs.at[n, i], seq, exp).wait_recv()

    def each_expert(do):
        def step(k, t):
            e = lax.rem(ex + k, E)

            @pl.when((e != expert) | (core != 0))
            def _():
                do(e)

            return t

        lax.fori_loop(0, E, step, 0)

    def each_list(do):
        def step(k, t):
            b = lax.rem(ex + k, E)

            @pl.when((b != ex) | (core != 0))
            def _():
                do(b)

            return t

        lax.fori_loop(0, E, step, 0)

    def out_start(n):
        @pl.when(core == 0)
        def _():
            x_recv[n, ex] = x_send[n, expert]

        each_expert(lambda e: to_expert(n, e).start())

    def back_start(n):
        @pl.when(core == 0)
        def _():
            x_recv[n, expert] = x_send[n, ex]

        each_list(lambda b: to_list(n, b).start())

    def out_recv(n):
        each_list(lambda b: wait_x(n, b, origin * Z + mz, b))

    def back_recv(n):
        each_expert(lambda e: wait_x(n, e, *expert_at(e)))

    sent = []

    def at_z(o):
        return lax.rem(mz + o + Z, Z)

    def piece(ref, sems, w, oz, half, seq, exp, ss):
        ax, az = (origin_p if w else origin), at_z(oz)
        view = ref.at[ax, az] if half is None else ref.at[ax, az, half]
        return remote(view, view, ss, sems.at[ax, az, half or 0], seq, exp)

    def send(*args):
        copy = piece(*args)
        copy.start()
        sent.append(copy)

    def wait(ref, sems, w, oz, halves):
        for half in (0, 1) if halves else (None,):
            piece(ref, sems, w, oz, half, me, 2 * yy + sib, init_ss.at[0]).wait_recv()

    kinds = ((gu, gu_rs), (dn, dn_rs))
    both = (1, -1)

    def hop(i, w, sgn, k):
        if k < Z // 2:
            half = None if k < Z // 2 - 1 else (0 if sgn > 0 else 1)
            ss = ring_ss.at[i, w, 0 if sgn > 0 else 1, k]
            send(*kinds[i], w, -sgn * k, half, mx * Z + at_z(sgn), ex, ss)

    def to_pair(i, oz):
        send(*kinds[i], 0, oz, None, partner * Z + mz, ex, pair_ss.at[i, oz % Z])

    def to_core(i, w, oz):
        send(*kinds[i], w, oz, None, me, 2 * yy + sib, core_ss.at[i, w, oz % Z])

    def along_z(i, w, k):
        if k == Z // 2:
            wait(*kinds[i], w, k, True)
            if i == 0:
                to_pair(i, k)
            to_core(i, w, k)
            return
        for s in both:
            wait(*kinds[i], w, -s * k, False)
            hop(i, w, s, k)
            if i == 0:
                to_pair(i, -s * k)
            to_core(i, w, -s * k)

    def from_pair(i, oz):
        wait(*kinds[i], 1, oz, False)
        to_core(i, 1, oz)

    def init_copies(seq, exp):
        return (
            remote(gate_w, gu.at[mx, mz, 0], init_ss.at[0], gu_rs.at[mx, mz, 0], seq, exp),
            remote(up_w, gu.at[mx, mz, 1], init_ss.at[1], gu_rs.at[mx, mz, 1], seq, exp),
            remote(down_w, dn.at[mx, mz], init_ss.at[2], dn_rs.at[mx, mz, 0], seq, exp),
        )

    @pl.when(core != grp)
    def _():
        for copy in init_copies(mirror * Z + mz, 2 * yy + 1):
            copy.start()

    @pl.when((core == 1) & (grp == 1))
    def _():
        for copy in init_copies(me, 2 * yy):
            copy.start()

    each_head(lambda h, p: kv_copy(h, p).start())
    each_head(lambda h, p: head_copy(q_send, q_recv, q_ss, q_rs, h, p).start())

    @pl.when((core == 1) | (grp == 1))
    def _():
        wait(gu, gu_rs, 0, 0, True)
        wait(dn, dn_rs, 0, 0, False)

    for s in both:
        hop(0, 0, s, 0)
    to_pair(1, 0)
    to_pair(0, 0)
    for i in (0, 1):
        to_core(i, 0, 0)

    slot_row = lax.broadcasted_iota(jnp.int32, (NS, KEEP), 0)
    slot_exp = slot_row // SLOT
    slot_pos = slot_row - slot_exp * SLOT
    entry = lax.broadcasted_iota(jnp.int32, (NS, KEEP), 1)
    live = entry < count
    assigned = jnp.zeros((NS, KEEP), F32)
    weight = jnp.zeros((NS, KEEP), F32)
    for k in range(expert_ids.shape[0]):
        match = (expert_ids[k : k + 1, :] == slot_exp) & live
        assigned = assigned + jnp.where(match, 1.0, 0.0)
        weight = weight + jnp.where(match, gate_values[k : k + 1, :], 0.0)
    ei = lax.broadcasted_iota(jnp.int32, (KEEP, KEEP), 0)
    ej = lax.broadcasted_iota(jnp.int32, (KEEP, KEEP), 1)
    earlier = jnp.where(ei < ej, 1.0, 0.0).astype(BF16)
    rank = nn(assigned.astype(BF16), earlier)
    table = jnp.where((assigned > 0.5) & (rank == slot_pos.astype(F32)), 1.0, 0.0)
    table_half = table.astype(BF16)
    weighted = table * weight
    slot_gate = jnp.sum(weighted, axis=1, keepdims=True)

    def turned(a):
        if a.shape[1] < 128:
            a = jnp.concatenate([a, jnp.zeros((a.shape[0], 128 - a.shape[1]), F32)], 1)
        return a.T

    table_t = turned(table)[:KEEP].astype(BF16)
    weighted_t = turned(weighted)[:KEEP]
    w_high = weighted_t.astype(BF16)
    w_low = (weighted_t - w_high.astype(F32)).astype(BF16)

    index_row = kept_index[...]
    index_col = jnp.sum(jnp.where(ei == ej, index_row, 0), axis=1, keepdims=True)
    pick = jnp.where(
        lax.broadcasted_iota(jnp.int32, (KEEP, TOK), 1) == index_col, 1.0, 0.0
    ).astype(BF16)
    grad_f = nn(pick, cotangent[...])
    kept_f = nn(pick, residual[...])
    grad_sel = nn(table_half, grad_f.astype(BF16))
    x_send[0] = (slot_gate * grad_sel).astype(BF16).reshape(E, SLOT, D)
    grad_sel = grad_sel.astype(BF16)
    out_start(0)

    along_z(0, 0, 1)
    from_pair(1, 0)
    for w in (0, 1):
        for s in both:
            hop(1, w, s, 0)
    along_z(0, 0, 2)

    def swap_copy(b):
        view = kv.at[core, pl.ds(b * QSRC, QSRC)]
        return remote(view, view, swap_ss.at[0, b], swap_rs.at[0, b], me, 2 * yy + sib)

    def swap_wait(b):
        view = kv.at[sib, pl.ds(b * QSRC, QSRC)]
        remote(view, view, swap_ss.at[0, b], swap_rs.at[0, b], me, 2 * yy + sib).wait_recv()

    for b in range(NB):
        each_source(wait_kv, b * QSRC, QSRC)
        swap_copy(b).start()
    each_source(lambda d: wait_source(q_recv, q_ss, q_rs, d))
    for b in range(NB):
        swap_wait(b)

    def key_block(c):
        return kv[0, c * QSRC : (c + 1) * QSRC].reshape(KB, HS)

    def value_block(c):
        return kv[1, c * QSRC : (c + 1) * QSRC].reshape(KB, HS)

    def query_block(b):
        return q_recv[b * QSRC : (b + 1) * QSRC].reshape(QB, HS)

    for b in range(NB):
        k_f = key_block(b).astype(F32)
        bias[b * KB : (b + 1) * KB] = jnp.where(k_f > MARK / 2, NEG, 0.0)
        k_t[:, b * KB : (b + 1) * KB] = k_f.T.astype(BF16)
        v_t[:, b * KB : (b + 1) * KB] = value_block(b).astype(F32).T.astype(BF16)

    qcol = lax.broadcasted_iota(jnp.int32, (KB, QB), 1)
    qent = (qcol // PR) * KEEP + core * PR + lax.rem(qcol, PR)
    causal = lax.broadcasted_iota(jnp.int32, (KB, QB), 0) <= qent

    def forward_block(b):
        cols = slice(b * QB, (b + 1) * QB)
        q_blk = query_block(b)
        top = None
        for c in range(b + 1):
            rows = slice(c * KB, (c + 1) * KB)
            half = bias[rows, :]
            sc = nt(key_block(c), q_blk) * scale + jnp.concatenate([half] * (QB // HS), 1)
            if c == b:
                sc = jnp.where(causal, sc, NEG)
            prob[rows, cols] = sc
            m = jnp.max(sc, axis=0, keepdims=True)
            top = m if top is None else jnp.maximum(top, m)
        total = jnp.zeros((1, QB), F32)
        for c in range(b + 1):
            rows = slice(c * KB, (c + 1) * KB)
            e = jnp.exp(prob[rows, cols] - top)
            prob[rows, cols] = e
            total = total + jnp.sum(e, axis=0, keepdims=True)
        inv = 1.0 / total
        out = jnp.zeros((HS, QB), F32)
        for c in range(b + 1):
            rows = slice(c * KB, (c + 1) * KB)
            pr = prob[rows, cols] * inv
            prob[rows, cols] = pr
            out = out + nn(v_t[:, rows], pr.astype(BF16))
        att_t[:, cols] = out
        a_send[b * QSRC : (b + 1) * QSRC] = out.T.astype(BF16).reshape(QSRC, PR, HS)
        each_source(
            lambda d: source_copy(a_send, a_recv, a_ss, a_rs, d).start(), b * QSRC, QSRC
        )

    for b in range(NB):
        forward_block(b)

    @pl.when(par == core)
    def _():
        a_recv[core, head] = a_send[me]

    along_z(0, 0, 3)
    from_pair(0, 0)
    along_z(1, 0, 1)
    along_z(1, 1, 1)
    each_head(lambda h, p: wait_head(a_recv, a_ss, a_rs, h, p))

    attended = jnp.concatenate(
        [jnp.concatenate([a_recv[p, h] for h in range(HEADS)], 1) for p in range(2)], 0
    )
    h1 = jnp.where(live_col, kept_f + attended.astype(F32), 0.0)
    inv_rms = lax.rsqrt(jnp.mean(h1 * h1, axis=1, keepdims=True) + EPSILON)
    normed = (h1 * inv_rms).astype(BF16)
    x_send[1] = nn(table_half, normed).astype(BF16).reshape(E, SLOT, D)
    out_start(1)
    along_z(0, 0, Z // 2)
    for k in range(2, Z // 2 + 1):
        for s in both:
            from_pair(0, s * (k - 1))
        for w in (0, 1):
            along_z(1, w, k)
    from_pair(0, Z // 2)
    out_recv(0)
    out_recv(1)
    for ax in (other_o, other_p):
        for az in range(Z):
            for ref, sems in kinds:
                view = ref.at[ax, az]
                remote(
                    view, view, init_ss.at[0], sems.at[ax, az, 0], me, 2 * yy + sib
                ).wait_recv()

    rows_in = x_recv[1].reshape(NS, D)
    grads_in = x_recv[0].reshape(NS, D)
    KC = Z * KEEP
    gate_pre = jnp.zeros((NS, FF), F32)
    up_pre = jnp.zeros((NS, FF), F32)
    mid_grad = jnp.zeros((NS, FF), F32)
    for c in range(X):
        r = rows_in[:, c * KC : (c + 1) * KC]
        gate_pre = gate_pre + nn(r, gu[c, :, 0].reshape(KC, FF))
        up_pre = up_pre + nn(r, gu[c, :, 1].reshape(KC, FF))
        mid_grad = mid_grad + nn(grads_in[:, c * KC : (c + 1) * KC], dn[c].reshape(KC, FF))
    sig = 1.0 / (1.0 + jnp.exp(-gate_pre))
    act = gate_pre * sig
    gate_grad = (mid_grad * up_pre * sig * (1.0 + gate_pre * (1.0 - sig))).astype(BF16)
    up_grad = (mid_grad * act).astype(BF16)
    mid = (act * up_pre).astype(BF16)
    for c in range(X):
        back = nt(gate_grad, gu[c, :, 0].reshape(KC, FF)) + nt(
            up_grad, gu[c, :, 1].reshape(KC, FF)
        )
        x_send[2, :, :, c * KC : (c + 1) * KC] = back.astype(BF16).reshape(E, SLOT, KC)
    back_start(2)
    for c in range(X):
        made = nt(mid, dn[c].reshape(KC, FF))
        x_send[3, :, :, c * KC : (c + 1) * KC] = made.astype(BF16).reshape(E, SLOT, KC)
    back_start(3)
    back_recv(2)
    normed_grad = nn(table_t, x_recv[2].reshape(NS, D))
    cubed = inv_rms * inv_rms * inv_rms
    h1_grad = (
        grad_f
        + inv_rms * normed_grad
        - h1 * cubed * jnp.mean(normed_grad * h1, axis=1, keepdims=True)
    )
    h1_grad = jnp.where(live_col, h1_grad, 0.0).astype(BF16)
    for h in range(HEADS):
        for p in range(2):
            g_send[p, h] = h1_grad[p * PR : (p + 1) * PR, h * HS : (h + 1) * HS]

    @pl.when(par == core)
    def _():
        g_recv[me] = g_send[core, head]

    each_head(lambda h, p: head_copy(g_send, g_recv, g_ss, g_rs, h, p).start())

    token = lax.broadcasted_iota(jnp.int32, (TOK, KEEP), 0)
    put = jnp.where(
        (token == index_row) & (lax.broadcasted_iota(jnp.int32, (TOK, KEEP), 1) < count),
        1.0,
        0.0,
    )
    replaced = jnp.sum(put, axis=1, keepdims=True) > 0.5
    put = put.astype(BF16)
    input_grad[...] = jnp.where(replaced, nn(put, h1_grad), cotangent[...].astype(F32)).astype(
        BF16
    )
    back_recv(3)
    results = x_recv[3].reshape(NS, D)
    mixture = nn(w_high, results) + nn(w_low, results)
    new_rows = (h1 + mixture).astype(BF16)
    output[...] = jnp.where(replaced, nn(put, new_rows), residual[...].astype(F32)).astype(BF16)
    per_slot = jnp.sum(results.astype(F32) * grad_sel.astype(F32), axis=1, keepdims=True)
    spread = table * per_slot
    for k in range(expert_ids.shape[0]):
        hit = expert_ids[k : k + 1, :] == slot_exp
        gate_grads[k : k + 1, :] = jnp.sum(jnp.where(hit, spread, 0.0), axis=0, keepdims=True)

    each_source(lambda d: wait_source(g_recv, g_ss, g_rs, d))
    acc[...] = jnp.zeros_like(acc)

    def give_copy(b):
        rows = pl.ds(b * KB, KB)
        return remote(
            acc.at[sib, rows],
            other.at[rows],
            swap_ss.at[1, b],
            swap_rs.at[1, b],
            me,
            2 * yy + sib,
        )

    def finish_block(b):
        give_copy(b).wait_recv()
        rows = slice(b * KB, (b + 1) * KB)
        src = slice(b * QSRC, (b + 1) * QSRC)
        whole = acc[core, rows] + other[rows]
        b_send[src, 0:KEEP] = whole.astype(BF16).reshape(QSRC, KEEP, HS)
        each_source(
            lambda d: source_copy(b_send, b_recv, b_ss, b_rs, d).start(), b * QSRC, QSRC
        )

    for b in reversed(range(NB)):
        cols = slice(b * QB, (b + 1) * QB)
        q_blk = query_block(b)
        dout = g_recv[b * QSRC : (b + 1) * QSRC].reshape(QB, HS)
        delta = jnp.sum(dout.astype(F32).T * att_t[:, cols], axis=0, keepdims=True)
        dq_t = jnp.zeros((HS, QB), F32)
        for c in range(b + 1):
            rows = slice(c * KB, (c + 1) * KB)
            pr = prob[rows, cols]
            ds = (pr * (nt(value_block(c), dout) - delta) * scale).astype(BF16)
            dq_t = dq_t + nn(k_t[:, rows], ds)
            acc[0, rows] += nn(ds, q_blk)
            acc[1, rows] += nn(pr.astype(BF16), dout)
        b_send[b * QSRC : (b + 1) * QSRC, KEEP:] = dq_t.T.astype(BF16).reshape(QSRC, PR, HS)
        give_copy(b).start()
        if b < NB - 1:
            finish_block(b + 1)
    finish_block(0)

    @pl.when(par == core)
    def _():
        b_recv[core, head] = b_send[me]

    each_head(lambda h, p: wait_head(b_recv, b_ss, b_rs, h, p))
    for h in range(HEADS):
        c0 = h * HS
        for p in range(2):
            projected_grad[p * PR : (p + 1) * PR, c0 : c0 + HS] = b_recv[p, h, KEEP:]
            o = (1 + p) * D + c0
            projected_grad[:, o : o + HS] = b_recv[p, h, 0:KEEP]

    each_head(lambda h, p: kv_copy(h, p).wait_send())
    each_head(lambda h, p: head_copy(q_send, q_recv, q_ss, q_rs, h, p).wait_send())
    each_head(lambda h, p: head_copy(g_send, g_recv, g_ss, g_rs, h, p).wait_send())
    each_source(lambda d: source_copy(a_send, a_recv, a_ss, a_rs, d).wait_send())
    each_source(lambda d: source_copy(b_send, b_recv, b_ss, b_rs, d).wait_send())
    for n in (0, 1):
        each_expert(lambda e, n=n: to_expert(n, e).wait_send())
    for n in (2, 3):
        each_list(lambda b, n=n: to_list(n, b).wait_send())
    for b in range(NB):
        swap_copy(b).wait_send()
        give_copy(b).wait_send()

    @pl.when(core != grp)
    def _():
        for copy in init_copies(mirror * Z + mz, 2 * yy + 1):
            copy.wait_send()

    @pl.when((core == 1) & (grp == 1))
    def _():
        for copy in init_copies(me, 2 * yy):
            copy.wait_send()

    for copy in sent:
        copy.wait_send()


def body(
    residual,
    kept_index,
    kept_count,
    projected,
    expert_ids,
    gate_values,
    gate_weight,
    up_weight,
    down_weight,
    cotangent,
):
    S = lax.axis_size("seq")
    E = lax.axis_size("exp")
    _, TOK, D = residual.shape
    KEEP = kept_index.shape[1]
    FF = gate_weight.shape[2]
    TOPK = expert_ids.shape[2]
    Z = S // X
    HEADS = D // HS
    PR = KEEP // 2
    NB = S // QSRC
    vm = pl.BlockSpec(memory_space=pltpu.VMEM)
    dma = pltpu.SemaphoreType.DMA
    out = pl.pallas_call(
        functools.partial(kernel, S, E),
        out_shape=[
            jax.ShapeDtypeStruct((TOK, D), BF16),
            jax.ShapeDtypeStruct((TOK, D), BF16),
            jax.ShapeDtypeStruct((KEEP, 3 * D), BF16),
            jax.ShapeDtypeStruct((TOPK, KEEP), F32),
        ],
        in_specs=[vm] * 10,
        out_specs=[vm] * 4,
        scratch_shapes=[
            pltpu.VMEM((2, HEADS, KEEP, HS), BF16),
            pltpu.VMEM((2, S, KEEP, HS), BF16),
            pltpu.VMEM((2, HEADS, PR, HS), BF16),
            pltpu.VMEM((S, PR, HS), BF16),
            pltpu.VMEM((S, PR, HS), BF16),
            pltpu.VMEM((2, HEADS, PR, HS), BF16),
            pltpu.VMEM((2, HEADS, PR, HS), BF16),
            pltpu.VMEM((S, PR, HS), BF16),
            pltpu.VMEM((S, KEEP + PR, HS), BF16),
            pltpu.VMEM((2, HEADS, KEEP + PR, HS), BF16),
            pltpu.VMEM((4, E, SLOT, D), BF16),
            pltpu.VMEM((4, E, SLOT, D), BF16),
            pltpu.VMEM((X, Z, 2, KEEP, FF), BF16),
            pltpu.VMEM((X, Z, 2, KEEP // 2, FF), BF16),
            pltpu.VMEM((S * KEEP, HS), F32),
            pltpu.VMEM((HS, S * KEEP), BF16),
            pltpu.VMEM((HS, S * KEEP), BF16),
            pltpu.VMEM((S * KEEP, S * PR), F32),
            pltpu.VMEM((HS, S * PR), F32),
            pltpu.VMEM((2, S * KEEP, HS), F32),
            pltpu.VMEM((S * KEEP, HS), F32),
        ]
        + [dma((2, HEADS))] * 5
        + [dma((S,))] * 5
        + [dma((4, E))] * 2
        + [dma((2, NB))] * 2
        + [
            dma((X, Z, 2)),
            dma((X, Z, 2)),
            dma((2, 2, 2, Z // 2)),
            dma((2, Z)),
            dma((2, 2, Z)),
            dma((3,)),
        ],
        compiler_params=pltpu.CompilerParams(
            collective_id=0, has_side_effects=True, vmem_limit_bytes=60 * 1024 * 1024
        ),
    )(
        residual[0],
        kept_index,
        kept_count,
        projected[0],
        expert_ids[0].T,
        gate_values[0].T,
        gate_weight[0],
        up_weight[0],
        down_weight[0].T.reshape(2, KEEP // 2, FF),
        cotangent[0],
    )
    return (out[0][None], out[1][None], out[2][None], out[3].T[None])


def solution(mesh):
    row = P("exp", "seq", None)
    in_specs = (row, P("exp", "seq"), P("exp", "seq")) + (row,) * 5 + (P("exp", None, "seq"), row)
    return jax.shard_map(
        body, mesh=mesh, in_specs=in_specs, out_specs=(row,) * 4, check_vma=False
    )
```

time: 237 us -> 169 us (0.71)
  Pallas kernels: 227 us -> 159 us
    pallas_call x1, Pallas kernels: 227 us -> 159 us  [body(): pl.pallas_call(functools.partial(kernel, S, E), out_shape=[jax.ShapeDtype...]
where the time goes in v2:
time: 169 us; the launch traced here: 168 us
  Pallas kernels  159 us (94%)
  local copies, waits for them, and re-layouts  7.99 us (5%)
    pallas_call x1, Pallas kernels, body(): pl.pallas_call(functools.partial(kernel, S, E), out_shape=[jax.ShapeDtype...  159 us
    unnamed x16, local copies, waits for them, and re-layouts  7.99 us

profile of v2, /device:TPU:1, one launch (start us, length us, event | category | flops | bytes accessed | tf_op | source)
XLA Modules:
  0.0 168.1 jit_solution(3296381344691253045)
XLA Ops:
  1.3 0.0 copy-start.3
  1.3 0.7 copy-done.3
  2.0 0.0 copy-start.4
  2.0 0.6 copy.20
  2.6 0.1 copy-done.4
  2.7 0.6 copy.19
  3.2 158.8 %shard_map.129 = (bf16[256,2048]{1,0:T(8,128)(2,1)}, bf16[256,2048]{1,0:T(8,128)(2,1)}, bf16[64,6144]{1,0:T(8,128)(2,1)}, f32[6,64]{1,0:T(8,128)}) custom-call(bf16[256,2048]{1,0:T(8,128)(2,1)} %bitcast.26, s32[1,64]{1,0:T(1,128)} %kept_index.1, s32[1,1]{1,0:T(1,128)S(6)} %copy.24.kept_count, bf16[64,6144]{1,0:T(8,128)(2,1)} %bitcast.31, s32[6,64]{1,0:T(8,128)} %bitcast.35, ...), custom_call_target="tpu_custom_call" | custom-call | tf_op jit(solution)/shard_map/pallas_call | solution.py:704
  162.0 0.0 copy-start.2
  162.0 0.7 copy-done.2
  162.7 0.6 copy.14
  163.3 0.0 copy-start
  163.3 2.4 %copy.25 = bf16[1,256,2048]{2,1,0:T(8,128)(2,1)} copy(bf16[1,256,2048]{2,1,0:T(8,128)(2,1)} %bitcast.29) | data formatting | bytes 2097152
  165.7 0.0 copy-done
  165.7 0.0 copy-start.1
  165.7 1.0 copy.26
  166.7 0.5 copy-done.1
  167.2 0.9 copy.27
Async XLA Ops:
  1.3 0.7 copy-start.3
  2.0 0.7 copy-start.4
  162.0 0.7 copy-start.2
  163.3 2.4 %copy-start = (bf16[256,2048]{1,0:T(8,128)(2,1)S(1)}, bf16[256,2048]{1,0:T(8,128)(2,1)}, u32[]{:S(2)}) copy-start(bf16[256,2048]{1,0:T(8,128)(2,1)} %get-tuple-element.9) | copy-start | bytes 3145732
  165.7 1.5 copy-start.1

commit v3 on v2

v3 whole, which is shorter than its diff:
```python
import functools

import jax
import jax.numpy as jnp
from jax import lax
from jax.experimental import pallas as pl
from jax.experimental.pallas import tpu as pltpu
from jax.sharding import PartitionSpec as P

HS = 128
SLOT = 16
EPSILON = 1e-06
X = 4
QSRC = 8
F32 = jnp.float32
BF16 = jnp.bfloat16
MESH = pl.DeviceIdType.MESH
NEG = -1e30
MARK = 1024.0


def nn(a, b):
    return lax.dot_general(a, b, (((1,), (0,)), ((), ())), preferred_element_type=F32)


def nt(a, b):
    return lax.dot_general(a, b, (((1,), (1,)), ((), ())), preferred_element_type=F32)


def kernel(
    S,
    E,
    residual_h,
    kept_index,
    kept_count,
    projected_h,
    expert_ids,
    gate_values,
    gate_w,
    up_w,
    down_w,
    cotangent_h,
    output_h,
    input_grad_h,
    projected_grad_h,
    gate_grads,
    residual,
    cotangent,
    projected,
    output,
    input_grad,
    projected_grad,
    io_sem,
    kv_send,
    kv,
    q_send,
    q_recv,
    a_send,
    a_recv,
    g_send,
    g_recv,
    b_send,
    b_recv,
    dq_send,
    dq_recv,
    x_send,
    x_recv,
    gu,
    dn,
    bias,
    k_t,
    v_t,
    prob,
    att_t,
    acc,
    other,
    send_ss,
    kv_rs,
    q_rs,
    a_rs,
    g_rs,
    b_rs,
    x_rs,
    rows_rs,
    swap_rs,
    gu_rs,
    dn_rs,
    core_rs,
    init_ss,
):
    Z = S // X
    KEEP = kept_index.shape[1]
    TOK, D = residual.shape
    FF = gate_w.shape[1]
    HEADS = D // HS
    PR = KEEP // 2
    NB = S // QSRC
    KB = QSRC * KEEP
    QB = QSRC * PR
    NS = E * SLOT
    scale = HS**-0.5
    me = lax.axis_index("seq")
    ex = lax.axis_index("exp")
    mx = me // Z
    mz = lax.rem(me, Z)
    yy = ex // 2
    core = lax.rem(ex, 2)
    sib = 1 - core
    grp = mx // 2
    mirror = X - 1 - mx
    partner = 4 * grp + 1 - mx
    head = me // 2
    par = lax.rem(me, 2)
    expert = 2 * yy + grp

    def load(i, src, dst):
        return pltpu.make_async_copy(src, dst, io_sem.at[i])

    projected_in = load(0, projected_h, projected)
    cotangent_in = load(1, cotangent_h, cotangent)
    residual_in = load(2, residual_h, residual)
    for copy in (projected_in, cotangent_in, residual_in):
        copy.start()

    def home_copies():
        return (
            load(3, gate_w, gu.at[mx, mz, 0]),
            load(4, up_w, gu.at[mx, mz, 1]),
            load(5, down_w, dn.at[mx, mz]),
        )

    @pl.when((core == 0) & (grp == 0))
    def _():
        for copy in home_copies():
            copy.start()

    barrier = pltpu.get_barrier_semaphore()

    def greet(seq, exp):
        pl.semaphore_signal(
            barrier, inc=1, device_id={"seq": seq, "exp": exp}, device_id_type=MESH
        )

    def greet_plane(k, t):
        i = lax.rem(2 * me + core + k, 2 * S)
        greet(i // 2, 2 * yy + lax.rem(i, 2))
        return t

    def greet_others(k, t):
        e = lax.rem(2 * yy + 2 + k, E)
        greet(me, e)
        greet(mirror * Z + mz, e)
        return t

    lax.fori_loop(1, 2 * S, greet_plane, 0)
    lax.fori_loop(0, E - 2, greet_others, 0)

    projected_in.wait()
    count = kept_count[...]
    live_col = lax.broadcasted_iota(jnp.int32, (KEEP, 1), 0) < count
    for h in range(HEADS):
        c0 = h * HS
        keys = projected[:, D + c0 : D + c0 + HS].astype(F32)
        kv_send[2 * h] = jnp.where(live_col, keys, MARK).astype(BF16)
        kv_send[2 * h + 1] = projected[:, 2 * D + c0 : 2 * D + c0 + HS]
        for p in range(2):
            q_send[2 * h + p] = projected[p * PR : (p + 1) * PR, c0 : c0 + HS]

    origin = mx + core * (X - 1 - 2 * mx)
    origin_p = partner + core * (X - 1 - 2 * partner)
    other_o = mx + sib * (X - 1 - 2 * mx)
    other_p = partner + sib * (X - 1 - 2 * partner)

    @pl.when((core == 0) & (grp == 0))
    def _():
        for copy in home_copies():
            copy.wait()

    slot_row = lax.broadcasted_iota(jnp.int32, (NS, KEEP), 0)
    slot_exp = slot_row // SLOT
    slot_pos = slot_row - slot_exp * SLOT
    entry = lax.broadcasted_iota(jnp.int32, (NS, KEEP), 1)
    live = entry < count
    assigned = jnp.zeros((NS, KEEP), F32)
    weight = jnp.zeros((NS, KEEP), F32)
    for k in range(expert_ids.shape[0]):
        match = (expert_ids[k] == slot_exp) & live
        assigned = assigned + jnp.where(match, 1.0, 0.0)
        weight = weight + jnp.where(match, gate_values[k], 0.0)
    ei = lax.broadcasted_iota(jnp.int32, (KEEP, KEEP), 0)
    ej = lax.broadcasted_iota(jnp.int32, (KEEP, KEEP), 1)
    earlier = jnp.where(ei < ej, 1.0, 0.0).astype(BF16)
    rank = nn(assigned.astype(BF16), earlier)
    table = jnp.where((assigned > 0.5) & (rank == slot_pos.astype(F32)), 1.0, 0.0)
    table_half = table.astype(BF16)
    weighted = table * weight
    slot_gate = jnp.sum(weighted, axis=1, keepdims=True)

    def turned(a):
        if a.shape[1] < 128:
            a = jnp.concatenate([a, jnp.zeros((a.shape[0], 128 - a.shape[1]), F32)], 1)
        return a.T

    table_t = turned(table)[:KEEP].astype(BF16)
    weighted_t = turned(weighted)[:KEEP]
    w_high = weighted_t.astype(BF16)
    w_low = (weighted_t - w_high.astype(F32)).astype(BF16)

    cotangent_in.wait()
    residual_in.wait()
    index_row = kept_index[...]
    index_col = jnp.sum(jnp.where(ei == ej, index_row, 0), axis=1, keepdims=True)
    pick = jnp.where(
        lax.broadcasted_iota(jnp.int32, (KEEP, TOK), 1) == index_col, 1.0, 0.0
    ).astype(BF16)
    grad_f = nn(pick, cotangent[...])
    kept_f = nn(pick, residual[...])
    grad_sel = nn(table_half, grad_f.astype(BF16))
    x_send[0] = (slot_gate * grad_sel).astype(BF16).reshape(E, SLOT, D)
    grad_sel = grad_sel.astype(BF16)
    pl.semaphore_wait(barrier, 2 * S - 1 + 2 * (E - 2))

    def remote(src, dst, ss, rs, seq, exp):
        return pltpu.make_async_remote_copy(
            src_ref=src,
            dst_ref=dst,
            send_sem=ss,
            recv_sem=rs,
            device_id={"seq": seq, "exp": exp},
            device_id_type=MESH,
        )

    def landed(view, sem):
        remote(view, view, init_ss.at[0], sem, me, 2 * yy + sib).wait_recv()

    def left(n, view):
        remote(view, view, send_ss.at[n], init_ss.at[0], me, 2 * yy + sib).wait_send()

    def left_all(n, ref):
        @pl.when(par == core)
        def _():
            left(n, ref.at[pl.ds(0, S - 1)])

        @pl.when(par != core)
        def _():
            left(n, ref)

    here = 2 * head + core

    def each_head(do):
        def step(k, t):
            i = lax.rem(k + 2 * head, S)

            @pl.when((2 * (i // 2) + core != me) | (lax.rem(i, 2) != core))
            def _():
                do(i)

            return t

        lax.fori_loop(0, S, step, 0)

    def each_source(do, first=0, n=S):
        def step(k, t):
            d = first + lax.rem(me + k, n)

            @pl.when((d != me) | (par != core))
            def _():
                do(d)

            return t

        lax.fori_loop(0, n, step, 0)

    def kv_copy(i):
        p = lax.rem(i, 2)
        return remote(
            kv_send.at[i],
            kv.at[p, me],
            send_ss.at[0],
            kv_rs.at[me // QSRC],
            2 * (i // 2) + core,
            2 * yy + p,
        )

    def head_copy(n, send, recv, rs, i):
        return remote(
            send.at[i],
            recv.at[me],
            send_ss.at[n],
            rs,
            2 * (i // 2) + core,
            2 * yy + lax.rem(i, 2),
        )

    def source_copy(n, send, recv, rs, d):
        return remote(send.at[d], recv.at[here], send_ss.at[n], rs, d, 2 * yy + par)

    def own_copy(src, dst, sem):
        @pl.when(par == core)
        def _():
            pltpu.make_async_copy(src, dst, sem).start()

    def expert_at(e):
        cross = (lax.rem(e, 2) - grp) * (lax.rem(e, 2) - grp)
        seq = (mx + cross * (X - 1 - 2 * mx)) * Z + mz
        return seq, 2 * (e // 2) + cross

    def to_expert(n, e):
        seq, exp = expert_at(e)
        return remote(
            x_send.at[n, e], x_recv.at[n, ex], send_ss.at[6 + n], x_rs.at[n], seq, exp
        )

    def to_list(n, b):
        return remote(
            x_send.at[n, b],
            x_recv.at[n, expert],
            send_ss.at[6 + n],
            x_rs.at[n],
            origin * Z + mz,
            b,
        )

    def each_expert(do):
        def step(k, t):
            e = lax.rem(ex + k, E)

            @pl.when((e != expert) | (core != 0))
            def _():
                do(e)

            return t

        lax.fori_loop(0, E, step, 0)

    def each_list(do):
        def step(k, t):
            b = lax.rem(ex + k, E)

            @pl.when((b != ex) | (core != 0))
            def _():
                do(b)

            return t

        lax.fori_loop(0, E, step, 0)

    def out_start(n):
        @pl.when(core == 0)
        def _():
            pltpu.make_async_copy(x_send.at[n, expert], x_recv.at[n, ex], x_rs.at[n]).start()

        each_expert(lambda e: to_expert(n, e).start())

    def back_start(n):
        @pl.when(core == 0)
        def _():
            pltpu.make_async_copy(x_send.at[n, ex], x_recv.at[n, expert], x_rs.at[n]).start()

        each_list(lambda b: to_list(n, b).start())

    def x_landed(n):
        landed(x_recv.at[n], x_rs.at[n])

    def x_left(n, i, cols):
        @pl.when(core == 0)
        def _():
            left(i, x_send.at[n, pl.ds(0, E - 1), :, cols])

        @pl.when(core != 0)
        def _():
            left(i, x_send.at[n, :, :, cols])

    def part_cols(c):
        return pl.ds(c * Z * KEEP, Z * KEEP)

    def rows_copy(c, b):
        cols = part_cols(c)
        return remote(
            x_send.at[2, b, :, cols],
            x_recv.at[2, expert, :, cols],
            send_ss.at[10 + c],
            rows_rs.at[c],
            origin * Z + mz,
            b,
        )

    def rows_start(c):
        cols = part_cols(c)

        @pl.when(core == 0)
        def _():
            pltpu.make_async_copy(
                x_send.at[2, ex, :, cols], x_recv.at[2, expert, :, cols], rows_rs.at[c]
            ).start()

        each_list(lambda b: rows_copy(c, b).start())

    def at_z(o):
        return lax.rem(mz + o + Z, Z)

    RING, PAIR, CORE = 14, 16, 18

    def piece(i, w, oz, half, group, seq, exp, sem):
        ref = kinds[i][0]
        ax, az = (origin_p if w else origin), at_z(oz)
        view = ref.at[ax, az] if half is None else ref.at[ax, az, half]
        return remote(view, view, send_ss.at[group + i], sem, seq, exp)

    def arrival(i, w, oz, half):
        return kinds[i][1].at[w, oz % Z if half != 1 else Z]

    def wait(i, w, oz, halves):
        for half in (0, 1) if halves else (None,):
            piece(i, w, oz, half, RING, me, 2 * yy + sib, arrival(i, w, oz, half)).wait_recv()

    kinds = ((gu, gu_rs), (dn, dn_rs))
    both = (1, -1)

    def hop(i, w, sgn, k):
        if k < Z // 2:
            half = None if k < Z // 2 - 1 else (0 if sgn > 0 else 1)
            sem = arrival(i, w, -sgn * (k + 1), half)
            piece(i, w, -sgn * k, half, RING, mx * Z + at_z(sgn), ex, sem).start()

    def to_pair(i, oz):
        piece(i, 0, oz, None, PAIR, partner * Z + mz, ex, arrival(i, 1, oz, None)).start()

    def to_core(i, w, oz):
        piece(i, w, oz, None, CORE, me, 2 * yy + sib, core_rs.at[i, w]).start()

    def along_z(i, w, k):
        if k == Z // 2:
            wait(i, w, k, True)
            if i == 0:
                to_pair(i, k)
            to_core(i, w, k)
            return
        for s in both:
            wait(i, w, -s * k, False)
            hop(i, w, s, k)
            if i == 0:
                to_pair(i, -s * k)
            to_core(i, w, -s * k)

    def from_pair(i, oz):
        wait(i, 1, oz, False)
        to_core(i, 1, oz)

    def init_copies(seq, exp):
        return (
            remote(gate_w, gu.at[mx, mz, 0], init_ss.at[0], gu_rs.at[0, 0], seq, exp),
            remote(up_w, gu.at[mx, mz, 1], init_ss.at[1], gu_rs.at[0, Z + 1], seq, exp),
            remote(down_w, dn.at[mx, mz], init_ss.at[2], dn_rs.at[0, 0], seq, exp),
        )

    @pl.when(core != grp)
    def _():
        for copy in init_copies(mirror * Z + mz, 2 * yy + 1):
            copy.start()

    @pl.when((core == 1) & (grp == 1))
    def _():
        for copy in init_copies(me, 2 * yy):
            copy.start()

    own_copy(kv_send.at[here], kv.at[core, me], kv_rs.at[me // QSRC])
    own_copy(q_send.at[here], q_recv.at[me], q_rs.at[0])
    each_head(lambda i: kv_copy(i).start())
    each_head(lambda i: head_copy(1, q_send, q_recv, q_rs.at[0], i).start())

    @pl.when((core == 1) | (grp == 1))
    def _():
        landed(gu.at[origin, mz, 0], gu_rs.at[0, 0])
        landed(gu.at[origin, mz, 1], gu_rs.at[0, Z + 1])
        landed(dn.at[origin, mz], dn_rs.at[0, 0])

    for s in both:
        hop(0, 0, s, 0)
    to_pair(1, 0)
    to_pair(0, 0)
    for i in (0, 1):
        to_core(i, 0, 0)

    out_start(0)

    along_z(0, 0, 1)
    along_z(0, 0, 2)

    def swap_copy(b):
        view = kv.at[core, pl.ds(b * QSRC, QSRC)]
        return remote(view, view, send_ss.at[20], swap_rs.at[0, b], me, 2 * yy + sib)

    for b in range(NB):
        landed(kv.at[core, pl.ds(b * QSRC, QSRC)], kv_rs.at[b])
        swap_copy(b).start()
    landed(q_recv, q_rs.at[0])
    for b in range(NB):
        landed(kv.at[sib, pl.ds(b * QSRC, QSRC)], swap_rs.at[0, b])

    def key_block(c):
        return kv[0, c * QSRC : (c + 1) * QSRC].reshape(KB, HS)

    def value_block(c):
        return kv[1, c * QSRC : (c + 1) * QSRC].reshape(KB, HS)

    def query_block(b):
        return q_recv[b * QSRC : (b + 1) * QSRC].reshape(QB, HS)

    for b in range(NB):
        k_f = key_block(b).astype(F32)
        bias[b * KB : (b + 1) * KB] = jnp.where(k_f > MARK / 2, NEG, 0.0)
        k_t[:, b * KB : (b + 1) * KB] = k_f.T.astype(BF16)
        v_t[:, b * KB : (b + 1) * KB] = value_block(b).astype(F32).T.astype(BF16)

    qcol = lax.broadcasted_iota(jnp.int32, (KB, QB), 1)
    qent = (qcol // PR) * KEEP + core * PR + lax.rem(qcol, PR)
    causal = lax.broadcasted_iota(jnp.int32, (KB, QB), 0) <= qent

    def forward_block(b):
        cols = slice(b * QB, (b + 1) * QB)
        q_blk = query_block(b)
        top = None
        for c in range(b + 1):
            rows = slice(c * KB, (c + 1) * KB)
            half = bias[rows, :]
            sc = nt(key_block(c), q_blk) * scale + jnp.concatenate([half] * (QB // HS), 1)
            if c == b:
                sc = jnp.where(causal, sc, NEG)
            prob[rows, cols] = sc
            m = jnp.max(sc, axis=0, keepdims=True)
            top = m if top is None else jnp.maximum(top, m)
        total = jnp.zeros((1, QB), F32)
        for c in range(b + 1):
            rows = slice(c * KB, (c + 1) * KB)
            e = jnp.exp(prob[rows, cols] - top)
            prob[rows, cols] = e
            total = total + jnp.sum(e, axis=0, keepdims=True)
        inv = 1.0 / total
        out = jnp.zeros((HS, QB), F32)
        for c in range(b + 1):
            rows = slice(c * KB, (c + 1) * KB)
            pr = prob[rows, cols] * inv
            prob[rows, cols] = pr
            out = out + nn(v_t[:, rows], pr.astype(BF16))
        att_t[:, cols] = out
        a_send[b * QSRC : (b + 1) * QSRC] = out.T.astype(BF16).reshape(QSRC, PR, HS)
        each_source(
            lambda d: source_copy(2, a_send, a_recv, a_rs.at[0], d).start(), b * QSRC, QSRC
        )

    for b in range(NB):
        forward_block(b)
        if b == 1:
            along_z(0, 0, 3)
            from_pair(1, 0)
            for w in (0, 1):
                for s in both:
                    hop(1, w, s, 0)

    own_copy(a_send.at[me], a_recv.at[here], a_rs.at[0])
    along_z(0, 0, Z // 2)
    for w in (0, 1):
        along_z(1, w, 1)
    from_pair(0, 0)
    for w in (0, 1):
        along_z(1, w, 2)
    landed(a_recv, a_rs.at[0])

    attended = jnp.concatenate(
        [jnp.concatenate([a_recv[2 * h + p] for h in range(HEADS)], 1) for p in range(2)], 0
    )
    h1 = jnp.where(live_col, kept_f + attended.astype(F32), 0.0)
    inv_rms = lax.rsqrt(jnp.mean(h1 * h1, axis=1, keepdims=True) + EPSILON)
    normed = (h1 * inv_rms).astype(BF16)
    x_send[1] = nn(table_half, normed).astype(BF16).reshape(E, SLOT, D)
    out_start(1)
    for o in (1, -1):
        from_pair(0, o)
    for w in (0, 1):
        along_z(1, w, 3)
    for o in (2, -2):
        from_pair(0, o)
    for w in (0, 1):
        along_z(1, w, Z // 2)
    x_landed(0)
    x_landed(1)

    KC = Z * KEEP
    pre = [jnp.zeros((NS, FF), F32)] * 3

    def expert_chunk(ax):
        cols = pl.ds(pl.multiple_of(ax * KC, KC), KC)
        r = x_recv[1, :, :, cols].reshape(NS, KC)
        g = x_recv[0, :, :, cols].reshape(NS, KC)
        pre[0] = pre[0] + nn(r, gu[ax, :, 0].reshape(KC, FF))
        pre[1] = pre[1] + nn(r, gu[ax, :, 1].reshape(KC, FF))
        pre[2] = pre[2] + nn(g, dn[ax].reshape(KC, FF))

    def core_landed(w, ax):
        for i, (ref, _) in enumerate(kinds):
            landed(ref.at[ax], core_rs.at[i, w])

    expert_chunk(origin)
    for o in (3, -3, Z // 2):
        from_pair(0, o)
    core_landed(0, other_o)
    expert_chunk(other_o)
    expert_chunk(origin_p)
    core_landed(1, other_p)
    expert_chunk(other_p)
    gate_pre, up_pre, mid_grad = pre
    sig = 1.0 / (1.0 + jnp.exp(-gate_pre))
    act = gate_pre * sig
    gate_grad = (mid_grad * up_pre * sig * (1.0 + gate_pre * (1.0 - sig))).astype(BF16)
    up_grad = (mid_grad * act).astype(BF16)
    mid = (act * up_pre).astype(BF16)
    for c in range(X):
        back = nt(gate_grad, gu[c, :, 0].reshape(KC, FF)) + nt(
            up_grad, gu[c, :, 1].reshape(KC, FF)
        )
        x_send[2, :, :, c * KC : (c + 1) * KC] = back.astype(BF16).reshape(E, SLOT, KC)
        rows_start(c)
    for c in range(X):
        made = nt(mid, dn[c].reshape(KC, FF))
        x_send[3, :, :, c * KC : (c + 1) * KC] = made.astype(BF16).reshape(E, SLOT, KC)
    parts = []
    for c in range(X):
        landed(x_recv.at[2, :, :, part_cols(c)], rows_rs.at[c])
        parts.append(nn(table_t, x_recv[2, :, :, c * KC : (c + 1) * KC].reshape(NS, KC)))
    normed_grad = jnp.concatenate(parts, 1)
    cubed = inv_rms * inv_rms * inv_rms
    h1_grad = (
        grad_f
        + inv_rms * normed_grad
        - h1 * cubed * jnp.mean(normed_grad * h1, axis=1, keepdims=True)
    )
    h1_grad = jnp.where(live_col, h1_grad, 0.0).astype(BF16)
    for h in range(HEADS):
        for p in range(2):
            g_send[2 * h + p] = h1_grad[p * PR : (p + 1) * PR, h * HS : (h + 1) * HS]
    own_copy(g_send.at[here], g_recv.at[me], g_rs.at[me // QSRC])
    each_head(lambda i: head_copy(3, g_send, g_recv, g_rs.at[me // QSRC], i).start())

    token = lax.broadcasted_iota(jnp.int32, (TOK, KEEP), 0)
    put = jnp.where(
        (token == index_row) & (lax.broadcasted_iota(jnp.int32, (TOK, KEEP), 1) < count),
        1.0,
        0.0,
    )
    replaced = jnp.sum(put, axis=1, keepdims=True) > 0.5
    put = put.astype(BF16)
    input_grad[...] = jnp.where(replaced, nn(put, h1_grad), cotangent[...].astype(F32)).astype(
        BF16
    )
    input_grad_out = load(0, input_grad, input_grad_h)
    input_grad_out.start()
    back_start(3)

    def give_copy(c):
        rows = pl.ds(c * KB, KB)
        return remote(
            acc.at[sib, rows],
            other.at[rows],
            send_ss.at[21],
            swap_rs.at[1, c],
            me,
            2 * yy + sib,
        )

    def finish_block(c):
        rows = slice(c * KB, (c + 1) * KB)
        landed(other.at[pl.ds(c * KB, KB)], swap_rs.at[1, c])
        whole = acc[core, rows] + other[rows]
        b_send[c * QSRC : (c + 1) * QSRC] = whole.astype(BF16).reshape(QSRC, KEEP, HS)
        each_source(
            lambda d: source_copy(4, b_send, b_recv, b_rs.at[0], d).start(), c * QSRC, QSRC
        )

    dout = [None] * NB
    delta = [None] * NB
    dq_t = [jnp.zeros((HS, QB), F32)] * NB
    for c in reversed(range(NB)):
        rows = slice(c * KB, (c + 1) * KB)
        block = pl.ds(c * QSRC, QSRC)
        landed(g_recv.at[block], g_rs.at[c])
        dout[c] = g_recv[c * QSRC : (c + 1) * QSRC].reshape(QB, HS)
        turn = dout[c].astype(F32).T * att_t[:, c * QB : (c + 1) * QB]
        delta[c] = jnp.sum(turn, axis=0, keepdims=True)
        dk = jnp.zeros((KB, HS), F32)
        dv = jnp.zeros((KB, HS), F32)
        for b in range(c, NB):
            pr = prob[rows, b * QB : (b + 1) * QB]
            ds = (pr * (nt(value_block(c), dout[b]) - delta[b]) * scale).astype(BF16)
            dq_t[b] = dq_t[b] + nn(k_t[:, rows], ds)
            dk = dk + nn(ds, query_block(b))
            dv = dv + nn(pr.astype(BF16), dout[b])
        acc[0, rows] = dk
        acc[1, rows] = dv
        give_copy(c).start()
        if c < NB - 1:
            finish_block(c + 1)
    for b in range(NB):
        dq_send[b * QSRC : (b + 1) * QSRC] = dq_t[b].T.astype(BF16).reshape(QSRC, PR, HS)
    each_source(lambda d: source_copy(5, dq_send, dq_recv, b_rs.at[1], d).start())
    finish_block(0)
    own_copy(dq_send.at[me], dq_recv.at[here], b_rs.at[1])
    own_copy(b_send.at[me], b_recv.at[here], b_rs.at[0])

    x_landed(3)
    results = x_recv[3].reshape(NS, D)
    mixture = nn(w_high, results) + nn(w_low, results)
    new_rows = (h1 + mixture).astype(BF16)
    output[...] = jnp.where(replaced, nn(put, new_rows), residual[...].astype(F32)).astype(BF16)
    per_slot = jnp.sum(results.astype(F32) * grad_sel.astype(F32), axis=1, keepdims=True)
    spread = table * per_slot
    for k in range(expert_ids.shape[0]):
        hit = expert_ids[k] == slot_exp
        gate_grads[k] = jnp.sum(jnp.where(hit, spread, 0.0), axis=0, keepdims=True)
    output_out = load(1, output, output_h)
    output_out.start()
    left_all(0, kv_send)
    left_all(1, q_send)
    left_all(2, a_send)
    left_all(3, g_send)
    for n in (0, 1, 3):
        x_left(n, 6 + n, pl.ds(0, D))
    for c in range(X):
        x_left(2, 10 + c, part_cols(c))
    for i, (ref, _) in enumerate(kinds):
        if i == 0:
            left(RING + i, ref.at[0, pl.ds(0, Z - 1)])
            left(PAIR + i, ref.at[0])
        else:
            left(RING + i, ref.at[pl.ds(0, 2), pl.ds(0, Z - 1)])
            left(PAIR + i, ref.at[0, 0])
        left(CORE + i, ref.at[pl.ds(0, 2)])
    left(20, kv.at[core])
    left(21, acc.at[sib])

    @pl.when(core != grp)
    def _():
        for copy in init_copies(mirror * Z + mz, 2 * yy + 1):
            copy.wait_send()

    @pl.when((core == 1) & (grp == 1))
    def _():
        for copy in init_copies(me, 2 * yy):
            copy.wait_send()

    landed(b_recv, b_rs.at[0])
    landed(dq_recv, b_rs.at[1])
    for h in range(HEADS):
        c0 = h * HS
        for p in range(2):
            projected_grad[p * PR : (p + 1) * PR, c0 : c0 + HS] = dq_recv[2 * h + p]
            o = (1 + p) * D + c0
            projected_grad[:, o : o + HS] = b_recv[2 * h + p]
    projected_grad_out = load(2, projected_grad, projected_grad_h)
    projected_grad_out.start()
    left_all(4, b_send)
    left_all(5, dq_send)
    for copy in (input_grad_out, output_out, projected_grad_out):
        copy.wait()


def body(
    residual,
    kept_index,
    kept_count,
    projected,
    expert_ids,
    gate_values,
    gate_weight,
    up_weight,
    down_weight,
    cotangent,
):
    S = lax.axis_size("seq")
    E = lax.axis_size("exp")
    _, TOK, D = residual.shape
    KEEP = kept_index.shape[1]
    FF = gate_weight.shape[2]
    TOPK = expert_ids.shape[2]
    Z = S // X
    HEADS = D // HS
    PR = KEEP // 2
    NB = S // QSRC
    vm = pl.BlockSpec(memory_space=pltpu.VMEM)
    hbm = pl.BlockSpec(memory_space=pl.ANY)
    dma = pltpu.SemaphoreType.DMA
    out = pl.pallas_call(
        functools.partial(kernel, S, E),
        out_shape=[
            jax.ShapeDtypeStruct((TOK, D), BF16),
            jax.ShapeDtypeStruct((TOK, D), BF16),
            jax.ShapeDtypeStruct((KEEP, 3 * D), BF16),
            jax.ShapeDtypeStruct((TOPK, 1, KEEP), F32),
        ],
        in_specs=[hbm, vm, vm, hbm, vm, vm, hbm, hbm, hbm, hbm],
        out_specs=[hbm, hbm, hbm, vm],
        scratch_shapes=[
            pltpu.VMEM((TOK, D), BF16),
            pltpu.VMEM((TOK, D), BF16),
            pltpu.VMEM((KEEP, 3 * D), BF16),
            pltpu.VMEM((TOK, D), BF16),
            pltpu.VMEM((TOK, D), BF16),
            pltpu.VMEM((KEEP, 3 * D), BF16),
            dma((6,)),
            pltpu.VMEM((S, KEEP, HS), BF16),
            pltpu.VMEM((2, S, KEEP, HS), BF16),
            pltpu.VMEM((S, PR, HS), BF16),
            pltpu.VMEM((S, PR, HS), BF16),
            pltpu.VMEM((S, PR, HS), BF16),
            pltpu.VMEM((S, PR, HS), BF16),
            pltpu.VMEM((S, PR, HS), BF16),
            pltpu.VMEM((S, PR, HS), BF16),
            pltpu.VMEM((S, KEEP, HS), BF16),
            pltpu.VMEM((S, KEEP, HS), BF16),
            pltpu.VMEM((S, PR, HS), BF16),
            pltpu.VMEM((S, PR, HS), BF16),
            pltpu.VMEM((4, E, SLOT, D), BF16),
            pltpu.VMEM((4, E, SLOT, D), BF16),
            pltpu.VMEM((X, Z, 2, KEEP, FF), BF16),
            pltpu.VMEM((X, Z, 2, KEEP // 2, FF), BF16),
            pltpu.VMEM((S * KEEP, HS), F32),
            pltpu.VMEM((HS, S * KEEP), BF16),
            pltpu.VMEM((HS, S * KEEP), BF16),
            pltpu.VMEM((S * KEEP, S * PR), F32),
            pltpu.VMEM((HS, S * PR), F32),
            pltpu.VMEM((2, S * KEEP, HS), F32),
            pltpu.VMEM((S * KEEP, HS), F32),
        ]
        + [
            dma((22,)),
            dma((NB,)),
            dma((1,)),
            dma((1,)),
            dma((NB,)),
            dma((2,)),
            dma((4,)),
            dma((X,)),
            dma((2, NB)),
            dma((2, Z + 2)),
            dma((2, Z + 2)),
            dma((2, 2)),
            dma((3,)),
        ],
        compiler_params=pltpu.CompilerParams(
            collective_id=0, has_side_effects=True, vmem_limit_bytes=60 * 1024 * 1024
        ),
    )(
        residual[0],
        kept_index,
        kept_count,
        projected[0],
        jnp.transpose(expert_ids, (2, 0, 1)),
        jnp.transpose(gate_values, (2, 0, 1)),
        gate_weight[0],
        up_weight[0],
        down_weight[0].T.reshape(2, KEEP // 2, FF),
        cotangent[0],
    )
    return (out[0][None], out[1][None], out[2][None], jnp.transpose(out[3], (1, 2, 0)))


def solution(mesh):
    row = P("exp", "seq", None)
    in_specs = (row, P("exp", "seq"), P("exp", "seq")) + (row,) * 5 + (P("exp", None, "seq"), row)
    return jax.shard_map(
        body, mesh=mesh, in_specs=in_specs, out_specs=(row,) * 4, check_vma=False
    )
```

time: 169 us -> 154 us (0.911)
  Pallas kernels: 159 us -> 146 us
  local copies, waits for them, and re-layouts: 7.99 us -> 5.37 us
    pallas_call x1, Pallas kernels: 159 us -> 146 us  [body(): pl.pallas_call(functools.partial(kernel, S, E), out_shape=[jax.ShapeDtype...]
    unnamed x16 -> x10, local copies, waits for them, and re-layouts: 7.99 us -> 5.37 us
where the time goes in v3:
time: 154 us; the launch traced here: 153 us
  Pallas kernels  146 us (95%)
  local copies, waits for them, and re-layouts  5.37 us (3%)
    pallas_call x1, Pallas kernels, body(): pl.pallas_call(functools.partial(kernel, S, E), out_shape=[jax.ShapeDtype...  146 us
    unnamed x10, local copies, waits for them, and re-layouts  5.37 us

profile of v3, /device:TPU:1, one launch (start us, length us, event | category | flops | bytes accessed | tf_op | source)
XLA Modules:
  0.0 153.0 jit_solution(9433945142274570410)
XLA Ops:
  1.3 146.4 %shard_map.129 = (bf16[256,2048]{1,0:T(8,128)(2,1)}, bf16[256,2048]{1,0:T(8,128)(2,1)}, bf16[64,6144]{1,0:T(8,128)(2,1)}, f32[6,1,64]{2,1,0:T(1,128)}) custom-call(bf16[256,2048]{1,0:T(8,128)(2,1)} %bitcast.18, s32[1,64]{1,0:T(1,128)} %kept_index.1, s32[1,1]{1,0:T(1,128)S(6)} %copy.18.kept_count, bf16[64,6144]{1,0:T(8,128)(2,1)} %bitcast.21, ...), custom_call_target="tpu_custom_call" | custom-call | tf_op jit(solution)/shard_map/pallas_call | solution.py:792
  147.7 0.0 copy-start
  147.7 2.4 %copy.19 = bf16[1,256,2048]{2,1,0:T(8,128)(2,1)} copy(bf16[1,256,2048]{2,1,0:T(8,128)(2,1)} %bitcast.17) | data formatting | bytes 2097152
  150.1 0.0 copy-done
  150.1 0.0 copy-start.1
  150.1 1.0 copy.20
  151.0 0.5 copy-done.1
  151.6 0.0 copy-start.2
  151.6 0.9 copy.21
  152.5 0.0 copy-done.2
  152.5 0.6 copy.22
Async XLA Ops:
  147.7 2.4 %copy-start = (bf16[256,2048]{1,0:T(8,128)(2,1)S(1)}, bf16[256,2048]{1,0:T(8,128)(2,1)}, u32[]{:S(2)}) copy-start(bf16[256,2048]{1,0:T(8,128)(2,1)} %get-tuple-element.9) | copy-start | bytes 3145732
  150.1 1.5 copy-start.1
  151.6 0.9 copy-start.2

commit v4 on v3

v4 whole, which is shorter than its diff:
```python
import functools

import jax
import jax.numpy as jnp
from jax import lax
from jax.experimental import pallas as pl
from jax.experimental.pallas import tpu as pltpu
from jax.sharding import PartitionSpec as P

HS = 128
SLOT = 16
CAP = 12
FOLDS = 3
EPSILON = 1e-06
PIECES = 2
X = 4
QSRC = 8
F32 = jnp.float32
BF16 = jnp.bfloat16
MESH = pl.DeviceIdType.MESH
NEG = -1e30
WIDE = 768
MARK = 1024.0


def nn(a, b):
    return lax.dot_general(a, b, (((1,), (0,)), ((), ())), preferred_element_type=F32)


def nt(a, b):
    return lax.dot_general(a, b, (((1,), (1,)), ((), ())), preferred_element_type=F32)


def kernel(
    S,
    E,
    residual_h,
    kept_index_h,
    kept_count_h,
    projected_h,
    expert_ids_h,
    gate_values_h,
    gate_w,
    up_w,
    down_w,
    cotangent_h,
    output_h,
    input_grad_h,
    projected_grad_h,
    gate_grads,
    residual,
    cotangent,
    projected,
    kept_index,
    kept_count,
    expert_ids,
    gate_values,
    io_sem,
    kv_send,
    kv,
    q_send,
    q_recv,
    a_send,
    a_recv,
    g_send,
    g_recv,
    b_send,
    b_recv,
    dq_send,
    dq_recv,
    x_send,
    x_recv,
    y_send,
    y_recv,
    x_rows,
    wt,
    bias,
    k_t,
    v_t,
    prob,
    att_t,
    acc,
    other,
    send_ss,
    kv_rs,
    q_rs,
    a_rs,
    g_rs,
    b_rs,
    x_rs,
    y_rs,
    rows_rs,
    swap_rs,
    wt_rs,
    core_rs,
):
    Z = S // X
    KEEP = kept_index.shape[1]
    TOK, D = residual.shape
    FF = gate_w.shape[2]
    HEADS = D // HS
    PR = KEEP // 2
    NB = S // QSRC
    KB = QSRC * KEEP
    QB = QSRC * PR
    NS = E * SLOT
    scale = HS**-0.5
    me = lax.axis_index("seq")
    ex = lax.axis_index("exp")
    mx = me // Z
    mz = lax.rem(me, Z)
    yy = ex // 2
    core = lax.rem(ex, 2)
    sib = 1 - core
    grp = mx // 2
    half = lax.rem(mx, 2)
    head = me // 2
    par = lax.rem(me, 2)
    expert = 2 * yy + grp

    def load(i, src, dst):
        return pltpu.make_async_copy(src, dst, io_sem.at[i])

    projected_in = load(0, projected_h, projected)
    cotangent_in = load(1, cotangent_h, cotangent)
    residual_in = load(2, residual_h, residual)
    small_in = (
        load(6, kept_count_h, kept_count),
        load(7, kept_index_h, kept_index),
        load(8, expert_ids_h, expert_ids),
        load(9, gate_values_h, gate_values),
    )
    for copy in (projected_in, *small_in, cotangent_in, residual_in):
        copy.start()

    def greet(seq, exp):
        pl.semaphore_signal(
            barrier, inc=1, device_id={"seq": seq, "exp": exp}, device_id_type=MESH
        )

    barrier = pltpu.get_barrier_semaphore()

    def greet_plane(k, t):
        i = lax.rem(2 * me + core + k, 2 * S)
        greet(i // 2, 2 * yy + lax.rem(i, 2))
        return t

    def greet_others(k, t):
        e = lax.rem(2 * yy + 2 + k, E)
        for x in range(X):
            greet(x * Z + mz, e)
        return t

    lax.fori_loop(1, 2 * S, greet_plane, 0)
    lax.fori_loop(0, E - 2, greet_others, 0)

    projected_in.wait()
    for copy in small_in:
        copy.wait()
    count = kept_count[...]
    live_col = lax.broadcasted_iota(jnp.int32, (KEEP, 1), 0) < count
    for h in range(HEADS):
        c0 = h * HS
        keys = projected[:, D + c0 : D + c0 + HS].astype(F32)
        kv_send[2 * h] = jnp.where(live_col, keys, MARK).astype(BF16)
        kv_send[2 * h + 1] = projected[:, 2 * D + c0 : 2 * D + c0 + HS]
        for p in range(2):
            q_send[2 * h + p] = projected[p * PR : (p + 1) * PR, c0 : c0 + HS]

    slot_row = lax.broadcasted_iota(jnp.int32, (NS, KEEP), 0)
    slot_exp = slot_row // SLOT
    slot_pos = slot_row - slot_exp * SLOT
    entry = lax.broadcasted_iota(jnp.int32, (NS, KEEP), 1)
    live = entry < count
    assigned = jnp.zeros((NS, KEEP), F32)
    weight = jnp.zeros((NS, KEEP), F32)
    for k in range(expert_ids.shape[0]):
        match = (expert_ids[k] == slot_exp) & live
        assigned = assigned + jnp.where(match, 1.0, 0.0)
        weight = weight + jnp.where(match, gate_values[k], 0.0)
    ei = lax.broadcasted_iota(jnp.int32, (KEEP, KEEP), 0)
    ej = lax.broadcasted_iota(jnp.int32, (KEEP, KEEP), 1)
    earlier = jnp.where(ei < ej, 1.0, 0.0).astype(BF16)
    rank = nn(assigned.astype(BF16), earlier)
    table = jnp.where((assigned > 0.5) & (rank == slot_pos.astype(F32)), 1.0, 0.0)
    table_half = table.astype(BF16)
    weighted = table * weight
    slot_gate = jnp.sum(weighted, axis=1, keepdims=True)

    def turned(a):
        if a.shape[1] < 128:
            a = jnp.concatenate([a, jnp.zeros((a.shape[0], 128 - a.shape[1]), F32)], 1)
        return a.T

    table_t = turned(table)[:KEEP].astype(BF16)
    weighted_t = turned(weighted)[:KEEP]
    w_high = weighted_t.astype(BF16)
    w_low = (weighted_t - w_high.astype(F32)).astype(BF16)

    KC = Z * KEEP
    NR = 2 * NS
    fr = lax.broadcasted_iota(jnp.int32, (NR, NR), 0)
    fc = lax.broadcasted_iota(jnp.int32, (NR, NR), 1)
    spot = lax.rem(fr, SLOT)
    fold, unfold = [], []
    for g in range(FOLDS):
        gap = CAP - 4 * g
        fold.append(jnp.where((spot >= CAP) & (fc == fr - gap), 1.0, 0.0).astype(BF16))
        unfold.append(jnp.where((spot // 4 == g) & (fc == fr + gap), 1.0, 0.0).astype(BF16))

    def quarter(g):
        return slice(g * KC, (g + 1) * KC)

    def pack(ref, g, chunk, last):
        n = chunk.shape[0]
        full = chunk + nn(fold[g][:n, :n], last)
        ref[:, :, quarter(g)] = full.astype(BF16).reshape(n // SLOT, SLOT, KC)

    def pack_all(ref, rows):
        for g in range(FOLDS):
            pack(ref, g, rows[:, quarter(g)], rows[:, quarter(FOLDS)].astype(BF16))

    cotangent_in.wait()
    residual_in.wait()
    index_row = kept_index[...]
    index_col = jnp.sum(jnp.where(ei == ej, index_row, 0), axis=1, keepdims=True)
    pick = jnp.where(
        lax.broadcasted_iota(jnp.int32, (KEEP, TOK), 1) == index_col, 1.0, 0.0
    ).astype(BF16)
    grad_f = nn(pick, cotangent[...])
    kept_f = nn(pick, residual[...])
    grad_sel = nn(table_half, grad_f.astype(BF16))
    pack_all(x_send.at[0], (slot_gate * grad_sel).astype(BF16).astype(F32))
    grad_sel = grad_sel.astype(BF16)
    pl.semaphore_wait(barrier, 2 * S - 1 + X * (E - 2))

    def remote(src, dst, ss, rs, seq, exp):
        return pltpu.make_async_remote_copy(
            src_ref=src,
            dst_ref=dst,
            send_sem=ss,
            recv_sem=rs,
            device_id={"seq": seq, "exp": exp},
            device_id_type=MESH,
        )

    def landed(view, sem):
        remote(view, view, send_ss.at[0], sem, me, 2 * yy + sib).wait_recv()

    def left(n, view):
        remote(view, view, send_ss.at[n], q_rs.at[0], me, 2 * yy + sib).wait_send()

    def left_all(n, ref):
        @pl.when(par == core)
        def _():
            left(n, ref.at[pl.ds(0, S - 1)])

        @pl.when(par != core)
        def _():
            left(n, ref)

    here = 2 * head + core

    def each_head(do):
        def step(k, t):
            i = lax.rem(k + 2 * head, S)

            @pl.when((2 * (i // 2) + core != me) | (lax.rem(i, 2) != core))
            def _():
                do(i)

            return t

        lax.fori_loop(0, S, step, 0)

    def each_source(do, first=0, n=S):
        def step(k, t):
            d = first + lax.rem(me + k, n)

            @pl.when((d != me) | (par != core))
            def _():
                do(d)

            return t

        lax.fori_loop(0, n, step, 0)

    def kv_copy(i):
        p = lax.rem(i, 2)
        return remote(
            kv_send.at[i],
            kv.at[p, me],
            send_ss.at[0],
            kv_rs.at[me // QSRC],
            2 * (i // 2) + core,
            2 * yy + p,
        )

    def head_copy(n, send, recv, rs, i):
        return remote(
            send.at[i],
            recv.at[me],
            send_ss.at[n],
            rs,
            2 * (i // 2) + core,
            2 * yy + lax.rem(i, 2),
        )

    def source_copy(n, send, recv, rs, d):
        return remote(send.at[d], recv.at[here], send_ss.at[n], rs, d, 2 * yy + par)

    def own_copy(src, dst, sem):
        @pl.when(par == core)
        def _():
            pltpu.make_async_copy(src, dst, sem).start()

    def each_expert(do):
        def step(k, t):
            e = lax.rem(ex + k, E)
            for hf in range(2):
                x = 2 * lax.rem(e, 2) + hf

                @pl.when((e != expert) | (hf != half) | (core != grp))
                def _():
                    do(e, x * Z + mz, 2 * (e // 2) + grp)

            return t

        lax.fori_loop(0, E, step, 0)

    def each_list(do):
        def step(k, t):
            b = lax.rem(ex + k, E)
            for r in range(2):
                x = 2 * core + r

                @pl.when((b != ex) | (x != mx))
                def _():
                    do(r * E + b, x * Z + mz, b)

            return t

        lax.fori_loop(0, E, step, 0)

    def out_start(n):
        slot = half * E + ex

        @pl.when(core == grp)
        def _():
            pltpu.make_async_copy(x_send.at[n, expert], x_recv.at[n, slot], x_rs.at[n]).start()

        each_expert(
            lambda e, seq, exp: remote(
                x_send.at[n, e], x_recv.at[n, slot], send_ss.at[6 + n], x_rs.at[n], seq, exp
            ).start()
        )

    def x_landed(n):
        landed(x_recv.at[n], x_rs.at[n])

    def part_cols(c):
        return pl.ds(c * Z * KEEP, Z * KEEP)

    def back_start(n, cols, ss, rs):
        slot = half * E + expert

        @pl.when(core == grp)
        def _():
            pltpu.make_async_copy(
                y_send.at[n, half * E + ex, :, cols], y_recv.at[n, slot, :, cols], rs
            ).start()

        each_list(
            lambda i, seq, exp: remote(
                y_send.at[n, i, :, cols], y_recv.at[n, slot, :, cols], ss, rs, seq, exp
            ).start()
        )

    def sixteen_left(n, ref, cols):
        @pl.when(core == grp)
        def _():
            left(n, ref.at[pl.ds(0, 2 * E - 1), :, cols])

        @pl.when(core != grp)
        def _():
            left(n, ref.at[:, :, cols])

    RING, CORE, INIT = 13, 14, 15
    part_all = pl.ds(0, FOLDS * Z * KEEP)

    def at_z(o):
        return lax.rem(mz + o + Z, Z)

    def arrival(w, oz, part):
        return wt_rs.at[w, oz % Z if part != 1 else Z]

    def piece(w, oz, part, group, seq, exp, sem):
        view = wt.at[2 * core + w, at_z(oz)]
        if part is not None:
            view = wt.at[2 * core + w, at_z(oz), :, part]
        return remote(view, view, send_ss.at[group], sem, seq, exp)

    def wait(w, oz, parts):
        for part in (0, 1) if parts else (None,):
            piece(w, oz, part, RING, me, 2 * yy + sib, arrival(w, oz, part)).wait_recv()

    both = (1, -1)

    def hop(w, sgn, k):
        if k < Z // 2:
            part = None if k < Z // 2 - 1 else (0 if sgn > 0 else 1)
            sem = arrival(w, -sgn * (k + 1), part)
            piece(w, -sgn * k, part, RING, mx * Z + at_z(sgn), ex, sem).start()

    def to_core(w, oz):
        piece(w, oz, None, CORE, me, 2 * yy + sib, core_rs.at[w]).start()

    def along_z(k):
        for w in (0, 1):
            if k == Z // 2:
                wait(w, k, True)
                to_core(w, k)
            else:
                for s in both:
                    wait(w, -s * k, False)
                    hop(w, s, k)
                    to_core(w, -s * k)

    def init_start():
        for hf in range(2):
            cols = pl.ds(hf * (FF - WIDE), WIDE)
            x = 2 * core + hf
            for n, ref in enumerate((gate_w, up_w, down_w)):
                src, dst, sem = ref.at[:, :, cols], wt.at[mx, mz, n], wt_rs.at[half, 0]

                @pl.when((x == mx) & (core == grp))
                def _():
                    pltpu.make_async_copy(src, dst, sem).start()

                @pl.when((x != mx) | (core != grp))
                def _():
                    seq = x * Z + mz
                    remote(src, dst, send_ss.at[INIT], sem, seq, 2 * yy + grp).start()

    init_start()
    own_copy(kv_send.at[here], kv.at[core, me], kv_rs.at[me // QSRC])
    own_copy(q_send.at[here], q_recv.at[me], q_rs.at[0])
    each_head(lambda i: kv_copy(i).start())
    each_head(lambda i: head_copy(1, q_send, q_recv, q_rs.at[0], i).start())

    for w in (0, 1):
        landed(wt.at[2 * core + w, mz], wt_rs.at[w, 0])
        for s in both:
            hop(w, s, 0)
        to_core(w, 0)
    out_start(0)

    along_z(1)
    def swap_copy(b):
        view = kv.at[core, pl.ds(b * QSRC, QSRC)]
        return remote(view, view, send_ss.at[16], swap_rs.at[0, b], me, 2 * yy + sib)

    for b in range(NB):
        landed(kv.at[core, pl.ds(b * QSRC, QSRC)], kv_rs.at[b])
        swap_copy(b).start()
    landed(q_recv, q_rs.at[0])
    for b in range(NB):
        landed(kv.at[sib, pl.ds(b * QSRC, QSRC)], swap_rs.at[0, b])

    def key_block(c):
        return kv[0, c * QSRC : (c + 1) * QSRC].reshape(KB, HS)

    def value_block(c):
        return kv[1, c * QSRC : (c + 1) * QSRC].reshape(KB, HS)

    def query_block(b):
        return q_recv[b * QSRC : (b + 1) * QSRC].reshape(QB, HS)

    for b in range(NB):
        k_f = key_block(b).astype(F32)
        bias[b * KB : (b + 1) * KB] = jnp.where(k_f > MARK / 2, NEG, 0.0)
        k_t[:, b * KB : (b + 1) * KB] = k_f.T.astype(BF16)
        v_t[:, b * KB : (b + 1) * KB] = value_block(b).astype(F32).T.astype(BF16)

    qcol = lax.broadcasted_iota(jnp.int32, (KB, QB), 1)
    qent = (qcol // PR) * KEEP + core * PR + lax.rem(qcol, PR)
    causal = lax.broadcasted_iota(jnp.int32, (KB, QB), 0) <= qent

    def forward_block(b):
        cols = slice(b * QB, (b + 1) * QB)
        q_blk = query_block(b)
        top = None
        for c in range(b + 1):
            rows = slice(c * KB, (c + 1) * KB)
            half = bias[rows, :]
            sc = nt(key_block(c), q_blk) * scale + jnp.concatenate([half] * (QB // HS), 1)
            if c == b:
                sc = jnp.where(causal, sc, NEG)
            prob[rows, cols] = sc
            m = jnp.max(sc, axis=0, keepdims=True)
            top = m if top is None else jnp.maximum(top, m)
        total = jnp.zeros((1, QB), F32)
        for c in range(b + 1):
            rows = slice(c * KB, (c + 1) * KB)
            e = jnp.exp(prob[rows, cols] - top)
            prob[rows, cols] = e
            total = total + jnp.sum(e, axis=0, keepdims=True)
        inv = 1.0 / total
        out = jnp.zeros((HS, QB), F32)
        for c in range(b + 1):
            rows = slice(c * KB, (c + 1) * KB)
            pr = prob[rows, cols] * inv
            prob[rows, cols] = pr
            out = out + nn(v_t[:, rows], pr.astype(BF16))
        att_t[:, cols] = out
        a_send[b * QSRC : (b + 1) * QSRC] = out.T.astype(BF16).reshape(QSRC, PR, HS)
        each_source(
            lambda d: source_copy(2, a_send, a_recv, a_rs.at[0], d).start(), b * QSRC, QSRC
        )

    for b in range(NB):
        forward_block(b)
    own_copy(a_send.at[me], a_recv.at[here], a_rs.at[0])
    along_z(2)
    landed(a_recv, a_rs.at[0])

    attended = jnp.concatenate(
        [jnp.concatenate([a_recv[2 * h + p] for h in range(HEADS)], 1) for p in range(2)], 0
    )
    h1 = jnp.where(live_col, kept_f + attended.astype(F32), 0.0)
    inv_rms = lax.rsqrt(jnp.mean(h1 * h1, axis=1, keepdims=True) + EPSILON)
    normed = (h1 * inv_rms).astype(BF16)
    pack_all(x_send.at[1], nn(table_half, normed))
    out_start(1)
    pre = [jnp.zeros((NR, WIDE), F32)] * 3

    def weight_of(ax, n):
        return wt[ax, :, n].reshape(KC, WIDE)

    def expert_chunk(ax):
        cols = pl.ds(pl.multiple_of(ax * KC, KC), KC)
        r = x_rows[1, :, cols]
        g = x_rows[0, :, cols]
        pre[0] = pre[0] + nn(r, weight_of(ax, 0))
        pre[1] = pre[1] + nn(r, weight_of(ax, 1))
        pre[2] = pre[2] + nn(g, weight_of(ax, 2))

    along_z(3)
    along_z(Z // 2)
    x_landed(0)
    x_landed(1)
    used = lax.rem(lax.broadcasted_iota(jnp.int32, (NR, KC), 0), SLOT) < CAP
    for n in (0, 1):
        last = jnp.zeros((NR, KC), F32)
        for g in range(FOLDS):
            chunk = x_recv[n, :, :, quarter(g)].reshape(NR, KC)
            last = last + nn(unfold[g], chunk)
            x_rows[n, :, quarter(g)] = jnp.where(used, chunk.astype(F32), 0.0).astype(BF16)
        x_rows[n, :, quarter(FOLDS)] = last.astype(BF16)
    for w in (0, 1):
        expert_chunk(2 * core + w)
    for w in (0, 1):
        landed(wt.at[2 * sib + w], core_rs.at[w])
        expert_chunk(2 * sib + w)
    gate_pre, up_pre, mid_grad = pre
    sig = 1.0 / (1.0 + jnp.exp(-gate_pre))
    act = gate_pre * sig
    lane = lax.broadcasted_iota(jnp.int32, (NR, WIDE), 1)
    own = (lane >= 2 * WIDE - FF) | (half == 0)
    mid_grad = jnp.where(own, mid_grad, 0.0)
    gate_grad = (mid_grad * up_pre * sig * (1.0 + gate_pre * (1.0 - sig))).astype(BF16)
    up_grad = (mid_grad * act).astype(BF16)
    mid = jnp.where(own, act * up_pre, 0.0).astype(BF16)
    def back_of(c):
        return nt(gate_grad, weight_of(c, 0)) + nt(up_grad, weight_of(c, 1))

    last = back_of(FOLDS).astype(BF16)
    for g in range(FOLDS):
        pack(y_send.at[0], g, back_of(g), last)
        back_start(0, part_cols(g), send_ss.at[9 + g], rows_rs.at[g])
    last = nt(mid, weight_of(FOLDS, 2)).astype(BF16)
    for g in range(FOLDS):
        pack(y_send.at[1], g, nt(mid, weight_of(g, 2)), last)
    table_t = jnp.concatenate([table_t, table_t], 1)
    parts, last = [], jnp.zeros((KEEP, KC), F32)
    for g in range(FOLDS):
        landed(y_recv.at[0, :, :, part_cols(g)], rows_rs.at[g])
        chunk = y_recv[0, :, :, quarter(g)].reshape(NR, KC)
        parts.append(nn(table_t, chunk))
        last = last + nn(nt(table_t, fold[g]).astype(BF16), chunk)
    parts.append(last)
    normed_grad = jnp.concatenate(parts, 1)
    cubed = inv_rms * inv_rms * inv_rms
    h1_grad = (
        grad_f
        + inv_rms * normed_grad
        - h1 * cubed * jnp.mean(normed_grad * h1, axis=1, keepdims=True)
    )
    h1_grad = jnp.where(live_col, h1_grad, 0.0).astype(BF16)
    for h in range(HEADS):
        for p in range(2):
            g_send[2 * h + p] = h1_grad[p * PR : (p + 1) * PR, h * HS : (h + 1) * HS]
    own_copy(g_send.at[here], g_recv.at[me], g_rs.at[me // QSRC])
    each_head(lambda i: head_copy(3, g_send, g_recv, g_rs.at[me // QSRC], i).start())

    token = lax.broadcasted_iota(jnp.int32, (TOK, KEEP), 0)
    put = jnp.where(
        (token == index_row) & (lax.broadcasted_iota(jnp.int32, (TOK, KEEP), 1) < count),
        1.0,
        0.0,
    )
    replaced = jnp.sum(put, axis=1, keepdims=True) > 0.5
    put = put.astype(BF16)
    cotangent[...] = jnp.where(replaced, nn(put, h1_grad), cotangent[...].astype(F32)).astype(
        BF16
    )
    input_grad_out = load(0, cotangent, input_grad_h)
    input_grad_out.start()
    back_start(1, part_all, send_ss.at[8], y_rs.at[0])

    def give_copy(c):
        rows = pl.ds(c * KB, KB)
        return remote(
            acc.at[sib, rows],
            other.at[rows],
            send_ss.at[17],
            swap_rs.at[1, c],
            me,
            2 * yy + sib,
        )

    def finish_block(c):
        rows = slice(c * KB, (c + 1) * KB)
        landed(other.at[pl.ds(c * KB, KB)], swap_rs.at[1, c])
        whole = acc[core, rows] + other[rows]
        b_send[c * QSRC : (c + 1) * QSRC] = whole.astype(BF16).reshape(QSRC, KEEP, HS)
        each_source(
            lambda d: source_copy(4, b_send, b_recv, b_rs.at[0], d).start(), c * QSRC, QSRC
        )

    dout = [None] * NB
    delta = [None] * NB
    dq_t = [jnp.zeros((HS, QB), F32)] * NB
    for c in reversed(range(NB)):
        rows = slice(c * KB, (c + 1) * KB)
        block = pl.ds(c * QSRC, QSRC)
        landed(g_recv.at[block], g_rs.at[c])
        dout[c] = g_recv[c * QSRC : (c + 1) * QSRC].reshape(QB, HS)
        turn = dout[c].astype(F32).T * att_t[:, c * QB : (c + 1) * QB]
        delta[c] = jnp.sum(turn, axis=0, keepdims=True)
        dk = jnp.zeros((KB, HS), F32)
        dv = jnp.zeros((KB, HS), F32)
        for b in range(c, NB):
            pr = prob[rows, b * QB : (b + 1) * QB]
            ds = (pr * (nt(value_block(c), dout[b]) - delta[b]) * scale).astype(BF16)
            dq_t[b] = dq_t[b] + nn(k_t[:, rows], ds)
            dk = dk + nn(ds, query_block(b))
            dv = dv + nn(pr.astype(BF16), dout[b])
        acc[0, rows] = dk
        acc[1, rows] = dv
        give_copy(c).start()
        if c < NB - 1:
            finish_block(c + 1)
    for b in range(NB):
        dq_send[b * QSRC : (b + 1) * QSRC] = dq_t[b].T.astype(BF16).reshape(QSRC, PR, HS)
    each_source(lambda d: source_copy(5, dq_send, dq_recv, b_rs.at[1], d).start())
    finish_block(0)
    own_copy(dq_send.at[me], dq_recv.at[here], b_rs.at[1])
    own_copy(b_send.at[me], b_recv.at[here], b_rs.at[0])

    landed(y_recv.at[1], y_rs.at[0])
    parts, last = [], jnp.zeros((KEEP, KC), F32)
    made_last = jnp.zeros((NR, KC), F32)
    per_slot = jnp.zeros((NS, 1), F32)

    def against(rows, g):
        both_halves = (rows[:NS] + rows[NS:]) * grad_sel[:, quarter(g)].astype(F32)
        return jnp.sum(both_halves, axis=1, keepdims=True)

    for g in range(FOLDS):
        chunk = y_recv[1, :, :, quarter(g)].reshape(NR, KC)
        there = jnp.zeros((KEEP, KC), F32)
        for w in (w_high, w_low):
            w = jnp.concatenate([w, w], 1)
            there = there + nn(w, chunk)
            last = last + nn(nt(w, fold[g]).astype(BF16), chunk)
        parts.append(there)
        made_last = made_last + nn(unfold[g], chunk)
        per_slot = per_slot + against(chunk.astype(F32), g)
    per_slot = per_slot + against(made_last, FOLDS)
    mixture = jnp.concatenate(parts + [last], 1)
    new_rows = (h1 + mixture).astype(BF16)
    residual[...] = jnp.where(replaced, nn(put, new_rows), residual[...].astype(F32)).astype(BF16)
    spread = table * per_slot
    for k in range(expert_ids.shape[0]):
        hit = expert_ids[k] == slot_exp
        gate_grads[k] = jnp.sum(jnp.where(hit, spread, 0.0), axis=0, keepdims=True)
    output_out = load(1, residual, output_h)
    output_out.start()
    left_all(0, kv_send)
    left_all(1, q_send)
    left_all(2, a_send)
    left_all(3, g_send)
    for n in (0, 1):
        sixteen_left(6 + n, x_recv.at[n], part_all)
    sixteen_left(8, y_send.at[1], part_all)
    for c in range(FOLDS):
        sixteen_left(9 + c, y_send.at[0], part_cols(c))
    left(RING, wt.at[pl.ds(0, 2), pl.ds(0, Z - 1)])
    left(CORE, wt.at[pl.ds(0, 2)])
    left(16, kv.at[core])
    left(17, acc.at[sib])

    @pl.when(core == grp)
    def _():
        left(INIT, wt.at[0, 0])

    @pl.when(core != grp)
    def _():
        left(INIT, wt.at[0, pl.ds(0, 2)])

    landed(b_recv, b_rs.at[0])
    landed(dq_recv, b_rs.at[1])
    for h in range(HEADS):
        c0 = h * HS
        for p in range(2):
            projected[p * PR : (p + 1) * PR, c0 : c0 + HS] = dq_recv[2 * h + p]
            o = (1 + p) * D + c0
            projected[:, o : o + HS] = b_recv[2 * h + p]
    projected_grad_out = load(2, projected, projected_grad_h)
    projected_grad_out.start()
    left_all(4, b_send)
    left_all(5, dq_send)
    for copy in (input_grad_out, output_out, projected_grad_out):
        copy.wait()


def finish(a, b, c, d, out_a, out_b, out_c, out_d, sa, sb, sc, sd, sem):
    ins, outs = [], []
    for src, stage, dst in ((a, sa, out_a), (b, sb, out_b), (c, sc, out_c)):
        n = src.shape[0] // PIECES
        for k in range(PIECES):
            rows = pl.ds(k * n, n)
            ins.append((src.at[rows], stage.at[rows]))
            outs.append((stage.at[rows], dst.at[0, rows]))
    ins.append((d, sd))
    outs.append((sd, out_d))
    ins = [pltpu.make_async_copy(*c, sem.at[0, i]) for i, c in enumerate(ins)]
    outs = [pltpu.make_async_copy(*c, sem.at[1, i]) for i, c in enumerate(outs)]
    for copy in ins:
        copy.start()
    for copy, after in zip(ins, outs):
        copy.wait()
        after.start()
    for copy in outs:
        copy.wait()


def body(
    residual,
    kept_index,
    kept_count,
    projected,
    expert_ids,
    gate_values,
    gate_weight,
    up_weight,
    down_weight,
    cotangent,
):
    S = lax.axis_size("seq")
    E = lax.axis_size("exp")
    _, TOK, D = residual.shape
    KEEP = kept_index.shape[1]
    FF = gate_weight.shape[2]
    TOPK = expert_ids.shape[2]
    Z = S // X
    HEADS = D // HS
    PR = KEEP // 2
    NB = S // QSRC
    vm = pl.BlockSpec(memory_space=pltpu.VMEM)
    hbm = pl.BlockSpec(memory_space=pl.ANY)
    dma = pltpu.SemaphoreType.DMA
    out = pl.pallas_call(
        functools.partial(kernel, S, E),
        out_shape=[
            jax.ShapeDtypeStruct((TOK, D), BF16),
            jax.ShapeDtypeStruct((TOK, D), BF16),
            jax.ShapeDtypeStruct((KEEP, 3 * D), BF16),
            jax.ShapeDtypeStruct((TOPK, 1, KEEP), F32),
        ],
        in_specs=[hbm] * 10,
        out_specs=[hbm, hbm, hbm, vm],
        scratch_shapes=[
            pltpu.VMEM((TOK, D), BF16),
            pltpu.VMEM((TOK, D), BF16),
            pltpu.VMEM((KEEP, 3 * D), BF16),
            pltpu.VMEM((1, KEEP), jnp.int32),
            pltpu.VMEM((1, 1), jnp.int32),
            pltpu.VMEM((TOPK, 1, KEEP), jnp.int32),
            pltpu.VMEM((TOPK, 1, KEEP), F32),
            dma((10,)),
            pltpu.VMEM((S, KEEP, HS), BF16),
            pltpu.VMEM((2, S, KEEP, HS), BF16),
            pltpu.VMEM((S, PR, HS), BF16),
            pltpu.VMEM((S, PR, HS), BF16),
            pltpu.VMEM((S, PR, HS), BF16),
            pltpu.VMEM((S, PR, HS), BF16),
            pltpu.VMEM((S, PR, HS), BF16),
            pltpu.VMEM((S, PR, HS), BF16),
            pltpu.VMEM((S, KEEP, HS), BF16),
            pltpu.VMEM((S, KEEP, HS), BF16),
            pltpu.VMEM((S, PR, HS), BF16),
            pltpu.VMEM((S, PR, HS), BF16),
            pltpu.VMEM((2, E, SLOT, D * CAP // SLOT), BF16),
            pltpu.VMEM((2, 2 * E, SLOT, D * CAP // SLOT), BF16),
            pltpu.VMEM((2, 2 * E, SLOT, D * CAP // SLOT), BF16),
            pltpu.VMEM((2, 2 * E, SLOT, D * CAP // SLOT), BF16),
            pltpu.VMEM((2, 2 * E * SLOT, D), BF16),
            pltpu.VMEM((X, Z, 3, 2, KEEP // 2, WIDE), BF16),
            pltpu.VMEM((S * KEEP, HS), F32),
            pltpu.VMEM((HS, S * KEEP), BF16),
            pltpu.VMEM((HS, S * KEEP), BF16),
            pltpu.VMEM((S * KEEP, S * PR), F32),
            pltpu.VMEM((HS, S * PR), F32),
            pltpu.VMEM((2, S * KEEP, HS), F32),
            pltpu.VMEM((S * KEEP, HS), F32),
        ]
        + [
            dma((18,)),
            dma((NB,)),
            dma((1,)),
            dma((1,)),
            dma((NB,)),
            dma((2,)),
            dma((2,)),
            dma((1,)),
            dma((X,)),
            dma((2, NB)),
            dma((2, Z + 1)),
            dma((2,)),
        ],
        compiler_params=pltpu.CompilerParams(
            collective_id=0, has_side_effects=True, vmem_limit_bytes=60 * 1024 * 1024
        ),
    )(
        residual[0],
        kept_index,
        kept_count,
        projected[0],
        jnp.transpose(expert_ids, (2, 0, 1)),
        jnp.transpose(gate_values, (2, 0, 1)),
        gate_weight[0].reshape(2, KEEP // 2, FF),
        up_weight[0].reshape(2, KEEP // 2, FF),
        down_weight[0].T.reshape(2, KEEP // 2, FF),
        cotangent[0],
    )
    out = pl.pallas_call(
        finish,
        out_shape=[
            jax.ShapeDtypeStruct((1, TOK, D), BF16),
            jax.ShapeDtypeStruct((1, TOK, D), BF16),
            jax.ShapeDtypeStruct((1, KEEP, 3 * D), BF16),
            jax.ShapeDtypeStruct((TOPK, 1, KEEP), F32),
        ],
        in_specs=[hbm] * 4,
        out_specs=[hbm] * 4,
        scratch_shapes=[
            pltpu.VMEM((TOK, D), BF16),
            pltpu.VMEM((TOK, D), BF16),
            pltpu.VMEM((KEEP, 3 * D), BF16),
            pltpu.VMEM((TOPK, 1, KEEP), F32),
            dma((2, 3 * PIECES + 1)),
        ],
        compiler_params=pltpu.CompilerParams(vmem_limit_bytes=60 * 1024 * 1024),
    )(*out)
    return (out[0], out[1], out[2], jnp.transpose(out[3], (1, 2, 0)))


def solution(mesh):
    row = P("exp", "seq", None)
    in_specs = (row, P("exp", "seq"), P("exp", "seq")) + (row,) * 5 + (P("exp", None, "seq"), row)
    return jax.shard_map(
        body, mesh=mesh, in_specs=in_specs, out_specs=(row,) * 4, check_vma=False
    )
```

time: 154 us -> 137 us (0.89)
  Pallas kernels: 146 us -> 136 us
  local copies, waits for them, and re-layouts: 5.37 us -> 0 us
    pallas_call x1, Pallas kernels: 146 us -> 133 us  [body(): pl.pallas_call(functools.partial(kernel, S, E), out_shape=[jax.ShapeDtype...]
    unnamed x10 -> x0, local copies, waits for them, and re-layouts: 5.37 us -> none
    pallas_call x0 -> x1, Pallas kernels: none -> 2.73 us  [body(): pl.pallas_call(finish, out_shape=[jax.ShapeDtypeStruct((1, TOK, D), BF16)...]
where the time goes in v4:
time: 137 us
  Pallas kernels  136 us (99%)
  between operations  1.45 us (1%)
    pallas_call x1, Pallas kernels, body(): pl.pallas_call(functools.partial(kernel, S, E), out_shape=[jax.ShapeDtype...  133 us

profile of v4, /device:TPU:1, one launch (start us, length us, event | category | flops | bytes accessed | tf_op | source)
XLA Modules:
  0.0 137.3 jit_solution(5420017797040746031)
XLA Ops:
  1.3 133.1 %shard_map.129 = (bf16[256,2048]{1,0:T(8,128)(2,1)}, bf16[256,2048]{1,0:T(8,128)(2,1)}, bf16[64,6144]{1,0:T(8,128)(2,1)}, f32[6,1,64]{2,1,0:T(1,128)}) custom-call(bf16[256,2048]{1,0:T(8,128)(2,1)} %bitcast.13, s32[1,64]{1,0:T(1,128)} %kept_index_h.1, s32[1,1]{1,0:T(1,128)S(6)} %copy.14.kept_count_h, bf16[64,6144]{1,0:T(8,128)(2,1)} %bitcast.15, ...), custom_call_target="tpu_custom_call" | custom-call | tf_op jit(solution)/shard_map/pallas_call | solution.py:784
  134.4 2.7 %shard_map.130 = (bf16[1,256,2048]{2,1,0:T(8,128)(2,1)}, bf16[1,256,2048]{2,1,0:T(8,128)(2,1)}, bf16[1,64,6144]{2,1,0:T(8,128)(2,1)}, f32[6,1,64]{2,1,0:T(1,128)}) custom-call(bf16[256,2048]{1,0:T(8,128)(2,1)} %get-tuple-element.12.a, bf16[256,2048]{1,0:T(8,128)(2,1)} %get-tuple-element.13.b, bf16[64,6144]{1,0:T(8,128)(2,1)} %get-tuple-element.14.c, ...), custom_call_target="tpu_custom_call" | custom-call | tf_op jit(solution)/shard_map/pallas_call | solution.py:858

commit v5 on v4

--- a/solution.py
+++ b/solution.py
@@ -19,7 +19,7 @@
 BF16 = jnp.bfloat16
 MESH = pl.DeviceIdType.MESH
 NEG = -1e30
-WIDE = 768
+LANES = 128
 MARK = 1024.0
 
 
@@ -73,6 +73,8 @@
     y_send,
     y_recv,
     x_rows,
+    tile,
+    mix,
     wt,
     bias,
     k_t,
@@ -104,6 +106,9 @@
     KB = QSRC * KEEP
     QB = QSRC * PR
     NS = E * SLOT
+    MAIN = FF // (2 * LANES) * LANES
+    WIDE = MAIN + LANES
+    GU = 2 * MAIN + LANES
     scale = HS**-0.5
     me = lax.axis_index("seq")
     ex = lax.axis_index("exp")
@@ -130,7 +135,12 @@
         load(8, expert_ids_h, expert_ids),
         load(9, gate_values_h, gate_values),
     )
-    for copy in (projected_in, *small_in, cotangent_in, residual_in):
+    shared = pl.ds(MAIN, LANES)
+    tile_in = (
+        load(3, gate_w.at[:, :, shared], tile.at[0]),
+        load(4, up_w.at[:, :, shared], tile.at[1]),
+    )
+    for copy in (projected_in, *tile_in, *small_in, cotangent_in, residual_in):
         copy.start()
 
     def greet(seq, exp):
@@ -167,6 +177,14 @@
         for p in range(2):
             q_send[2 * h + p] = projected[p * PR : (p + 1) * PR, c0 : c0 + HS]
 
+    for copy in tile_in:
+        copy.wait()
+    tile_lane = lax.broadcasted_iota(jnp.int32, (KEEP, LANES), 1) // (LANES // 2)
+    tile_g = tile[0].reshape(KEEP, LANES).astype(F32)
+    tile_u = pltpu.roll(tile[1].reshape(KEEP, LANES).astype(F32), LANES // 2, 1)
+    for hf in range(2):
+        blend = jnp.where(tile_lane == hf, tile_g, tile_u).astype(BF16)
+        mix[hf] = blend.reshape(2, KEEP // 2, LANES)
     slot_row = lax.broadcasted_iota(jnp.int32, (NS, KEEP), 0)
     slot_exp = slot_row // SLOT
     slot_pos = slot_row - slot_exp * SLOT
@@ -261,50 +279,38 @@
 
     here = 2 * head + core
 
+    col_x = [lax.rem(mx + o, X) for o in range(X)]
+    row_z = [lax.rem(mz + o, Z) for o in range(Z)]
+
+    def unless_own(maybe, do, *args):
+        if maybe is None:
+            do(*args)
+        else:
+            pl.when(maybe)(lambda: do(*args))
+
     def each_head(do):
-        def step(k, t):
-            i = lax.rem(k + 2 * head, S)
-
-            @pl.when((2 * (i // 2) + core != me) | (lax.rem(i, 2) != core))
-            def _():
-                do(i)
-
-            return t
-
-        lax.fori_loop(0, S, step, 0)
-
-    def each_source(do, first=0, n=S):
-        def step(k, t):
-            d = first + lax.rem(me + k, n)
-
-            @pl.when((d != me) | (par != core))
-            def _():
-                do(d)
-
-            return t
-
-        lax.fori_loop(0, n, step, 0)
-
-    def kv_copy(i):
-        p = lax.rem(i, 2)
+        for q in range(2):
+            for j in range(Z // 4):
+                for o, x in enumerate(col_x):
+                    z = lax.rem(mz // 4 * 2 + 2 * j, Z // 2) + lax.rem(q + x, 2)
+                    h = x * (Z // 2) + z
+                    for p in range(2):
+                        away = None if o else (h != head) | (par != core) | (core != p)
+                        unless_own(away, do, 2 * h + p, h, p)
+
+    def each_source(do, x0=None):
+        for o, x in enumerate(col_x) if x0 is None else ((0, x0),):
+            for k, z in enumerate(row_z):
+                away = None if o or k else (x != mx) | (par != core)
+                unless_own(away, do, x * Z + z)
+
+    def kv_copy(i, h, p):
         return remote(
-            kv_send.at[i],
-            kv.at[p, me],
-            send_ss.at[0],
-            kv_rs.at[me // QSRC],
-            2 * (i // 2) + core,
-            2 * yy + p,
+            kv_send.at[i], kv.at[p, me], send_ss.at[0], kv_rs.at[me // QSRC], 2 * h + core, 2 * yy + p
         )
 
-    def head_copy(n, send, recv, rs, i):
-        return remote(
-            send.at[i],
-            recv.at[me],
-            send_ss.at[n],
-            rs,
-            2 * (i // 2) + core,
-            2 * yy + lax.rem(i, 2),
-        )
+    def head_copy(n, send, recv, rs, i, h, p):
+        return remote(send.at[i], recv.at[me], send_ss.at[n], rs, 2 * h + core, 2 * yy + p)
 
     def source_copy(n, send, recv, rs, d):
         return remote(send.at[d], recv.at[here], send_ss.at[n], rs, d, 2 * yy + par)
@@ -397,7 +403,7 @@
     def piece(w, oz, part, group, seq, exp, sem):
         view = wt.at[2 * core + w, at_z(oz)]
         if part is not None:
-            view = wt.at[2 * core + w, at_z(oz), :, part]
+            view = wt.at[2 * core + w, at_z(oz), part]
         return remote(view, view, send_ss.at[group], sem, seq, exp)
 
     def wait(w, oz, parts):
@@ -428,10 +434,17 @@
 
     def init_start():
         for hf in range(2):
-            cols = pl.ds(hf * (FF - WIDE), WIDE)
             x = 2 * core + hf
-            for n, ref in enumerate((gate_w, up_w, down_w)):
-                src, dst, sem = ref.at[:, :, cols], wt.at[mx, mz, n], wt_rs.at[half, 0]
+            main = pl.ds(hf * WIDE, MAIN)
+            parts = (
+                (gate_w.at[:, :, main], 0, MAIN),
+                (up_w.at[:, :, main], MAIN, MAIN),
+                (mix.at[hf], 2 * MAIN, LANES),
+                (down_w.at[:, :, main], GU, MAIN),
+                (down_w.at[:, :, shared], GU + MAIN, LANES),
+            )
+            for src, at, n in parts:
+                dst, sem = wt.at[mx, mz, :, :, pl.ds(at, n)], wt_rs.at[half, 0]
 
                 @pl.when((x == mx) & (core == grp))
                 def _():
@@ -445,8 +458,8 @@
     init_start()
     own_copy(kv_send.at[here], kv.at[core, me], kv_rs.at[me // QSRC])
     own_copy(q_send.at[here], q_recv.at[me], q_rs.at[0])
-    each_head(lambda i: kv_copy(i).start())
-    each_head(lambda i: head_copy(1, q_send, q_recv, q_rs.at[0], i).start())
+    each_head(lambda *i: kv_copy(*i).start())
+    each_head(lambda *i: head_copy(1, q_send, q_recv, q_rs.at[0], *i).start())
 
     for w in (0, 1):
         landed(wt.at[2 * core + w, mz], wt_rs.at[w, 0])
@@ -515,7 +528,7 @@
         att_t[:, cols] = out
         a_send[b * QSRC : (b + 1) * QSRC] = out.T.astype(BF16).reshape(QSRC, PR, HS)
         each_source(
-            lambda d: source_copy(2, a_send, a_recv, a_rs.at[0], d).start(), b * QSRC, QSRC
+            lambda d: source_copy(2, a_send, a_recv, a_rs.at[0], d).start(), b
         )
 
     for b in range(NB):
@@ -532,21 +545,20 @@
     normed = (h1 * inv_rms).astype(BF16)
     pack_all(x_send.at[1], nn(table_half, normed))
     out_start(1)
-    pre = [jnp.zeros((NR, WIDE), F32)] * 3
-
-    def weight_of(ax, n):
-        return wt[ax, :, n].reshape(KC, WIDE)
+    pre = [jnp.zeros((NR, GU), F32), jnp.zeros((NR, WIDE), F32)]
+
+    def gate_up_of(ax):
+        return wt[ax, :, :, :, 0:GU].reshape(KC, GU)
+
+    def down_of(ax):
+        return wt[ax, :, :, :, GU:].reshape(KC, WIDE)
 
     def expert_chunk(ax):
         cols = pl.ds(pl.multiple_of(ax * KC, KC), KC)
-        r = x_rows[1, :, cols]
-        g = x_rows[0, :, cols]
-        pre[0] = pre[0] + nn(r, weight_of(ax, 0))
-        pre[1] = pre[1] + nn(r, weight_of(ax, 1))
-        pre[2] = pre[2] + nn(g, weight_of(ax, 2))
+        pre[0] = pre[0] + nn(x_rows[1, :, cols], gate_up_of(ax))
+        pre[1] = pre[1] + nn(x_rows[0, :, cols], down_of(ax))
 
     along_z(3)
-    along_z(Z // 2)
     x_landed(0)
     x_landed(1)
     used = lax.rem(lax.broadcasted_iota(jnp.int32, (NR, KC), 0), SLOT) < CAP
@@ -557,30 +569,38 @@
             last = last + nn(unfold[g], chunk)
             x_rows[n, :, quarter(g)] = jnp.where(used, chunk.astype(F32), 0.0).astype(BF16)
         x_rows[n, :, quarter(FOLDS)] = last.astype(BF16)
+    along_z(Z // 2)
     for w in (0, 1):
         expert_chunk(2 * core + w)
     for w in (0, 1):
         landed(wt.at[2 * sib + w], core_rs.at[w])
         expert_chunk(2 * sib + w)
-    gate_pre, up_pre, mid_grad = pre
+    ahead, mid_grad = pre
+    turned_tile = pltpu.roll(ahead[:, 2 * MAIN :], LANES // 2, 1)
+    gate_pre = jnp.concatenate([ahead[:, :MAIN], ahead[:, 2 * MAIN :]], 1)
+    up_pre = jnp.concatenate([ahead[:, MAIN : 2 * MAIN], turned_tile], 1)
     sig = 1.0 / (1.0 + jnp.exp(-gate_pre))
     act = gate_pre * sig
     lane = lax.broadcasted_iota(jnp.int32, (NR, WIDE), 1)
-    own = (lane >= 2 * WIDE - FF) | (half == 0)
+    own = (lane < MAIN) | ((lane - MAIN) // (LANES // 2) == half)
     mid_grad = jnp.where(own, mid_grad, 0.0)
-    gate_grad = (mid_grad * up_pre * sig * (1.0 + gate_pre * (1.0 - sig))).astype(BF16)
-    up_grad = (mid_grad * act).astype(BF16)
+    gate_grad = mid_grad * up_pre * sig * (1.0 + gate_pre * (1.0 - sig))
+    up_grad = mid_grad * act
+    turned_tile = pltpu.roll(up_grad[:, MAIN:], LANES // 2, 1)
+    behind = jnp.concatenate(
+        [gate_grad[:, :MAIN], up_grad[:, :MAIN], gate_grad[:, MAIN:] + turned_tile], 1
+    ).astype(BF16)
     mid = jnp.where(own, act * up_pre, 0.0).astype(BF16)
     def back_of(c):
-        return nt(gate_grad, weight_of(c, 0)) + nt(up_grad, weight_of(c, 1))
+        return nt(behind, gate_up_of(c))
 
     last = back_of(FOLDS).astype(BF16)
     for g in range(FOLDS):
         pack(y_send.at[0], g, back_of(g), last)
         back_start(0, part_cols(g), send_ss.at[9 + g], rows_rs.at[g])
-    last = nt(mid, weight_of(FOLDS, 2)).astype(BF16)
+    last = nt(mid, down_of(FOLDS)).astype(BF16)
     for g in range(FOLDS):
-        pack(y_send.at[1], g, nt(mid, weight_of(g, 2)), last)
+        pack(y_send.at[1], g, nt(mid, down_of(g)), last)
     table_t = jnp.concatenate([table_t, table_t], 1)
     parts, last = [], jnp.zeros((KEEP, KC), F32)
     for g in range(FOLDS):
@@ -601,7 +621,7 @@
         for p in range(2):
             g_send[2 * h + p] = h1_grad[p * PR : (p + 1) * PR, h * HS : (h + 1) * HS]
     own_copy(g_send.at[here], g_recv.at[me], g_rs.at[me // QSRC])
-    each_head(lambda i: head_copy(3, g_send, g_recv, g_rs.at[me // QSRC], i).start())
+    each_head(lambda *i: head_copy(3, g_send, g_recv, g_rs.at[me // QSRC], *i).start())
 
     token = lax.broadcasted_iota(jnp.int32, (TOK, KEEP), 0)
     put = jnp.where(
@@ -635,7 +655,7 @@
         whole = acc[core, rows] + other[rows]
         b_send[c * QSRC : (c + 1) * QSRC] = whole.astype(BF16).reshape(QSRC, KEEP, HS)
         each_source(
-            lambda d: source_copy(4, b_send, b_recv, b_rs.at[0], d).start(), c * QSRC, QSRC
+            lambda d: source_copy(4, b_send, b_recv, b_rs.at[0], d).start(), c
         )
 
     dout = [None] * NB
@@ -817,7 +837,9 @@
             pltpu.VMEM((2, 2 * E, SLOT, D * CAP // SLOT), BF16),
             pltpu.VMEM((2, 2 * E, SLOT, D * CAP // SLOT), BF16),
             pltpu.VMEM((2, 2 * E * SLOT, D), BF16),
-            pltpu.VMEM((X, Z, 3, 2, KEEP // 2, WIDE), BF16),
+            pltpu.VMEM((2, 2, KEEP // 2, LANES), BF16),
+            pltpu.VMEM((2, 2, KEEP // 2, LANES), BF16),
+            pltpu.VMEM((X, Z, 2, KEEP // 2, FF // LANES // 2 * LANES * 3 + 2 * LANES), BF16),
             pltpu.VMEM((S * KEEP, HS), F32),
             pltpu.VMEM((HS, S * KEEP), BF16),
             pltpu.VMEM((HS, S * KEEP), BF16),

time: 137 us -> 134 us (0.978)
  Pallas kernels: 136 us -> 133 us
    pallas_call x1, Pallas kernels: 133 us -> 130 us  [body(): pl.pallas_call(functools.partial(kernel, S, E), out_shape=[jax.ShapeDtype...]
where the time goes in v5:
time: 134 us
  Pallas kernels  133 us (99%)
  between operations  1.45 us (1%)
    pallas_call x1, Pallas kernels, body(): pl.pallas_call(functools.partial(kernel, S, E), out_shape=[jax.ShapeDtype...  130 us
    pallas_call x1, Pallas kernels, body(): pl.pallas_call(finish, out_shape=[jax.ShapeDtypeStruct((1, TOK, D), BF16)...  2.73 us

profile of v5, /device:TPU:1, one launch (start us, length us, event | category | flops | bytes accessed | tf_op | source)
XLA Modules:
  0.0 134.3 jit_solution(12352124925064530956)
XLA Ops:
  1.3 130.1 %shard_map.129 = (bf16[256,2048]{1,0:T(8,128)(2,1)}, bf16[256,2048]{1,0:T(8,128)(2,1)}, bf16[64,6144]{1,0:T(8,128)(2,1)}, f32[6,1,64]{2,1,0:T(1,128)}) custom-call(bf16[256,2048]{1,0:T(8,128)(2,1)} %bitcast.13, s32[1,64]{1,0:T(1,128)} %kept_index_h.1, s32[1,1]{1,0:T(1,128)S(6)} %copy.14.kept_count_h, bf16[64,6144]{1,0:T(8,128)(2,1)} %bitcast.15, ...), custom_call_target="tpu_custom_call" | custom-call | tf_op jit(solution)/shard_map/pallas_call | solution.py:804
  131.4 2.7 %shard_map.130 = (bf16[1,256,2048]{2,1,0:T(8,128)(2,1)}, bf16[1,256,2048]{2,1,0:T(8,128)(2,1)}, bf16[1,64,6144]{2,1,0:T(8,128)(2,1)}, f32[6,1,64]{2,1,0:T(1,128)}) custom-call(bf16[256,2048]{1,0:T(8,128)(2,1)} %get-tuple-element.12.a, bf16[256,2048]{1,0:T(8,128)(2,1)} %get-tuple-element.13.b, bf16[64,6144]{1,0:T(8,128)(2,1)} %get-tuple-element.14.c, ...), custom_call_target="tpu_custom_call" | custom-call | tf_op jit(solution)/shard_map/pallas_call | solution.py:880

commit v6 on v5

--- a/solution.py
+++ b/solution.py
@@ -12,7 +12,6 @@
 CAP = 12
 FOLDS = 3
 EPSILON = 1e-06
-PIECES = 2
 X = 4
 QSRC = 8
 F32 = jnp.float32
@@ -46,7 +45,8 @@
     cotangent_h,
     output_h,
     input_grad_h,
-    projected_grad_h,
+    b_recv,
+    dq_recv,
     gate_grads,
     residual,
     cotangent,
@@ -65,9 +65,7 @@
     g_send,
     g_recv,
     b_send,
-    b_recv,
     dq_send,
-    dq_recv,
     x_send,
     x_recv,
     y_send,
@@ -289,14 +287,12 @@
             pl.when(maybe)(lambda: do(*args))
 
     def each_head(do):
-        for q in range(2):
-            for j in range(Z // 4):
-                for o, x in enumerate(col_x):
-                    z = lax.rem(mz // 4 * 2 + 2 * j, Z // 2) + lax.rem(q + x, 2)
-                    h = x * (Z // 2) + z
-                    for p in range(2):
-                        away = None if o else (h != head) | (par != core) | (core != p)
-                        unless_own(away, do, 2 * h + p, h, p)
+        for q in range(Z // 2):
+            for o, x in enumerate(col_x):
+                h = x * (Z // 2) + lax.rem(x + q, Z // 2)
+                for p in range(2):
+                    away = None if o else (h != head) | (par != core) | (core != p)
+                    unless_own(away, do, 2 * h + p, h, p)
 
     def each_source(do, x0=None):
         for o, x in enumerate(col_x) if x0 is None else ((0, x0),):
@@ -592,15 +588,15 @@
     ).astype(BF16)
     mid = jnp.where(own, act * up_pre, 0.0).astype(BF16)
     def back_of(c):
-        return nt(behind, gate_up_of(c))
+        return nt(gate_up_of(c), behind).T
 
     last = back_of(FOLDS).astype(BF16)
     for g in range(FOLDS):
         pack(y_send.at[0], g, back_of(g), last)
         back_start(0, part_cols(g), send_ss.at[9 + g], rows_rs.at[g])
-    last = nt(mid, down_of(FOLDS)).astype(BF16)
+    last = nt(down_of(FOLDS), mid).T.astype(BF16)
     for g in range(FOLDS):
-        pack(y_send.at[1], g, nt(mid, down_of(g)), last)
+        pack(y_send.at[1], g, nt(down_of(g), mid).T, last)
     table_t = jnp.concatenate([table_t, table_t], 1)
     parts, last = [], jnp.zeros((KEEP, KC), F32)
     for g in range(FOLDS):
@@ -741,35 +737,33 @@
 
     landed(b_recv, b_rs.at[0])
     landed(dq_recv, b_rs.at[1])
-    for h in range(HEADS):
-        c0 = h * HS
-        for p in range(2):
-            projected[p * PR : (p + 1) * PR, c0 : c0 + HS] = dq_recv[2 * h + p]
-            o = (1 + p) * D + c0
-            projected[:, o : o + HS] = b_recv[2 * h + p]
-    projected_grad_out = load(2, projected, projected_grad_h)
-    projected_grad_out.start()
     left_all(4, b_send)
     left_all(5, dq_send)
-    for copy in (input_grad_out, output_out, projected_grad_out):
+    for copy in (input_grad_out, output_out):
         copy.wait()
 
 
-def finish(a, b, c, d, out_a, out_b, out_c, out_d, sa, sb, sc, sd, sem):
+def finish(a, b, c, e, d, out_a, out_b, out_c, out_d, sa, sb, sc, se, sd, sp, sem):
+    heads, _, width = c.shape
+    rows = e.shape[1]
     ins, outs = [], []
-    for src, stage, dst in ((a, sa, out_a), (b, sb, out_b), (c, sc, out_c)):
-        n = src.shape[0] // PIECES
-        for k in range(PIECES):
-            rows = pl.ds(k * n, n)
-            ins.append((src.at[rows], stage.at[rows]))
-            outs.append((stage.at[rows], dst.at[0, rows]))
-    ins.append((d, sd))
-    outs.append((sd, out_d))
-    ins = [pltpu.make_async_copy(*c, sem.at[0, i]) for i, c in enumerate(ins)]
-    outs = [pltpu.make_async_copy(*c, sem.at[1, i]) for i, c in enumerate(outs)]
+    pairs = ((c, sc, None), (e, se, None), (a, sa, out_a.at[0]), (b, sb, out_b.at[0]), (d, sd, out_d))
+    for i, (src, stage, dst) in enumerate(pairs):
+        ins.append(pltpu.make_async_copy(src, stage, sem.at[0, i]))
+        if dst is not None:
+            outs.append(pltpu.make_async_copy(stage, dst, sem.at[1, i]))
     for copy in ins:
         copy.start()
-    for copy, after in zip(ins, outs):
+    for copy in ins[:2]:
+        copy.wait()
+    for i in range(heads):
+        c0, p = i // 2 * width, i % 2
+        o = (1 + p) * (heads // 2) * width + c0
+        sp[p * rows : (p + 1) * rows, c0 : c0 + width] = se[i]
+        sp[:, o : o + width] = sc[i]
+    outs.append(pltpu.make_async_copy(sp, out_c.at[0], sem.at[1, 0]))
+    outs[-1].start()
+    for copy, after in zip(ins[2:], outs):
         copy.wait()
         after.start()
     for copy in outs:
@@ -806,11 +800,12 @@
         out_shape=[
             jax.ShapeDtypeStruct((TOK, D), BF16),
             jax.ShapeDtypeStruct((TOK, D), BF16),
-            jax.ShapeDtypeStruct((KEEP, 3 * D), BF16),
+            jax.ShapeDtypeStruct((S, KEEP, HS), BF16),
+            jax.ShapeDtypeStruct((S, PR, HS), BF16),
             jax.ShapeDtypeStruct((TOPK, 1, KEEP), F32),
         ],
         in_specs=[hbm] * 10,
-        out_specs=[hbm, hbm, hbm, vm],
+        out_specs=[hbm, hbm, hbm, hbm, vm],
         scratch_shapes=[
             pltpu.VMEM((TOK, D), BF16),
             pltpu.VMEM((TOK, D), BF16),
@@ -829,8 +824,6 @@
             pltpu.VMEM((S, PR, HS), BF16),
             pltpu.VMEM((S, PR, HS), BF16),
             pltpu.VMEM((S, KEEP, HS), BF16),
-            pltpu.VMEM((S, KEEP, HS), BF16),
-            pltpu.VMEM((S, PR, HS), BF16),
             pltpu.VMEM((S, PR, HS), BF16),
             pltpu.VMEM((2, E, SLOT, D * CAP // SLOT), BF16),
             pltpu.VMEM((2, 2 * E, SLOT, D * CAP // SLOT), BF16),
@@ -885,14 +878,16 @@
             jax.ShapeDtypeStruct((1, KEEP, 3 * D), BF16),
             jax.ShapeDtypeStruct((TOPK, 1, KEEP), F32),
         ],
-        in_specs=[hbm] * 4,
+        in_specs=[hbm] * 5,
         out_specs=[hbm] * 4,
         scratch_shapes=[
             pltpu.VMEM((TOK, D), BF16),
             pltpu.VMEM((TOK, D), BF16),
+            pltpu.VMEM((S, KEEP, HS), BF16),
+            pltpu.VMEM((S, PR, HS), BF16),
+            pltpu.VMEM((TOPK, 1, KEEP), F32),
             pltpu.VMEM((KEEP, 3 * D), BF16),
-            pltpu.VMEM((TOPK, 1, KEEP), F32),
-            dma((2, 3 * PIECES + 1)),
+            dma((2, 5)),
         ],
         compiler_params=pltpu.CompilerParams(vmem_limit_bytes=60 * 1024 * 1024),
     )(*out)

time: 134 us -> 133 us (level)
  Pallas kernels: 133 us -> 131 us
    pallas_call x1, Pallas kernels: 130 us -> 128 us  [body(): pl.pallas_call(functools.partial(kernel, S, E), out_shape=[jax.ShapeDtype...]
where the time goes in v6:
time: 133 us; the launch traced here: 132 us
  Pallas kernels  131 us (98%)
  between operations  1.45 us (1%)
    pallas_call x1, Pallas kernels, body(): pl.pallas_call(functools.partial(kernel, S, E), out_shape=[jax.ShapeDtype...  128 us
    pallas_call x1, Pallas kernels, body(): pl.pallas_call(finish, out_shape=[jax.ShapeDtypeStruct((1, TOK, D), BF16)...  2.99 us

profile of v6, /device:TPU:1, one launch (start us, length us, event | category | flops | bytes accessed | tf_op | source)
XLA Modules:
  0.0 132.4 jit_solution(15526340129622254671)
XLA Ops:
  1.3 128.0 %shard_map.129 = (bf16[256,2048]{1,0:T(8,128)(2,1)}, bf16[256,2048]{1,0:T(8,128)(2,1)}, bf16[32,64,128]{2,1,0:T(8,128)(2,1)}, bf16[32,32,128]{2,1,0:T(8,128)(2,1)}, f32[6,1,64]{2,1,0:T(1,128)}) custom-call(bf16[256,2048]{1,0:T(8,128)(2,1)} %bitcast.13, s32[1,64]{1,0:T(1,128)} %kept_index_h.1, s32[1,1]{1,0:T(1,128)S(6)} %copy.14.kept_count_h, ...), custom_call_target="tpu_custom_call" | custom-call | tf_op jit(solution)/shard_map/pallas_call | solution.py:798
  129.3 3.0 %shard_map.130 = (bf16[1,256,2048]{2,1,0:T(8,128)(2,1)}, bf16[1,256,2048]{2,1,0:T(8,128)(2,1)}, bf16[1,64,6144]{2,1,0:T(8,128)(2,1)}, f32[6,1,64]{2,1,0:T(1,128)}) custom-call(bf16[256,2048]{1,0:T(8,128)(2,1)} %get-tuple-element.13.a, bf16[256,2048]{1,0:T(8,128)(2,1)} %get-tuple-element.14.b, bf16[32,64,128]{2,1,0:T(8,128)(2,1)} %get-tuple-element.15.c, ...), custom_call_target="tpu_custom_call" | custom-call | tf_op jit(solution)/shard_map/pallas_call | solution.py:873

commit v7 on v6

--- a/solution.py
+++ b/solution.py
@@ -632,7 +632,6 @@
     )
     input_grad_out = load(0, cotangent, input_grad_h)
     input_grad_out.start()
-    back_start(1, part_all, send_ss.at[8], y_rs.at[0])
 
     def give_copy(c):
         rows = pl.ds(c * KB, KB)
@@ -661,6 +660,8 @@
         rows = slice(c * KB, (c + 1) * KB)
         block = pl.ds(c * QSRC, QSRC)
         landed(g_recv.at[block], g_rs.at[c])
+        if c == 0:
+            back_start(1, part_all, send_ss.at[8], y_rs.at[0])
         dout[c] = g_recv[c * QSRC : (c + 1) * QSRC].reshape(QB, HS)
         turn = dout[c].astype(F32).T * att_t[:, c * QB : (c + 1) * QB]
         delta[c] = jnp.sum(turn, axis=0, keepdims=True)

time: 133 us -> 133 us (level)
  no operation moved by 1% of the time
where the time goes in v7:
time: 133 us
  Pallas kernels  132 us (99%)
  between operations  1.45 us (1%)
    pallas_call x1, Pallas kernels, body(): pl.pallas_call(functools.partial(kernel, S, E), out_shape=[jax.ShapeDtype...  129 us
    pallas_call x1, Pallas kernels, body(): pl.pallas_call(finish, out_shape=[jax.ShapeDtypeStruct((1, TOK, D), BF16)...  2.99 us

profile of v7, /device:TPU:1, one launch (start us, length us, event | category | flops | bytes accessed | tf_op | source)
XLA Modules:
  0.0 133.3 jit_solution(39662006193427359)
XLA Ops:
  1.3 128.9 %shard_map.129 = (bf16[256,2048]{1,0:T(8,128)(2,1)}, bf16[256,2048]{1,0:T(8,128)(2,1)}, bf16[32,64,128]{2,1,0:T(8,128)(2,1)}, bf16[32,32,128]{2,1,0:T(8,128)(2,1)}, f32[6,1,64]{2,1,0:T(1,128)}) custom-call(bf16[256,2048]{1,0:T(8,128)(2,1)} %bitcast.13, s32[1,64]{1,0:T(1,128)} %kept_index_h.1, s32[1,1]{1,0:T(1,128)S(6)} %copy.14.kept_count_h, ...), custom_call_target="tpu_custom_call" | custom-call | tf_op jit(solution)/shard_map/pallas_call | solution.py:799
  130.2 3.0 %shard_map.130 = (bf16[1,256,2048]{2,1,0:T(8,128)(2,1)}, bf16[1,256,2048]{2,1,0:T(8,128)(2,1)}, bf16[1,64,6144]{2,1,0:T(8,128)(2,1)}, f32[6,1,64]{2,1,0:T(1,128)}) custom-call(bf16[256,2048]{1,0:T(8,128)(2,1)} %get-tuple-element.13.a, bf16[256,2048]{1,0:T(8,128)(2,1)} %get-tuple-element.14.b, bf16[32,64,128]{2,1,0:T(8,128)(2,1)} %get-tuple-element.15.c, ...), custom_call_target="tpu_custom_call" | custom-call | tf_op jit(solution)/shard_map/pallas_call | solution.py:874
